TPU v7x, 32 devices: a whole 2x2x4 slice. The times are simulated.
32 devices in a mesh: fsdp: 8 (over z, y), dp: 4 (over x, core).
Axes of the slice: x: 2, y: 2, z: 4, core: 2. Of those that a mesh axis runs over, the one named last changes fastest.
Arguments:
- patches: bfloat16 [32768, 128], P(('fsdp', 'dp')), may hold values from -6 to 6
- targets: float32 [32768, 128], P(('fsdp', 'dp')), may hold values from -6 to 6
- size_ids: int32 [32768], P(('fsdp', 'dp')), may hold values from 0 to 4
- time_ids: int32 [32768], P(('fsdp', 'dp')), may hold values from 0 to 255
- variate_ids: int32 [32768], P(('fsdp', 'dp')), may hold values from 0 to 3
- lengths: int32 [512], P(('fsdp', 'dp')), may hold values from 32 to 64, as said below
- w_in: float32 [248, 384], P(None, 'fsdp'), may hold values from -0.75 to 0.75
- w_qkv: float32 [3, 384, 1152], P(None, 'fsdp'), may hold values from -0.3125 to 0.3125
- w_o: float32 [3, 384, 384], P(None, 'fsdp'), may hold values from -1.25 to 1.25
- w_gu: float32 [3, 384, 2048], P(None, 'fsdp'), may hold values from -0.3125 to 0.3125
- w_down: float32 [3, 1024, 384], P(None, 'fsdp'), may hold values from -0.1875 to 0.1875
- w_head: float32 [384, 1152], P('fsdp'), may hold values from -0.3125 to 0.3125
- gains: float32 [7, 384], P(None, 'fsdp'), may hold values from 0.4 to 1.8
- var_bias: float32 [3, 2, 6], replicated, may hold values from -4 to 4
- first_in: float32 [248, 384], P(None, 'fsdp'), may hold values from -2.9802322e-07 to 2.9802322e-07
- first_qkv: float32 [3, 384, 1152], P(None, 'fsdp'), may hold values from -2.9802322e-07 to 2.9802322e-07
- first_o: float32 [3, 384, 384], P(None, 'fsdp'), may hold values from -2.9802322e-07 to 2.9802322e-07
- first_gu: float32 [3, 384, 2048], P(None, 'fsdp'), may hold values from -2.9802322e-07 to 2.9802322e-07
- first_down: float32 [3, 1024, 384], P(None, 'fsdp'), may hold values from -2.9802322e-07 to 2.9802322e-07
- first_head: float32 [384, 1152], P('fsdp'), may hold values from -2.9802322e-07 to 2.9802322e-07
- first_gains: float32 [7, 384], P(None, 'fsdp'), may hold values from -1.1920929e-06 to 1.1920929e-06
- first_bias: float32 [3, 2, 6], replicated, may hold values from -4.172325e-07 to 4.172325e-07
- second_in: float32 [248, 384], P(None, 'fsdp'), may hold values from 8.99339e-15 to 3.590517e-14
- second_qkv: float32 [3, 384, 1152], P(None, 'fsdp'), may hold values from 8.99339e-15 to 3.590517e-14
- second_o: float32 [3, 384, 384], P(None, 'fsdp'), may hold values from 8.99339e-15 to 3.590517e-14
- second_gu: float32 [3, 384, 2048], P(None, 'fsdp'), may hold values from 8.99339e-15 to 3.590517e-14
- second_down: float32 [3, 1024, 384], P(None, 'fsdp'), may hold values from 8.99339e-15 to 3.590517e-14
- second_head: float32 [384, 1152], P('fsdp'), may hold values from 8.99339e-15 to 3.590517e-14
- second_gains: float32 [7, 384], P(None, 'fsdp'), may hold values from 1.4362068e-13 to 5.813218e-13
- second_bias: float32 [3, 2, 6], replicated, may hold values from 2.0175286e-14 to 8.035919e-14
Outputs:
- loss_sum: float32 [], replicated
- target_count: float32 [], replicated
- grad_norm: float32 [], replicated
- new_in: float32 [248, 384], P(None, 'fsdp')
- new_qkv: float32 [3, 384, 1152], P(None, 'fsdp')
- new_o: float32 [3, 384, 384], P(None, 'fsdp')
- new_gu: float32 [3, 384, 2048], P(None, 'fsdp')
- new_down: float32 [3, 1024, 384], P(None, 'fsdp')
- new_head: float32 [384, 1152], P('fsdp')
- new_gains: float32 [7, 384], P(None, 'fsdp')
- new_bias: float32 [3, 2, 6], replicated
- first_in_new: float32 [248, 384], P(None, 'fsdp')
- first_qkv_new: float32 [3, 384, 1152], P(None, 'fsdp')
- first_o_new: float32 [3, 384, 384], P(None, 'fsdp')
- first_gu_new: float32 [3, 384, 2048], P(None, 'fsdp')
- first_down_new: float32 [3, 1024, 384], P(None, 'fsdp')
- first_head_new: float32 [384, 1152], P('fsdp')
- first_gains_new: float32 [7, 384], P(None, 'fsdp')
- first_bias_new: float32 [3, 2, 6], replicated
- second_in_new: float32 [248, 384], P(None, 'fsdp')
- second_qkv_new: float32 [3, 384, 1152], P(None, 'fsdp')
- second_o_new: float32 [3, 384, 384], P(None, 'fsdp')
- second_gu_new: float32 [3, 384, 2048], P(None, 'fsdp')
- second_down_new: float32 [3, 1024, 384], P(None, 'fsdp')
- second_head_new: float32 [384, 1152], P('fsdp')
- second_gains_new: float32 [7, 384], P(None, 'fsdp')
- second_bias_new: float32 [3, 2, 6], replicated
Inputs may be any that keep to these rules, and one draw needn't show every extreme that they name: `lengths`: live tokens at the head of each bucket of 64 slots; the rest are padding.
All inputs are finite; a program needn't handle non-finite values.
Results may differ from a plain program's by a relative error of at most 0.03.
Values may be sent and summed in bfloat16 or wider, within the bound.
No kernel may reach another device: no remote copies, remote signals or barrier semaphores. Data moves between devices by JAX's collectives and lax.ppermute only.
A program may use at most 256 MiB of HBM per device.

v0:
```python
import jax
import jax.numpy as jnp
from jax import lax
from jax.sharding import PartitionSpec as P

D = 384
H = 6
HD = 64
FF = 1024
PMAX = 128
NQ = 9
BUCKET = 64
L = 3
MICRO = 2
STEP_NUM = 10
TOK_MB = 512


EPS_NORM = 1e-05
SMOOTH = 0.5
THETA = 10000.0
MASKED_SCORE = -1e30
CLIP_NORM = 0.001
BETA_ONE = 0.9
BETA_TWO = 0.95
ADAM_EPS = 1e-08
WEIGHT_DECAY = 0.1
RATE_MATRIX = 0.15
RATE_GAIN = 0.8


def dot_left(left_side, right_side):
    return lax.dot_general(
        left_side, right_side, (((0,), (0,)), ((), ())), preferred_element_type=jnp.float32
    )


def dot_right(left_side, right_side):
    return lax.dot_general(
        left_side, right_side, (((1,), (1,)), ((), ())), preferred_element_type=jnp.float32
    )


def rms_norm(stream, gain_row):
    return (
        stream * lax.rsqrt(jnp.mean(stream * stream, axis=-1, keepdims=True) + EPS_NORM) * gain_row
    )


def rms_back(stream, gain_row, grad_normed):
    inverse = lax.rsqrt(jnp.mean(stream * stream, axis=-1, keepdims=True) + EPS_NORM)
    unit_rows = stream * inverse
    grad_unit = grad_normed * gain_row
    grad_stream = inverse * (
        grad_unit - unit_rows * jnp.mean(grad_unit * unit_rows, axis=-1, keepdims=True)
    )
    return (grad_stream, jnp.sum(grad_normed * unit_rows, axis=0))


def half_turn(tensor):
    middle = tensor.shape[-1] // 2
    return jnp.concatenate([-tensor[..., middle:], tensor[..., :middle]], axis=-1)


def rotary(tensor, cos_table, sin_table):
    return tensor * cos_table + half_turn(tensor) * sin_table


def unrotary(grad_rot, cos_table, sin_table):
    return grad_rot * cos_table - half_turn(grad_rot * sin_table)


def angle_tables(time_ids):
    frequency = THETA ** (-2.0 * jnp.arange(HD // 2, dtype=jnp.float32) / HD)
    phase_table = time_ids.astype(jnp.float32)[:, None] * frequency[None, :]
    phase_table = jnp.concatenate([phase_table, phase_table], axis=-1)[:, None, :]
    return (jnp.cos(phase_table), jnp.sin(phase_table))


def target_table(size_ids, lengths_block, row_count):
    position = jnp.arange(row_count, dtype=jnp.int32)
    live_rows = position % BUCKET < jnp.repeat(lengths_block, BUCKET, total_repeat_length=row_count)
    widths = sum(
        ((size_ids == size_id).astype(jnp.int32) * (PMAX >> 4 - size_id) for size_id in range(5))
    )
    target_mask = (
        live_rows[:, None] & (jnp.arange(PMAX, dtype=jnp.int32)[None, :] < widths[:, None])
    ).astype(jnp.float32)
    return (target_mask, live_rows)


def patch_concat(patches, size_ids):
    pieces = []
    for size_id in range(5):
        span_cols = PMAX >> 4 - size_id
        pieces.append(
            patches[:, :span_cols].astype(jnp.float32)
            * (size_ids == size_id).astype(jnp.float32)[:, None]
        )
    return jnp.concatenate(pieces, axis=1).astype(jnp.bfloat16)


def layer_forward(stream, weights, gain_pair, bias_pair, context):
    w_qkv, w_o, w_gu, w_down = weights
    cos_table, sin_table, key_live, same_var = context
    row_count = stream.shape[0]
    nbuckets = row_count // BUCKET
    normed = rms_norm(stream, gain_pair[0]).astype(jnp.bfloat16)
    qkv_out = jnp.dot(normed, w_qkv, preferred_element_type=jnp.float32).reshape(
        row_count, 3, H, HD
    )
    queries = (
        rotary(qkv_out[:, 0], cos_table, sin_table)
        .astype(jnp.bfloat16)
        .reshape(nbuckets, BUCKET, H, HD)
    )
    keys_rot = (
        rotary(qkv_out[:, 1], cos_table, sin_table)
        .astype(jnp.bfloat16)
        .reshape(nbuckets, BUCKET, H, HD)
    )
    values = qkv_out[:, 2].astype(jnp.bfloat16).reshape(nbuckets, BUCKET, H, HD)
    score_bias = jnp.where(
        same_var, bias_pair[1][None, :, None, None], bias_pair[0][None, :, None, None]
    )
    scores = (
        jnp.einsum("bqhd,bkhd->bhqk", queries, keys_rot, preferred_element_type=jnp.float32)
        * HD ** (-0.5)
        + score_bias
    )
    scores = jnp.where(key_live, scores, MASKED_SCORE)
    shifted = jnp.exp(scores - jnp.max(scores, axis=-1, keepdims=True))
    attn_prob = shifted / jnp.sum(shifted, axis=-1, keepdims=True)
    prob_low = attn_prob.astype(jnp.bfloat16)
    mixed_low = (
        jnp.einsum("bhqk,bkhd->bqhd", prob_low, values, preferred_element_type=jnp.float32)
        .reshape(row_count, D)
        .astype(jnp.bfloat16)
    )
    middle_stream = stream + jnp.dot(mixed_low, w_o, preferred_element_type=jnp.float32)
    ffn_in = rms_norm(middle_stream, gain_pair[1]).astype(jnp.bfloat16)
    gate_up = jnp.dot(ffn_in, w_gu, preferred_element_type=jnp.float32)
    hidden = (jax.nn.silu(gate_up[:, :FF]) * gate_up[:, FF:]).astype(jnp.bfloat16)
    layer_out = middle_stream + jnp.dot(hidden, w_down, preferred_element_type=jnp.float32)
    stored = (
        normed,
        queries,
        keys_rot,
        values,
        attn_prob,
        prob_low,
        mixed_low,
        middle_stream,
        ffn_in,
        gate_up,
        hidden,
    )
    return (layer_out, stored)


def layer_backward(stream, grad_out, weights, gain_pair, bias_pair, context):
    unused, stored = layer_forward(stream, weights, gain_pair, bias_pair, context)
    (
        normed,
        queries,
        keys_rot,
        values,
        attn_prob,
        prob_low,
        mixed_low,
        middle_stream,
        ffn_in,
        gate_up,
        hidden,
    ) = stored
    w_qkv, w_o, w_gu, w_down = weights
    cos_table, sin_table, key_live, same_var = context
    row_count = stream.shape[0]
    nbuckets = row_count // BUCKET
    grad_low = grad_out.astype(jnp.bfloat16)
    grad_down = dot_left(hidden, grad_low)
    grad_hidden = dot_right(grad_low, w_down)
    gate_pre = gate_up[:, :FF]
    up_pre = gate_up[:, FF:]
    gate_sig = jax.nn.sigmoid(gate_pre)
    grad_gate = grad_hidden * up_pre * gate_sig * (1.0 + gate_pre * (1.0 - gate_sig))
    grad_up = grad_hidden * gate_pre * gate_sig
    grad_gu_low = jnp.concatenate([grad_gate, grad_up], axis=1).astype(jnp.bfloat16)
    grad_gu = dot_left(ffn_in, grad_gu_low)
    grad_middle, grad_gain_ffn = rms_back(middle_stream, gain_pair[1], dot_right(grad_gu_low, w_gu))
    grad_middle = grad_middle + grad_out
    grad_attn_low = grad_middle.astype(jnp.bfloat16)
    grad_o = dot_left(mixed_low, grad_attn_low)
    grad_mixed = dot_right(grad_attn_low, w_o).astype(jnp.bfloat16).reshape(nbuckets, BUCKET, H, HD)
    grad_values = jnp.einsum(
        "bhqk,bqhd->bkhd", prob_low, grad_mixed, preferred_element_type=jnp.float32
    )
    grad_prob = jnp.einsum(
        "bqhd,bkhd->bhqk", grad_mixed, values, preferred_element_type=jnp.float32
    )
    grad_scores = attn_prob * (grad_prob - jnp.sum(attn_prob * grad_prob, axis=-1, keepdims=True))
    grad_scores_low = grad_scores.astype(jnp.bfloat16)
    zero_low = jnp.zeros((), jnp.bfloat16)
    grad_bias_same = jnp.sum(
        jnp.where(same_var, grad_scores_low, zero_low), axis=(0, 2, 3), dtype=jnp.float32
    )
    grad_bias_other = jnp.sum(
        jnp.where(same_var, zero_low, grad_scores_low), axis=(0, 2, 3), dtype=jnp.float32
    )
    grad_queries = jnp.einsum(
        "bhqk,bkhd->bqhd", grad_scores_low, keys_rot, preferred_element_type=jnp.float32
    ) * HD ** (-0.5)
    grad_keys = jnp.einsum(
        "bhqk,bqhd->bkhd", grad_scores_low, queries, preferred_element_type=jnp.float32
    ) * HD ** (-0.5)
    grad_queries = grad_queries.reshape(row_count, H, HD)
    grad_keys = grad_keys.reshape(row_count, H, HD)
    grad_values = grad_values.reshape(row_count, H, HD)
    grad_qkv_low = jnp.stack(
        [
            unrotary(grad_queries, cos_table, sin_table),
            unrotary(grad_keys, cos_table, sin_table),
            grad_values,
        ],
        axis=1,
    )
    grad_qkv_low = grad_qkv_low.reshape(row_count, 3 * D).astype(jnp.bfloat16)
    grad_qkv = dot_left(normed, grad_qkv_low)
    grad_stream, grad_gain_attn = rms_back(stream, gain_pair[0], dot_right(grad_qkv_low, w_qkv))
    matrices = (grad_qkv, grad_o, grad_gu, grad_down)
    return (
        grad_stream + grad_middle,
        matrices,
        (grad_gain_attn, grad_gain_ffn),
        jnp.stack([grad_bias_other, grad_bias_same]),
    )


def adam_update(master, clipped, first_old, second_old, matrix):
    first_new = BETA_ONE * first_old + (1.0 - BETA_ONE) * clipped
    second_new = BETA_TWO * second_old + (1.0 - BETA_TWO) * clipped * clipped
    first_hat = first_new / (1.0 - BETA_ONE**STEP_NUM)
    second_hat = second_new / (1.0 - BETA_TWO**STEP_NUM)
    direction = first_hat / (jnp.sqrt(second_hat) + ADAM_EPS)
    if matrix:
        master_new = master - RATE_MATRIX * (direction + WEIGHT_DECAY * master)
    else:
        master_new = master - RATE_GAIN * direction
    return (master_new, first_new, second_new)


def per_device(
    patches,
    targets,
    size_ids,
    time_ids,
    variate_ids,
    lengths,
    w_in,
    w_qkv,
    w_o,
    w_gu,
    w_down,
    w_head,
    gains,
    var_bias,
    first_in,
    first_qkv,
    first_o,
    first_gu,
    first_down,
    first_head,
    first_gains,
    first_bias,
    second_in,
    second_qkv,
    second_o,
    second_gu,
    second_down,
    second_head,
    second_gains,
    second_bias,
):
    in_full, head_full, gain_low = (
        lax.all_gather(w_in.astype(jnp.bfloat16), "fsdp", axis=1, tiled=True),
        lax.all_gather(w_head.astype(jnp.bfloat16), "fsdp", axis=0, tiled=True),
        lax.all_gather(gains.astype(jnp.bfloat16), "fsdp", axis=1, tiled=True),
    )
    gain_full = gain_low.astype(jnp.float32)
    count_mask, unused = target_table(size_ids, lengths, patches.shape[0])
    total_count = lax.psum(jnp.sum(count_mask), ("fsdp", "dp"))
    inverse_count = 1.0 / total_count
    levels = (jnp.arange(NQ, dtype=jnp.float32) + 1.0) / (NQ + 1)
    buckets_micro = TOK_MB // BUCKET
    per_layer = [None] * L
    grad_in_acc = jnp.zeros(in_full.shape, jnp.float32)
    grad_head_acc = jnp.zeros(head_full.shape, jnp.float32)
    grad_gain_acc = jnp.zeros(gain_full.shape, jnp.float32)
    grad_bias_acc = jnp.zeros(var_bias.shape, jnp.float32)
    loss_local = jnp.zeros((), jnp.float32)
    for micro_id in range(MICRO):
        start_row = micro_id * TOK_MB
        part_patches = patches[start_row : start_row + TOK_MB]
        part_targets = targets[start_row : start_row + TOK_MB]
        part_sizes = size_ids[start_row : start_row + TOK_MB]
        part_times = time_ids[start_row : start_row + TOK_MB]
        part_vars = variate_ids[start_row : start_row + TOK_MB].reshape(buckets_micro, BUCKET)
        part_lengths = lengths[micro_id * buckets_micro : (micro_id + 1) * buckets_micro]
        target_mask, live_rows = target_table(part_sizes, part_lengths, TOK_MB)
        key_live = live_rows.reshape(buckets_micro, 1, 1, BUCKET)
        same_var = (part_vars[:, :, None] == part_vars[:, None, :])[:, None]
        cos_table, sin_table = angle_tables(part_times)
        context = (cos_table, sin_table, key_live, same_var)
        concat_low = patch_concat(part_patches, part_sizes)
        stream = jnp.dot(concat_low, in_full, preferred_element_type=jnp.float32)
        inputs_kept = []
        weights_kept = []
        for layer_id in range(L):
            weights = (
                lax.all_gather(w_qkv[layer_id].astype(jnp.bfloat16), "fsdp", axis=0, tiled=True),
                lax.all_gather(w_o[layer_id].astype(jnp.bfloat16), "fsdp", axis=0, tiled=True),
                lax.all_gather(w_gu[layer_id].astype(jnp.bfloat16), "fsdp", axis=0, tiled=True),
                lax.all_gather(w_down[layer_id].astype(jnp.bfloat16), "fsdp", axis=0, tiled=True),
            )
            inputs_kept.append(stream)
            weights_kept.append(weights)
            stream, unused_stored = layer_forward(
                stream,
                weights,
                gain_full[2 * layer_id : 2 * layer_id + 2],
                var_bias[layer_id],
                context,
            )
        final_in = rms_norm(stream, gain_full[2 * L]).astype(jnp.bfloat16)
        predicted = jnp.dot(final_in, head_full, preferred_element_type=jnp.float32).reshape(
            TOK_MB, NQ, PMAX
        )
        residual = part_targets[:, None, :] - predicted
        pinball = levels[None, :, None] * residual + SMOOTH * jax.nn.softplus(-residual / SMOOTH)
        loss_local = loss_local + jnp.sum(pinball * target_mask[:, None, :])
        slope = levels[None, :, None] - jax.nn.sigmoid(-residual / SMOOTH)
        grad_pred = (
            (-(slope * target_mask[:, None, :]) * inverse_count)
            .reshape(TOK_MB, NQ * PMAX)
            .astype(jnp.bfloat16)
        )
        grad_head_acc = grad_head_acc + dot_left(final_in, grad_pred)
        grad_stream, grad_gain_final = rms_back(
            stream, gain_full[2 * L], dot_right(grad_pred, head_full)
        )
        grad_gain_acc = grad_gain_acc.at[2 * L].add(grad_gain_final)
        for layer_id in reversed(range(L)):
            weights = (
                lax.all_gather(w_qkv[layer_id].astype(jnp.bfloat16), "fsdp", axis=0, tiled=True),
                lax.all_gather(w_o[layer_id].astype(jnp.bfloat16), "fsdp", axis=0, tiled=True),
                lax.all_gather(w_gu[layer_id].astype(jnp.bfloat16), "fsdp", axis=0, tiled=True),
                lax.all_gather(w_down[layer_id].astype(jnp.bfloat16), "fsdp", axis=0, tiled=True),
            )
            grad_stream, matrices, gain_grads, bias_grads = layer_backward(
                inputs_kept[layer_id],
                grad_stream,
                weights,
                gain_full[2 * layer_id : 2 * layer_id + 2],
                var_bias[layer_id],
                context,
            )
            if per_layer[layer_id] is None:
                per_layer[layer_id] = tuple(matrices)
            else:
                per_layer[layer_id] = tuple(
                    (earlier + latest for earlier, latest in zip(per_layer[layer_id], matrices))
                )
            grad_gain_acc = (
                grad_gain_acc.at[2 * layer_id]
                .add(gain_grads[0])
                .at[2 * layer_id + 1]
                .add(gain_grads[1])
            )
            grad_bias_acc = grad_bias_acc.at[layer_id].add(bias_grads)
        grad_in_acc = grad_in_acc + dot_left(concat_low, grad_stream.astype(jnp.bfloat16))
    stacks = tuple(
        (
            jnp.stack([per_layer[layer_id][member_id] for layer_id in range(L)])
            for member_id in range(4)
        )
    )
    shards = (
        lax.psum_scatter(
            stacks[0].astype(jnp.bfloat16), "fsdp", scatter_dimension=1, tiled=True
        ).astype(jnp.float32),
        lax.psum_scatter(
            stacks[1].astype(jnp.bfloat16), "fsdp", scatter_dimension=1, tiled=True
        ).astype(jnp.float32),
        lax.psum_scatter(
            stacks[2].astype(jnp.bfloat16), "fsdp", scatter_dimension=1, tiled=True
        ).astype(jnp.float32),
        lax.psum_scatter(
            stacks[3].astype(jnp.bfloat16), "fsdp", scatter_dimension=1, tiled=True
        ).astype(jnp.float32),
        lax.psum_scatter(
            grad_in_acc.astype(jnp.bfloat16), "fsdp", scatter_dimension=1, tiled=True
        ).astype(jnp.float32),
        lax.psum_scatter(
            grad_head_acc.astype(jnp.bfloat16), "fsdp", scatter_dimension=0, tiled=True
        ).astype(jnp.float32),
        lax.psum_scatter(
            grad_gain_acc.astype(jnp.bfloat16), "fsdp", scatter_dimension=1, tiled=True
        ).astype(jnp.float32),
    )
    reduced = (
        lax.psum(shards[0].astype(jnp.bfloat16), "dp").astype(jnp.float32),
        lax.psum(shards[1].astype(jnp.bfloat16), "dp").astype(jnp.float32),
        lax.psum(shards[2].astype(jnp.bfloat16), "dp").astype(jnp.float32),
        lax.psum(shards[3].astype(jnp.bfloat16), "dp").astype(jnp.float32),
        lax.psum(shards[4].astype(jnp.bfloat16), "dp").astype(jnp.float32),
        lax.psum(shards[5].astype(jnp.bfloat16), "dp").astype(jnp.float32),
        lax.psum(shards[6].astype(jnp.bfloat16), "dp").astype(jnp.float32),
    )
    loss_sum, bias_grad = lax.psum((loss_local, grad_bias_acc), ("fsdp", "dp"))
    square_local = sum((jnp.sum(member * member) for member in reduced))
    grad_norm = jnp.sqrt(lax.psum(square_local, "fsdp") + jnp.sum(bias_grad * bias_grad))
    factor = jnp.minimum(1.0, CLIP_NORM / grad_norm)
    gradients = (
        reduced[4],
        reduced[0],
        reduced[1],
        reduced[2],
        reduced[3],
        reduced[5],
        reduced[6],
        bias_grad,
    )
    masters = (w_in, w_qkv, w_o, w_gu, w_down, w_head, gains, var_bias)
    firsts = (
        first_in,
        first_qkv,
        first_o,
        first_gu,
        first_down,
        first_head,
        first_gains,
        first_bias,
    )
    seconds = (
        second_in,
        second_qkv,
        second_o,
        second_gu,
        second_down,
        second_head,
        second_gains,
        second_bias,
    )
    fresh = [
        adam_update(
            masters[member_id],
            gradients[member_id] * factor,
            firsts[member_id],
            seconds[member_id],
            member_id < 6,
        )
        for member_id in range(8)
    ]
    return (
        loss_sum,
        total_count,
        grad_norm,
        fresh[0][0],
        fresh[1][0],
        fresh[2][0],
        fresh[3][0],
        fresh[4][0],
        fresh[5][0],
        fresh[6][0],
        fresh[7][0],
        fresh[0][1],
        fresh[1][1],
        fresh[2][1],
        fresh[3][1],
        fresh[4][1],
        fresh[5][1],
        fresh[6][1],
        fresh[7][1],
        fresh[0][2],
        fresh[1][2],
        fresh[2][2],
        fresh[3][2],
        fresh[4][2],
        fresh[5][2],
        fresh[6][2],
        fresh[7][2],
    )


def solution(mesh):
    in_specs = (
        P(("fsdp", "dp"), None),
        P(("fsdp", "dp"), None),
        P(("fsdp", "dp")),
        P(("fsdp", "dp")),
        P(("fsdp", "dp")),
        P(("fsdp", "dp")),
        P(None, "fsdp"),
        P(None, "fsdp", None),
        P(None, "fsdp", None),
        P(None, "fsdp", None),
        P(None, "fsdp", None),
        P("fsdp", None),
        P(None, "fsdp"),
        P(),
        P(None, "fsdp"),
        P(None, "fsdp", None),
        P(None, "fsdp", None),
        P(None, "fsdp", None),
        P(None, "fsdp", None),
        P("fsdp", None),
        P(None, "fsdp"),
        P(),
        P(None, "fsdp"),
        P(None, "fsdp", None),
        P(None, "fsdp", None),
        P(None, "fsdp", None),
        P(None, "fsdp", None),
        P("fsdp", None),
        P(None, "fsdp"),
        P(),
    )
    out_specs = (
        P(),
        P(),
        P(),
        P(None, "fsdp"),
        P(None, "fsdp", None),
        P(None, "fsdp", None),
        P(None, "fsdp", None),
        P(None, "fsdp", None),
        P("fsdp", None),
        P(None, "fsdp"),
        P(),
        P(None, "fsdp"),
        P(None, "fsdp", None),
        P(None, "fsdp", None),
        P(None, "fsdp", None),
        P(None, "fsdp", None),
        P("fsdp", None),
        P(None, "fsdp"),
        P(),
        P(None, "fsdp"),
        P(None, "fsdp", None),
        P(None, "fsdp", None),
        P(None, "fsdp", None),
        P(None, "fsdp", None),
        P("fsdp", None),
        P(None, "fsdp"),
        P(),
    )
    return jax.shard_map(
        per_device, mesh=mesh, in_specs=in_specs, out_specs=out_specs, check_vma=False
    )
```

profile of v0, /device:TPU:0, one launch (start us, length us, event | category | flops | bytes accessed | tf_op | source)
XLA Modules:
  0.0 1541.7 jit_solution(6856732510121050787)
XLA Ops:
  13.0 32.7 %all_gather.30 = bf16[248,384]{0,1:T(8,128)(2,1)S(1)} all-gather(bf16[248,48]{0,1:T(8,128)(2,1)S(1)} %convert_element_type.670), channel_id=1, replica_groups=mesh['fsdp'=8,'dp'=4] {'fsdp'}, dimensions={1}, use_global_device_ids=true | all-gather | bytes 214272 | tf_op jit(solution)/shard_map/all_gather | solution.py:285
  48.8 26.1 %all-gather.12 = bf16[8,48,7]{1,2,0:T(8,128)(2,1)S(1)} all-gather(bf16[1,48,7]{1,2,0:T(8,128)(2,1)S(1)} %convert_bitcast_fusion), channel_id=1, replica_groups=mesh['fsdp'=8,'dp'=4] {'fsdp'}, dimensions={0}, use_global_device_ids=true | all-gather | bytes 6048 | tf_op jit(solution)/shard_map/all_gather | solution.py:287
  76.4 34.3 %all-gather = bf16[1,384,1152]{2,1,0:T(8,128)(2,1)S(1)} all-gather(bf16[1,48,1152]{2,1,0:T(8,128)(2,1)S(1)} %get-tuple-element.528), channel_id=2, replica_groups=mesh['fsdp'=8,'dp'=4] {'fsdp'}, dimensions={1}, use_global_device_ids=true | all-gather | bytes 995328 | tf_op jit(solution)/shard_map/all_gather | solution.py:320
  133.9 10.5 select_compare_fusion.1
  163.9 31.0 %all-gather.1 = bf16[1,384,384]{2,1,0:T(8,128)(2,1)S(1)} all-gather(bf16[1,48,384]{2,1,0:T(8,128)(2,1)S(1)} %get-tuple-element.572), channel_id=3, replica_groups=mesh['fsdp'=8,'dp'=4] {'fsdp'}, dimensions={1}, use_global_device_ids=true | all-gather | bytes 331776 | tf_op jit(solution)/shard_map/all_gather | solution.py:321
  195.5 34.5 %all-gather.3 = bf16[1,1024,384]{2,1,0:T(8,128)(2,1)} all-gather(bf16[1,128,384]{2,1,0:T(8,128)(2,1)S(1)} %get-tuple-element.531), channel_id=5, replica_groups=mesh['fsdp'=8,'dp'=4] {'fsdp'}, dimensions={1}, use_global_device_ids=true | all-gather | bytes 884736 | tf_op jit(solution)/shard_map/all_gather | solution.py:323
  230.0 34.1 %all-gather.4 = bf16[1,384,1152]{2,1,0:T(8,128)(2,1)} all-gather(bf16[1,48,1152]{2,1,0:T(8,128)(2,1)S(1)} %copy-done.305), channel_id=6, replica_groups=mesh['fsdp'=8,'dp'=4] {'fsdp'}, dimensions={1}, use_global_device_ids=true | all-gather | bytes 995328 | tf_op jit(solution)/shard_map/all_gather | solution.py:320
  264.1 31.0 %all-gather.5 = bf16[1,384,384]{2,1,0:T(8,128)(2,1)S(1)} all-gather(bf16[1,48,384]{2,1,0:T(8,128)(2,1)S(1)} %get-tuple-element.571), channel_id=7, replica_groups=mesh['fsdp'=8,'dp'=4] {'fsdp'}, dimensions={1}, use_global_device_ids=true | all-gather | bytes 331776 | tf_op jit(solution)/shard_map/all_gather | solution.py:321
  295.1 34.3 %all-gather.7 = bf16[1,1024,384]{2,1,0:T(8,128)(2,1)} all-gather(bf16[1,128,384]{2,1,0:T(8,128)(2,1)S(1)} %get-tuple-element.530), channel_id=9, replica_groups=mesh['fsdp'=8,'dp'=4] {'fsdp'}, dimensions={1}, use_global_device_ids=true | all-gather | bytes 884736 | tf_op jit(solution)/shard_map/all_gather | solution.py:323
  329.4 34.3 %all-gather.8 = bf16[1,384,1152]{2,1,0:T(8,128)(2,1)} all-gather(bf16[1,48,1152]{2,1,0:T(8,128)(2,1)S(1)} %copy-done.304), channel_id=10, replica_groups=mesh['fsdp'=8,'dp'=4] {'fsdp'}, dimensions={1}, use_global_device_ids=true | all-gather | bytes 995328 | tf_op jit(solution)/shard_map/all_gather | solution.py:320
  363.7 33.2 %all-gather.9 = bf16[1,384,384]{2,1,0:T(8,128)(2,1)} all-gather(bf16[1,48,384]{2,1,0:T(8,128)(2,1)S(1)} %get-tuple-element.570), channel_id=11, replica_groups=mesh['fsdp'=8,'dp'=4] {'fsdp'}, dimensions={1}, use_global_device_ids=true | all-gather | bytes 331776 | tf_op jit(solution)/shard_map/all_gather | solution.py:321
  396.9 34.1 %all-gather.11 = bf16[1,1024,384]{2,1,0:T(8,128)(2,1)} all-gather(bf16[1,128,384]{2,1,0:T(8,128)(2,1)S(1)} %get-tuple-element.529), channel_id=13, replica_groups=mesh['fsdp'=8,'dp'=4] {'fsdp'}, dimensions={1}, use_global_device_ids=true | all-gather | bytes 884736 | tf_op jit(solution)/shard_map/all_gather | solution.py:323
  459.5 33.8 %all_gather.44 = bf16[384,1152]{1,0:T(8,128)(2,1)} all-gather(bf16[48,1152]{1,0:T(8,128)(2,1)S(1)} %convert_element_type.718), channel_id=1, replica_groups=mesh['fsdp'=8,'dp'=4] {'fsdp'}, dimensions={0}, use_global_device_ids=true | all-gather | bytes 995328 | tf_op jit(solution)/shard_map/all_gather | solution.py:286
  509.6 37.8 %psum.78 = f32[]{:T(128)} all-reduce(f32[]{:T(128)} %convert_reduce_fusion.12), channel_id=1, replica_groups=mesh['fsdp'=8,'dp'=4] {'fsdp','dp'}, use_global_device_ids=true, to_apply=%region_30.32 | all-reduce | flops 1 | bytes 8 | tf_op jit(solution)/shard_map/psum | solution.py:291
  725.2 7.1 fusion.23
  1087.2 56.7 %reduce-scatter.16.cloned.1.call-done = bf16[3,128,384]{2,1,0:T(8,128)(2,1)} async-done(((bf16[3,1024,384]{2,1,0:T(8,128)(2,1)}), bf16[3,128,384]{2,1,0:T(8,128)(2,1)}) %reduce-scatter.16.cloned.1.call-update) | async-done | bytes 294928 | tf_op jit(solution)/shard_map/reduce_scatter | solution.py:397
  1143.9 73.2 %reduce-scatter.10.cloned.1.call-done = bf16[3,48,1152]{2,1,0:T(8,128)(2,1)} async-done(((bf16[3,384,1152]{2,1,0:T(8,128)(2,1)}), bf16[3,48,1152]{2,1,0:T(8,128)(2,1)}) %reduce-scatter.10.cloned.1.call-update) | async-done | bytes 331792 | tf_op jit(solution)/shard_map/reduce_scatter | solution.py:388
  1217.1 98.4 %reduce-scatter.14.cloned.1.call-done = bf16[3,48,2048]{2,1,0:T(8,128)(2,1)} async-done(((bf16[3,384,2048]{2,1,0:T(8,128)(2,1)}), bf16[3,48,2048]{2,1,0:T(8,128)(2,1)}) %reduce-scatter.14.cloned.1.call-update) | async-done | bytes 589840 | tf_op jit(solution)/shard_map/reduce_scatter | solution.py:394
  1317.1 40.3 %all-reduce.2 = (f32[]{:T(128)}, f32[3,2,6]{2,1,0:T(2,128)S(1)}) all-reduce(f32[]{:T(128)S(6)} %add.935, f32[3,2,6]{2,1,0:T(2,128)S(1)} %constant_dynamic-update-slice_fusion), channel_id=1, replica_groups=mesh['fsdp'=8,'dp'=4] {'fsdp','dp'}, use_global_device_ids=true, to_apply=%region_28.30 | all-reduce | flops 37 | bytes 296 | tf_op jit(solution)/shard_map/psum | solution.py:419
  1357.4 19.7 %reduce-scatter.22.cloned.1.call-done = bf16[48,7]{1,0:T(8,128)(2,1)} async-done(((bf16[384,7]{1,0:T(8,128)(2,1)}), bf16[48,7]{1,0:T(8,128)(2,1)}) %reduce-scatter.22.cloned.1.call-update) | async-done | bytes 688
  1377.9 63.4 %reduce-scatter.18.cloned.1.call-done = bf16[248,48]{0,1:T(8,128)(2,1)} async-done(((bf16[248,384]{0,1:T(8,128)(2,1)}), bf16[248,48]{0,1:T(8,128)(2,1)}) %reduce-scatter.18.cloned.1.call-update) | async-done | bytes 23824 | tf_op jit(solution)/shard_map/reduce_scatter | solution.py:400
  1441.3 11.3 all-reduce.3
  1453.8 31.1 %all-reduce.7.cloned.1.call-done = (bf16[3,48,1152]{2,1,0:T(8,128)(2,1)}, bf16[3,48,384]{2,1,0:T(8,128)(2,1)}, bf16[3,48,2048]{2,1,0:T(8,128)(2,1)}, bf16[3,128,384]{2,1,0:T(8,128)(2,1)}, bf16[48,1152]{1,0:T(8,128)(2,1)}) async-done(((bf16[3,48,1152]{2,1,0:T(8,128)(2,1)}, bf16[3,48,384]{2,1,0:T(8,128)(2,1)}, bf16[3,48,2048]{2,1,0:T(8,128)(2,1)}, bf16[3,128,384]{2,1,0:T(8,128)(2,1)}, ...) | async-done | bytes 1437712 | tf_op jit(solution)/shard_map/psum | solution.py:411
  1498.6 21.9 %psum.86 = f32[]{:T(128)} all-reduce(f32[]{:T(128)S(6)} %add.999), channel_id=1, replica_groups=mesh['fsdp'=8,'dp'=4] {'fsdp'}, use_global_device_ids=true, to_apply=%region_86.88 | all-reduce | flops 1 | bytes 8 | tf_op jit(solution)/shard_map/psum | solution.py:421
  (1369 shorter events, 648.9 us)
Async XLA Ops:
  7.2 558.0 %all-gather.17.cloned.1.call-start = ((), (), s32[]{:S(2)}) async-start(), calls=%async_computation.13 | async-start | bytes 1769472 | tf_op jit(solution)/shard_map/all_gather | solution.py:322
  9.5 590.5 %all-gather.19.cloned.1.call-start = ((), (), s32[]{:S(2)}) async-start(), calls=%async_computation.14 | async-start | bytes 1769472 | tf_op jit(solution)/shard_map/all_gather | solution.py:322
  10.3 666.0 %all-gather.21.cloned.1.call-start = ((), (), s32[]{:S(2)}) async-start(), calls=%async_computation.15 | async-start | bytes 1769472 | tf_op jit(solution)/shard_map/all_gather | solution.py:322
  11.0 1076.1 %reduce-scatter.20.cloned.1.call-start = ((), (), s32[]{:S(2)}) async-start(), calls=%async_computation.12 | async-start | bytes 995328 | tf_op jit(solution)/shard_map/reduce_scatter | solution.py:403
  75.7 534.1 %copy-start.301 = (f32[384]{0:T(512)}, f32[384]{0:T(512)S(1)}, u32[]{:S(2)}) copy-start(f32[384]{0:T(512)S(1)} %get-tuple-element.353) | copy-start | bytes 4612
  116.1 342.3 %copy-start = (f32[512,384]{0,1:T(8,128)}, f32[512,384]{0,1:T(8,128)S(1)}, u32[]{:S(2)}) copy-start(f32[512,384]{0,1:T(8,128)S(1)} %get-tuple-element.658) | copy-start | bytes 2359300
  195.3 373.3 %copy-start.26 = (f32[512,384]{0,1:T(8,128)}, f32[512,384]{0,1:T(8,128)S(1)}, u32[]{:S(2)}) copy-start(f32[512,384]{0,1:T(8,128)S(1)} %get-tuple-element.642) | copy-start | bytes 2359300
  195.4 369.8 %copy-start.338 = (f32[512]{0:T(512)}, f32[512]{0:T(512)S(1)}, u32[]{:S(2)}) copy-start(f32[512]{0:T(512)S(1)} %add_rsqrt_fusion.5) | copy-start | bytes 6148
  946.9 140.3 %reduce-scatter.12.cloned.1.call-start = ((), (), s32[]{:S(2)}) async-start(), calls=%async_computation.8 | async-start | bytes 995328 | tf_op jit(solution)/shard_map/reduce_scatter | solution.py:391
  973.0 170.9 %reduce-scatter.16.cloned.1.call-start = ((), (), s32[]{:S(2)}) async-start(), calls=%async_computation.10 | async-start | bytes 2654208 | tf_op jit(solution)/shard_map/reduce_scatter | solution.py:397
  993.0 224.0 %reduce-scatter.10.cloned.1.call-start = ((), (), s32[]{:S(2)}) async-start(), calls=%async_computation.7 | async-start | bytes 2985984 | tf_op jit(solution)/shard_map/reduce_scatter | solution.py:388
  1058.3 257.2 %reduce-scatter.14.cloned.1.call-start = ((), (), s32[]{:S(2)}) async-start(), calls=%async_computation.9 | async-start | bytes 5308416 | tf_op jit(solution)/shard_map/reduce_scatter | solution.py:394
  1072.7 304.5 %reduce-scatter.22.cloned.1.call-start = ((), (), s32[]{:S(2)}) async-start(), calls=%async_computation.16 | async-start | bytes 110592
  1084.3 357.0 %reduce-scatter.18.cloned.1.call-start = ((), (), s32[]{:S(2)}) async-start(), calls=%async_computation.11 | async-start | bytes 221184 | tf_op jit(solution)/shard_map/reduce_scatter | solution.py:400
  1086.8 435.0 %copy-start.369 = (f32[3,2,6]{2,1,0:T(2,128)S(1)}, f32[3,2,6]{2,1,0:T(2,128)}, u32[]{:S(2)}) copy-start(f32[3,2,6]{2,1,0:T(2,128)} %param.91) | copy-start | bytes 436
  1086.8 435.0 %copy-start.379 = (f32[3,2,6]{2,1,0:T(2,128)S(1)}, f32[3,2,6]{2,1,0:T(2,128)}, u32[]{:S(2)}) copy-start(f32[3,2,6]{2,1,0:T(2,128)} %param.99) | copy-start | bytes 436
  1086.9 435.0 %copy-start.380 = (f32[3,2,6]{2,1,0:T(2,128)S(1)}, f32[3,2,6]{2,1,0:T(2,128)}, u32[]{:S(2)}) copy-start(f32[3,2,6]{2,1,0:T(2,128)} %param.107) | copy-start | bytes 436
  1086.9 435.6 %copy-start.366 = (f32[7,48]{1,0:T(8,128)S(1)}, f32[7,48]{1,0:T(8,128)}, u32[]{:S(2)}) copy-start(f32[7,48]{1,0:T(8,128)} %param.90) | copy-start | bytes 4036
  1086.9 435.6 %copy-start.377 = (f32[7,48]{1,0:T(8,128)S(1)}, f32[7,48]{1,0:T(8,128)}, u32[]{:S(2)}) copy-start(f32[7,48]{1,0:T(8,128)} %param.98) | copy-start | bytes 4036
  1086.9 435.6 %copy-start.378 = (f32[7,48]{1,0:T(8,128)S(1)}, f32[7,48]{1,0:T(8,128)}, u32[]{:S(2)}) copy-start(f32[7,48]{1,0:T(8,128)} %param.106) | copy-start | bytes 4036
  1086.9 436.2 %copy-start.282 = (f32[48,1152]{1,0:T(8,128)S(1)}, f32[48,1152]{1,0:T(8,128)}, u32[]{:S(2)}) copy-start(f32[48,1152]{1,0:T(8,128)} %param.89) | copy-start | bytes 663556
  1086.9 436.2 %copy-start.314 = (f32[48,1152]{1,0:T(8,128)S(1)}, f32[48,1152]{1,0:T(8,128)}, u32[]{:S(2)}) copy-start(f32[48,1152]{1,0:T(8,128)} %param.97) | copy-start | bytes 663556
  1086.9 436.2 %copy-start.315 = (f32[48,1152]{1,0:T(8,128)S(1)}, f32[48,1152]{1,0:T(8,128)}, u32[]{:S(2)}) copy-start(f32[48,1152]{1,0:T(8,128)} %param.105) | copy-start | bytes 663556
  1086.9 397.9 %all-reduce.7.cloned.1.call-start = ((), (), s32[]{:S(2)}) async-start(), calls=%async_computation.17 | async-start | bytes 2875392 | tf_op jit(solution)/shard_map/psum | solution.py:411
  (418 other events, 5829.4 us)
Sparse Core Ops, SparseCore 0:
  10.8 47.3 all-gather.16
  60.9 48.8 all-gather.18
  112.6 44.2 all-gather.20
  947.0 62.2 reduce-scatter.19
  1012.5 60.1 reduce-scatter.11
  1076.0 67.8 reduce-scatter.15
  1147.5 69.4 reduce-scatter.9
  1221.2 94.3 reduce-scatter.13
  1319.7 57.3 reduce-scatter.21
  1381.2 60.1 reduce-scatter.17
  1444.3 40.5 all-reduce.6
where the time goes:
time: 1550 us; the launch traced here: 1540 us
  blocking collectives  505 us (33%)
  waiting for transfers between devices  344 us (22%)
  local copies, waits for them, and re-layouts  324 us (21%)
  matrix products  204 us (13%)
  other arithmetic  135 us (9%)
  between operations  28 us (2%)
    all_gather x3, blocking collectives, per_device(): lax.all_gather(w_down[layer_id].astype(jnp.bfloat16), 'fsdp', axis=0, til...  103 us
    all_gather x3, blocking collectives, per_device(): lax.all_gather(w_qkv[layer_id].astype(jnp.bfloat16), 'fsdp', axis=0, tile...  103 us
    reduce_scatter x1, waiting for transfers between devices, per_device(): lax.psum_scatter(stacks[2].astype(jnp.bfloat16), 'fsdp', scatter_dimensio...  98.4 us
    all_gather x3, blocking collectives, per_device(): lax.all_gather(w_o[layer_id].astype(jnp.bfloat16), 'fsdp', axis=0, tiled=...  95.1 us
    reduce_scatter x1, waiting for transfers between devices, per_device(): lax.psum_scatter(stacks[0].astype(jnp.bfloat16), 'fsdp', scatter_dimensio...  73.2 us
    unnamed x868, local copies, waits for them, and re-layouts  64.1 us
    reduce_scatter x1, waiting for transfers between devices, per_device(): lax.psum_scatter(grad_in_acc.astype(jnp.bfloat16), 'fsdp', scatter_dimens...  63.4 us
    reduce_scatter x1, waiting for transfers between devices, per_device(): lax.psum_scatter(stacks[3].astype(jnp.bfloat16), 'fsdp', scatter_dimensio...  56.7 us
  transfers between devices with their start and end apart: 11, of which 6 were waited for; matrix products, arithmetic and copies ran while one was open for 22% of the time, Pallas kernels for 0%

commit v1 on v0

v1 whole, which is shorter than its diff:
```python
import functools

import jax
import jax.numpy as jnp
from jax import lax
from jax.experimental import pallas as pl
from jax.experimental.pallas import tpu as pltpu
from jax.sharding import PartitionSpec as P

D = 384
H = 6
HD = 64
FF = 1024
PMAX = 128
NQ = 9
BUCKET = 64
L = 3
STEP_NUM = 10
IN_CAT = 248
NGAIN = 7
QKV = 3 * D
HEADW = NQ * PMAX
PAIRS = H // 2
LANES = 2 * HD

TILE = 256

EPS_NORM = 1e-05
SMOOTH = 0.5
THETA = 10000.0
MASKED_SCORE = -1e30
CLIP_NORM = 0.001
BETA_ONE = 0.9
BETA_TWO = 0.95
ADAM_EPS = 1e-08
WEIGHT_DECAY = 0.1
RATE_MATRIX = 0.15
RATE_GAIN = 0.8

BF = jnp.bfloat16
F32 = jnp.float32
AXES = ("fsdp", "dp")


def dot_nn(a, b):
    return lax.dot_general(a, b, (((1,), (0,)), ((), ())), preferred_element_type=F32)


def dot_nt(a, b):
    return lax.dot_general(a, b, (((1,), (1,)), ((), ())), preferred_element_type=F32)


def dot_tn(a, b):
    return lax.dot_general(a, b, (((0,), (0,)), ((), ())), preferred_element_type=F32)


def unit(x):
    inverse = lax.rsqrt(jnp.mean(x * x, axis=-1, keepdims=True) + EPS_NORM)
    return x * inverse, inverse


def rms_backward(u, inverse, gain_row, grad):
    grad_unit = grad * gain_row
    grad_x = inverse * (grad_unit - u * jnp.mean(grad_unit * u, axis=-1, keepdims=True))
    return grad_x, rows_to_eight(grad * u)


def rows_to_eight(x):
    return jnp.sum(x.reshape(x.shape[0] // 8, 8, x.shape[1]), axis=0)


def lane_of(shape):
    return lax.broadcasted_iota(jnp.int32, shape, len(shape) - 1)


def swap_halves(x):
    lane = lane_of(x.shape)
    return jnp.where((lane & 32) == 0, pltpu.roll(x, 96, 1), pltpu.roll(x, 32, 1))


def low_lanes(shape):
    return lane_of(shape) < HD


def two_blocks(x):
    keep = low_lanes(x.shape)
    zero = jnp.zeros_like(x)
    return jnp.concatenate([jnp.where(keep, x, zero), jnp.where(keep, zero, x)], axis=0)


def fold_blocks(x):
    return jnp.where(low_lanes((BUCKET, LANES)), x[:BUCKET], x[BUCKET:])


def half_max(x):
    keep = low_lanes(x.shape)
    floor = jnp.full_like(x, -3e38)
    left = jnp.max(jnp.where(keep, x, floor), axis=-1, keepdims=True)
    right = jnp.max(jnp.where(keep, floor, x), axis=-1, keepdims=True)
    return jnp.where(keep, left, right)


def half_sum(x):
    keep = low_lanes(x.shape)
    zero = jnp.zeros_like(x)
    left = jnp.sum(jnp.where(keep, x, zero), axis=-1, keepdims=True)
    right = jnp.sum(jnp.where(keep, zero, x), axis=-1, keepdims=True)
    return jnp.where(keep, left, right)


def forward_body(first, *refs):
    if first:
        (
            x_ref,
            win_ref,
            wqkv_ref,
            wo_ref,
            wgu_ref,
            wdown_ref,
            gain_ref,
            bias_ref,
            cos_ref,
            sin_ref,
            code_ref,
            base_ref,
            out_ref,
            qkv_ref,
            prob_ref,
            mixed_ref,
            mid_ref,
            gu_ref,
        ) = refs
        stream = dot_nt(x_ref[...], win_ref[...])
        base_ref[...] = stream
    else:
        (
            x_ref,
            wqkv_ref,
            wo_ref,
            wgu_ref,
            wdown_ref,
            gain_ref,
            bias_ref,
            cos_ref,
            sin_ref,
            code_ref,
            out_ref,
            qkv_ref,
            prob_ref,
            mixed_ref,
            mid_ref,
            gu_ref,
        ) = refs
        stream = x_ref[...]
    rows = stream.shape[0]
    normed = (unit(stream)[0] * gain_ref[0:1, :]).astype(BF)
    cos = cos_ref[...]
    sin = sin_ref[...]
    qk = dot_nn(normed, wqkv_ref[:, : 2 * D])
    for j in range(2 * PAIRS):
        part = qk[:, j * LANES : (j + 1) * LANES]
        qkv_ref[:, j * LANES : (j + 1) * LANES] = (part * cos + swap_halves(part) * sin).astype(BF)
    qkv_ref[:, 2 * D :] = dot_nn(normed, wqkv_ref[:, 2 * D :]).astype(BF)
    for b in range(rows // BUCKET):
        here = slice(b * BUCKET, (b + 1) * BUCKET)
        code = code_ref[here, :]
        for p in range(PAIRS):
            q = qkv_ref[here, p * LANES : (p + 1) * LANES]
            k = qkv_ref[here, D + p * LANES : D + (p + 1) * LANES]
            v = qkv_ref[here, 2 * D + p * LANES : 2 * D + (p + 1) * LANES]
            scores = dot_nt(q, two_blocks(k)) * HD ** (-0.5)
            bias = jnp.where(code > 0.5, bias_ref[p + 8 : p + 9, :], bias_ref[p : p + 1, :])
            scores = jnp.where(code < -0.5, MASKED_SCORE, scores + bias)
            e = jnp.exp(scores - half_max(scores))
            prob = (e / half_sum(e)).astype(BF)
            prob_ref[here, p * LANES : (p + 1) * LANES] = prob
            mixed_ref[here, p * LANES : (p + 1) * LANES] = dot_nn(prob, two_blocks(v)).astype(BF)
    middle = stream + dot_nn(mixed_ref[...], wo_ref[...])
    mid_ref[...] = middle
    ffn_in = (unit(middle)[0] * gain_ref[1:2, :]).astype(BF)
    gate_up = dot_nn(ffn_in, wgu_ref[...])
    gu_ref[...] = gate_up.astype(BF)
    gate = gate_up[:, :FF]
    hidden = (gate * (1.0 / (1.0 + jnp.exp(-gate))) * gate_up[:, FF:]).astype(BF)
    out_ref[...] = middle + dot_nn(hidden, wdown_ref[...])


def rows_spec(width):
    return pl.BlockSpec((TILE, width), lambda i: (i, 0))


def whole_spec(shape):
    zeros = (0,) * len(shape)
    return pl.BlockSpec(shape, lambda i: zeros)


def params(limit):
    return pltpu.CompilerParams(
        dimension_semantics=("arbitrary",), vmem_limit_bytes=limit * 1024 * 1024
    )


def forward_layer(x, win, weights, gain_pair, bias_rows, tables):
    first = win is not None
    rows = x.shape[0]
    args = [x] + ([win] if first else []) + list(weights) + [gain_pair, bias_rows] + list(tables)
    in_specs = (
        [rows_spec(x.shape[1])]
        + ([whole_spec(win.shape)] if first else [])
        + [whole_spec(w.shape) for w in weights]
        + [whole_spec(gain_pair.shape), whole_spec(bias_rows.shape)]
        + [rows_spec(LANES)] * 3
    )
    outs = ([(D, F32)] if first else []) + [
        (D, F32),
        (QKV, BF),
        (D, BF),
        (D, BF),
        (D, F32),
        (2 * FF, BF),
    ]
    flops = 2 * rows * (D * QKV + D * D + 3 * D * FF)
    got = pl.pallas_call(
        functools.partial(forward_body, first),
        grid=(rows // TILE,),
        in_specs=in_specs,
        out_specs=[rows_spec(w) for w, _ in outs],
        out_shape=[jax.ShapeDtypeStruct((rows, w), t) for w, t in outs],
        compiler_params=params(48),
        cost_estimate=pl.CostEstimate(flops=flops, bytes_accessed=16 << 20, transcendentals=0),
    )(*args)
    if first:
        return got[1], [got[0]] + list(got[2:])
    return got[0], [x] + list(got[1:])


def head_body(x_ref, target_ref, mask_ref, whead_ref, gain_ref, dx_ref, dw_ref, dg_ref, loss_ref, acc_ref):
    step = pl.program_id(0)

    @pl.when(step == 0)
    def _():
        acc_ref[...] = jnp.zeros_like(acc_ref)
        dg_ref[...] = jnp.zeros_like(dg_ref)
        loss_ref[...] = jnp.zeros_like(loss_ref)

    u, inverse = unit(x_ref[...])
    gain_row = gain_ref[0:1, :]
    final_in = (u * gain_row).astype(BF)
    predicted = dot_nn(final_in, whead_ref[...])
    target = target_ref[...]
    mask = mask_ref[...]
    loss = jnp.zeros((8, PMAX), F32)
    grads = []
    for q in range(NQ):
        level = (q + 1.0) / (NQ + 1)
        r = target - predicted[:, q * PMAX : (q + 1) * PMAX]
        a = r * (-1.0 / SMOOTH)
        e = jnp.exp(-jnp.abs(a))
        recip = 1.0 / (1.0 + e)
        sigmoid = jnp.where(a >= 0, recip, e * recip)
        softplus = jnp.maximum(a, 0.0) + jnp.log(1.0 + e)
        loss = loss + rows_to_eight((level * r + SMOOTH * softplus) * mask)
        grads.append(((sigmoid - level) * mask).astype(BF))
    loss_ref[...] += loss
    grad_pred = jnp.concatenate(grads, axis=1)
    acc_ref[...] += dot_tn(final_in, grad_pred)
    grad_x, grad_gain = rms_backward(u, inverse, gain_row, dot_nt(grad_pred, whead_ref[...]))
    dx_ref[...] = grad_x
    dg_ref[...] += grad_gain

    @pl.when(step == pl.num_programs(0) - 1)
    def _():
        dw_ref[...] = acc_ref[...].astype(BF)


def head(x, targets, mask, whead, gain):
    rows = x.shape[0]
    return pl.pallas_call(
        head_body,
        grid=(rows // TILE,),
        in_specs=[
            rows_spec(D),
            rows_spec(PMAX),
            rows_spec(PMAX),
            whole_spec(whead.shape),
            whole_spec(gain.shape),
        ],
        out_specs=[
            rows_spec(D),
            whole_spec((D, HEADW)),
            whole_spec((8, D)),
            whole_spec((8, PMAX)),
        ],
        out_shape=[
            jax.ShapeDtypeStruct((rows, D), F32),
            jax.ShapeDtypeStruct((D, HEADW), BF),
            jax.ShapeDtypeStruct((8, D), F32),
            jax.ShapeDtypeStruct((8, PMAX), F32),
        ],
        scratch_shapes=[pltpu.VMEM((D, HEADW), F32)],
        compiler_params=params(40),
        cost_estimate=pl.CostEstimate(
            flops=6 * rows * D * HEADW, bytes_accessed=8 << 20, transcendentals=0
        ),
    )(x, targets, mask, whead, gain)


def backward_body(first, *refs):
    if first:
        concat_ref, refs = refs[0], refs[1:]
    (
        dout_ref,
        x_ref,
        qkv_ref,
        prob_ref,
        mixed_ref,
        mid_ref,
        gu_ref,
        wqkv_ref,
        wo_ref,
        wgu_ref,
        wdown_ref,
        gain_ref,
        cos_ref,
        sin_ref,
        code_ref,
        *refs,
    ) = refs
    if first:
        dwin_ref, refs = refs[0], refs[1:]
    else:
        dx_ref, refs = refs[0], refs[1:]
    dqkv_w_ref, do_w_ref, dgu_w_ref, ddown_w_ref, dg_ref, db_ref, *refs = refs
    aqkv_ref, ao_ref, agu_ref, adown_ref, dgu_ref, dqkv_ref = refs[:6]
    step = pl.program_id(0)

    @pl.when(step == 0)
    def _():
        aqkv_ref[...] = jnp.zeros_like(aqkv_ref)
        ao_ref[...] = jnp.zeros_like(ao_ref)
        agu_ref[...] = jnp.zeros_like(agu_ref)
        adown_ref[...] = jnp.zeros_like(adown_ref)
        dg_ref[...] = jnp.zeros_like(dg_ref)
        db_ref[...] = jnp.zeros_like(db_ref)
        if first:
            refs[6][...] = jnp.zeros_like(refs[6])

    dout = dout_ref[...]
    rows = dout.shape[0]
    dout_low = dout.astype(BF)
    gate = gu_ref[:, :FF].astype(F32)
    up = gu_ref[:, FF:].astype(F32)
    sig = 1.0 / (1.0 + jnp.exp(-gate))
    silu = gate * sig
    adown_ref[...] += dot_tn((silu * up).astype(BF), dout_low)
    grad_hidden = dot_nt(dout_low, wdown_ref[...])
    dgu_ref[:, :FF] = (grad_hidden * up * (sig + silu * (1.0 - sig))).astype(BF)
    dgu_ref[:, FF:] = (grad_hidden * silu).astype(BF)
    u_mid, inverse_mid = unit(mid_ref[...])
    gain_mid = gain_ref[1:2, :]
    agu_ref[...] += dot_tn((u_mid * gain_mid).astype(BF), dgu_ref[...])
    grad_mid, dgain_mid = rms_backward(
        u_mid, inverse_mid, gain_mid, dot_nt(dgu_ref[...], wgu_ref[...])
    )
    dg_ref[8:16, :] += dgain_mid
    grad_mid = grad_mid + dout
    grad_attn_low = grad_mid.astype(BF)
    ao_ref[...] += dot_tn(mixed_ref[...], grad_attn_low)
    grad_mixed = dot_nt(grad_attn_low, wo_ref[...]).astype(BF)
    for p in range(PAIRS):
        other_sum = jnp.zeros((8, LANES), F32)
        same_sum = jnp.zeros((8, LANES), F32)
        cols = slice(p * LANES, (p + 1) * LANES)
        kcols = slice(D + p * LANES, D + (p + 1) * LANES)
        vcols = slice(2 * D + p * LANES, 2 * D + (p + 1) * LANES)
        for b in range(rows // BUCKET):
            here = slice(b * BUCKET, (b + 1) * BUCKET)
            code = code_ref[here, :]
            cos = cos_ref[here, :]
            sin = sin_ref[here, :]
            q = qkv_ref[here, cols]
            k2 = two_blocks(qkv_ref[here, kcols])
            v2 = two_blocks(qkv_ref[here, vcols])
            prob_low = prob_ref[here, cols]
            prob = prob_low.astype(F32)
            dm = grad_mixed[here, cols]
            dprob = dot_nt(dm, v2)
            ds = prob * (dprob - half_sum(prob * dprob))
            ds_low = ds.astype(BF)
            ds = ds_low.astype(F32)
            same = code > 0.5
            same_sum = same_sum + rows_to_eight(jnp.where(same, ds, 0.0))
            other_sum = other_sum + rows_to_eight(jnp.where(same, 0.0, ds))
            dq = dot_nn(ds_low, k2) * HD ** (-0.5)
            dk = fold_blocks(dot_tn(ds_low, q)) * HD ** (-0.5)
            dv = fold_blocks(dot_tn(prob_low, dm))
            dqkv_ref[here, cols] = (dq * cos + swap_halves(dq * sin)).astype(BF)
            dqkv_ref[here, kcols] = (dk * cos + swap_halves(dk * sin)).astype(BF)
            dqkv_ref[here, vcols] = dv.astype(BF)
        db_ref[p * 8 : (p + 1) * 8, :] += other_sum
        db_ref[(PAIRS + p) * 8 : (PAIRS + p + 1) * 8, :] += same_sum
    u, inverse = unit(x_ref[...])
    gain_row = gain_ref[0:1, :]
    aqkv_ref[...] += dot_tn((u * gain_row).astype(BF), dqkv_ref[...])
    grad_x, dgain = rms_backward(u, inverse, gain_row, dot_nt(dqkv_ref[...], wqkv_ref[...]))
    dg_ref[0:8, :] += dgain
    grad_x = grad_x + grad_mid
    if first:
        refs[6][...] += dot_tn(grad_x.astype(BF), concat_ref[...])
    else:
        dx_ref[...] = grad_x

    @pl.when(step == pl.num_programs(0) - 1)
    def _():
        dqkv_w_ref[...] = aqkv_ref[...].astype(BF)
        do_w_ref[...] = ao_ref[...].astype(BF)
        dgu_w_ref[...] = agu_ref[...].astype(BF)
        ddown_w_ref[...] = adown_ref[...].astype(BF)
        if first:
            dwin_ref[...] = refs[6][...].astype(BF)


def backward_layer(concat, dout, saved, weights, gain_pair, tables):
    first = concat is not None
    rows = dout.shape[0]
    args = (
        ([concat] if first else [])
        + [dout]
        + list(saved)
        + list(weights)
        + [gain_pair]
        + list(tables)
    )
    in_specs = (
        ([rows_spec(concat.shape[1])] if first else [])
        + [rows_spec(D)]
        + [rows_spec(s.shape[1]) for s in saved]
        + [whole_spec(w.shape) for w in weights]
        + [whole_spec(gain_pair.shape)]
        + [rows_spec(LANES)] * 3
    )
    if first:
        out_specs = [whole_spec((D, concat.shape[1]))]
        out_shape = [jax.ShapeDtypeStruct((D, concat.shape[1]), BF)]
    else:
        out_specs = [rows_spec(D)]
        out_shape = [jax.ShapeDtypeStruct((rows, D), F32)]
    shapes = [(D, QKV), (D, D), (D, 2 * FF), (FF, D)]
    out_specs += [whole_spec(s) for s in shapes] + [whole_spec((16, D)), whole_spec((48, LANES))]
    out_shape += [jax.ShapeDtypeStruct(s, BF) for s in shapes] + [
        jax.ShapeDtypeStruct((16, D), F32),
        jax.ShapeDtypeStruct((48, LANES), F32),
    ]
    scratch = [pltpu.VMEM(s, F32) for s in shapes]
    scratch += [pltpu.VMEM((TILE, 2 * FF), BF), pltpu.VMEM((TILE, QKV), BF)]
    if first:
        scratch.append(pltpu.VMEM((D, concat.shape[1]), F32))
    flops = 4 * rows * (D * QKV + D * D + 3 * D * FF)
    return pl.pallas_call(
        functools.partial(backward_body, first),
        grid=(rows // TILE,),
        in_specs=in_specs,
        out_specs=out_specs,
        out_shape=out_shape,
        scratch_shapes=scratch,
        compiler_params=params(56),
        cost_estimate=pl.CostEstimate(flops=flops, bytes_accessed=24 << 20, transcendentals=0),
    )(*args)


def partners(sizes, fsdp_mask, dp_mask):
    fsdp, dp = sizes
    return [
        (f * dp + d, (f ^ fsdp_mask) * dp + (d ^ dp_mask)) for f in range(fsdp) for d in range(dp)
    ]


def masks_of(size):
    masks = []
    size //= 2
    while size:
        masks.append(size)
        size //= 2
    return masks


def slot_of(offset, masks):
    slot = 0
    for bit, mask in enumerate(masks):
        slot = slot + jnp.where((offset & mask) != 0, 1 << bit, 0)
    return slot


def swap(x, sizes, fsdp_mask, dp_mask):
    return lax.ppermute(x, AXES, partners(sizes, fsdp_mask, dp_mask))


def reorder(slots, masks):
    me = lax.axis_index("fsdp")
    return jnp.stack(
        [
            lax.dynamic_index_in_dim(slots, slot_of(me ^ j, masks), 0, keepdims=False)
            for j in range(slots.shape[0])
        ]
    )


def gather(halves, sizes):
    core = lax.axis_index("dp") & 1
    masks = masks_of(sizes[0])
    mine = jnp.where(core == 0, halves[0], halves[1])[None]
    for mask in masks:
        mine = jnp.concatenate([mine, swap(mine, sizes, mask, 0)], axis=0)
    other = swap(mine, sizes, 0, 1)
    low = jnp.where(core == 0, mine, other)
    high = jnp.where(core == 0, other, mine)
    return reorder(low, masks), reorder(high, masks)


def add(a, b):
    return (a.astype(F32) + b.astype(F32)).astype(BF)


def to_slots(shards, masks):
    me = lax.axis_index("fsdp")
    slots = [None] * shards.shape[0]
    for v in range(shards.shape[0]):
        slot = sum((1 << bit) for bit, mask in enumerate(masks) if v & mask)
        slots[slot] = lax.dynamic_index_in_dim(shards, me ^ v, 0, keepdims=False)
    return jnp.stack(slots)


def scatter(halves, sizes):
    core = lax.axis_index("dp") & 1
    masks = masks_of(sizes[0])
    low, high = halves
    keep = jnp.where(core == 0, low, high)
    give = jnp.where(core == 0, high, low)
    total = to_slots(add(keep, swap(give, sizes, 0, 1)), masks)
    for mask in reversed(masks):
        half = total.shape[0] // 2
        total = add(total[:half], swap(total[half:], sizes, mask, 0))
    total = total[0]
    dp_mask = 2
    while dp_mask < sizes[1]:
        total = add(total, swap(total, sizes, 0, dp_mask))
        dp_mask *= 2
    return total


def exchange(total, sizes):
    core = lax.axis_index("dp") & 1
    other = swap(total, sizes, 0, 1)
    return jnp.where(core == 0, total, other), jnp.where(core == 0, other, total)


def pad_rows(x, rows):
    return jnp.pad(x, ((0, 0),) * (x.ndim - 2) + ((0, rows - x.shape[-2]), (0, 0)))


def pack_layer(qkv, out, gate_up, down):
    rows = qkv.shape[-2]
    parts = [pad_rows(down[..., i * rows : (i + 1) * rows, :], rows) for i in range(3)]
    blank = jnp.zeros(qkv.shape[:-1] + (LANES,), qkv.dtype)
    low = jnp.concatenate([qkv, out, parts[0], parts[1], blank], axis=-1)
    high = jnp.concatenate([gate_up, parts[2]], axis=-1)
    return low, high


def unpack_layer(low, high, down_rows):
    rows = low.shape[-2]
    qkv = low[..., :QKV]
    out = low[..., QKV : QKV + D]
    first = low[..., QKV + D : QKV + 2 * D]
    second = low[..., QKV + 2 * D : QKV + 3 * D]
    gate_up = high[..., : 2 * FF]
    third = high[..., : down_rows - 2 * rows, 2 * FF :]
    return qkv, out, gate_up, jnp.concatenate([first, second, third], axis=-2)


def pack_ends(head_w, in_rows):
    low = head_w[..., : 6 * LANES]
    blank = jnp.zeros(head_w.shape[:-1] + (LANES,), head_w.dtype)
    return low, jnp.concatenate([head_w[..., 6 * LANES :], in_rows, blank], axis=-1)


def unpack_ends(low, high):
    head_w = jnp.concatenate([low, high[..., : 3 * LANES]], axis=-1)
    return head_w, high[..., 3 * LANES : 5 * LANES]


def join_rows(x):
    return x.reshape(x.shape[0] * x.shape[1], x.shape[2])


def rotary_tables(time_ids):
    frequency = THETA ** (-2.0 * jnp.arange(HD // 2, dtype=F32) / HD)
    phase = time_ids.astype(F32)[:, None] * frequency[None, :]
    cos, sin = jnp.cos(phase), jnp.sin(phase)
    return jnp.concatenate([cos] * 4, axis=1), jnp.concatenate([-sin, sin, -sin, sin], axis=1)


def token_tables(size_ids, variate_ids, lengths):
    rows = size_ids.shape[0]
    buckets = rows // BUCKET
    live = jnp.arange(BUCKET, dtype=jnp.int32)[None, :] < lengths[:, None]
    widths = jnp.where(live.reshape(rows), PMAX >> (4 - size_ids), 0)
    mask = (jnp.arange(PMAX, dtype=jnp.int32)[None, :] < widths[:, None]).astype(F32)
    variates = variate_ids.reshape(buckets, BUCKET)
    same = (variates[:, :, None] == variates[:, None, :]).astype(F32)
    code = jnp.where(live[:, None, :], same, -1.0).reshape(rows, BUCKET)
    return mask, jnp.concatenate([code, code], axis=1)


def patch_concat(patches, size_ids):
    pieces = []
    for size_id in range(5):
        span = PMAX >> 4 - size_id
        chosen = (size_ids == size_id)[:, None]
        pieces.append(jnp.where(chosen, patches[:, :span], jnp.zeros((), BF)))
    pieces.append(jnp.zeros((patches.shape[0], 2 * PMAX - IN_CAT), BF))
    return jnp.concatenate(pieces, axis=1)


def adam_update(master, clipped, first_old, second_old, matrix):
    first_new = BETA_ONE * first_old + (1.0 - BETA_ONE) * clipped
    second_new = BETA_TWO * second_old + (1.0 - BETA_TWO) * clipped * clipped
    first_hat = first_new / (1.0 - BETA_ONE**STEP_NUM)
    second_hat = second_new / (1.0 - BETA_TWO**STEP_NUM)
    direction = first_hat / (jnp.sqrt(second_hat) + ADAM_EPS)
    if matrix:
        master_new = master - RATE_MATRIX * (direction + WEIGHT_DECAY * master)
    else:
        master_new = master - RATE_GAIN * direction
    return (master_new, first_new, second_new)


def all_sum(x, sizes, dp_from=1):
    dp_mask = dp_from
    while dp_mask < sizes[1]:
        x = x + swap(x, sizes, 0, dp_mask)
        dp_mask *= 2
    for mask in masks_of(sizes[0]):
        x = x + swap(x, sizes, mask, 0)
    return x


def per_device(sizes, *args):
    patches, targets, size_ids, time_ids, variate_ids, lengths = args[:6]
    masters = args[6:14]
    firsts = args[14:22]
    seconds = args[22:30]
    w_in, w_qkv, w_o, w_gu, w_down, w_head, gains, var_bias = masters
    own = w_head.shape[0]
    down_rows = w_down.shape[1]

    lows, highs = [], []
    for layer in range(L):
        low, high = pack_layer(
            *(w[layer].astype(BF) for w in (w_qkv, w_o, w_gu, w_down))
        )
        lows.append(low)
        highs.append(high)
    in_rows = jnp.concatenate(
        [w_in.T, gains.T, jnp.zeros((own, 2 * PMAX - IN_CAT - NGAIN), F32)], axis=1
    ).astype(BF)
    low, high = pack_ends(w_head.astype(BF), in_rows)
    lows.append(low)
    highs.append(high)
    low, high = gather((jnp.concatenate(lows, axis=1), jnp.concatenate(highs, axis=1)), sizes)
    layer_width = lows[0].shape[1]
    weights = []
    for layer in range(L):
        cols = slice(layer * layer_width, (layer + 1) * layer_width)
        parts = unpack_layer(low[..., cols], high[..., cols], down_rows)
        weights.append(tuple(join_rows(part) for part in parts))
    head_full, in_full = unpack_ends(low[..., L * layer_width :], high[..., L * layer_width :])
    head_full, in_full = join_rows(head_full), join_rows(in_full)
    gain_full = in_full[:, IN_CAT : IN_CAT + NGAIN].T.astype(F32)
    gain_full = jnp.concatenate([gain_full, jnp.zeros((1, D), F32)], axis=0)

    cos, sin = rotary_tables(time_ids)
    mask, code = token_tables(size_ids, variate_ids, lengths)
    tables = (cos, sin, code)
    concat = patch_concat(patches, size_ids)
    count = jnp.sum(mask)
    bias_lanes = jnp.repeat(var_bias, HD, axis=2).reshape(L, 2, PAIRS, LANES)
    bias_lanes = jnp.pad(bias_lanes, ((0, 0), (0, 0), (0, 8 - PAIRS), (0, 0)))
    bias_lanes = bias_lanes.reshape(L, 16, LANES)

    stream = concat
    kept = []
    for layer in range(L):
        stream, saved = forward_layer(
            stream,
            in_full if layer == 0 else None,
            weights[layer],
            gain_full[2 * layer : 2 * layer + 2],
            bias_lanes[layer],
            tables,
        )
        kept.append(saved)
    grad, head_grad, gain_grad, loss = head(
        stream, targets, mask, head_full, gain_full[2 * L : 2 * L + 2]
    )
    loss = jnp.sum(loss)
    gain_grads = {2 * L: jnp.sum(gain_grad, axis=0)}
    bias_grads = [None] * L
    layer_grads = [None] * L
    for layer in reversed(range(L)):
        first, *matrices, gain_grad, bias_grad = backward_layer(
            concat if layer == 0 else None,
            grad,
            kept[layer],
            weights[layer],
            gain_full[2 * layer : 2 * layer + 2],
            tables,
        )
        if layer == 0:
            in_grad = first
        else:
            grad = first
        layer_grads[layer] = matrices
        gain_grads[2 * layer] = jnp.sum(gain_grad[:8], axis=0)
        gain_grads[2 * layer + 1] = jnp.sum(gain_grad[8:], axis=0)
        bias_grads[layer] = jnp.sum(bias_grad.reshape(2, PAIRS, 8, 2, HD), axis=(2, 4)).reshape(2, H)
    gain_grad = jnp.stack([gain_grads[g] for g in range(NGAIN)], axis=1).astype(BF)
    bias_grad = jnp.stack(bias_grads)

    fsdp = sizes[0]

    def shards_of(x):
        return x.reshape(fsdp, x.shape[0] // fsdp, x.shape[1])

    lows, highs = [], []
    for layer in range(L):
        low, high = pack_layer(*(shards_of(g) for g in layer_grads[layer]))
        lows.append(low)
        highs.append(high)
    in_grad = jnp.concatenate(
        [in_grad[:, :IN_CAT], gain_grad, jnp.zeros((D, 2 * PMAX - IN_CAT - NGAIN), BF)], axis=1
    )
    low, high = pack_ends(shards_of(head_grad), shards_of(in_grad))
    lows.append(low)
    highs.append(high)
    total = scatter((jnp.concatenate(lows, axis=-1), jnp.concatenate(highs, axis=-1)), sizes)
    low, high = exchange(total, sizes)

    sums = jnp.concatenate([jnp.stack([loss, count]), bias_grad.reshape(-1)])
    sums = all_sum(jnp.pad(sums, (0, PMAX - sums.shape[0])).reshape(1, PMAX), sizes)[0]
    loss_sum, total_count = sums[0], sums[1]
    inverse_count = 1.0 / total_count
    bias_grad = sums[2 : 2 + bias_grad.size].reshape(bias_grad.shape) * inverse_count

    squares = jnp.sum(jnp.square(low.astype(F32))) + jnp.sum(jnp.square(high.astype(F32)))
    squares = all_sum(squares.reshape(1, 1), sizes, dp_from=sizes[1])[0, 0]
    grad_norm = jnp.sqrt(
        squares * (inverse_count * inverse_count) + jnp.sum(bias_grad * bias_grad)
    )
    factor = jnp.minimum(1.0, CLIP_NORM / grad_norm)
    scale = factor * inverse_count

    pieces = []
    for layer in range(L):
        cols = slice(layer * layer_width, (layer + 1) * layer_width)
        pieces.append(unpack_layer(low[:, cols], high[:, cols], down_rows))
    head_piece, in_piece = unpack_ends(low[:, L * layer_width :], high[:, L * layer_width :])
    gradients = [in_piece[:, :IN_CAT].T]
    gradients += [jnp.stack([pieces[layer][m] for layer in range(L)]) for m in range(4)]
    gradients += [head_piece, in_piece[:, IN_CAT : IN_CAT + NGAIN].T]
    clipped = [g.astype(F32) * scale for g in gradients] + [bias_grad * factor]
    fresh = [
        adam_update(masters[m], clipped[m], firsts[m], seconds[m], m < 6) for m in range(8)
    ]
    return (
        (loss_sum, total_count, grad_norm)
        + tuple(f[0] for f in fresh)
        + tuple(f[1] for f in fresh)
        + tuple(f[2] for f in fresh)
    )


def solution(mesh):
    sizes = (mesh.shape["fsdp"], mesh.shape["dp"])
    tokens = P(("fsdp", "dp"))
    tokens_two = P(("fsdp", "dp"), None)
    columns = P(None, "fsdp")
    stacked = P(None, "fsdp", None)
    states = (columns, stacked, stacked, stacked, stacked, P("fsdp", None), columns, P())
    in_specs = (tokens_two, tokens_two, tokens, tokens, tokens, tokens) + states * 3
    out_specs = (P(), P(), P()) + states * 3
    return jax.shard_map(
        functools.partial(per_device, sizes),
        mesh=mesh,
        in_specs=in_specs,
        out_specs=out_specs,
        check_vma=False,
    )
```

time: 1550 us -> 764 us (0.49)
  blocking collectives: 505 us -> 0 us
  matrix products: 204 us -> 0 us
  local copies, waits for them, and re-layouts: 324 us -> 128 us
  Pallas kernels: 0 us -> 193 us
  waiting for transfers between devices: 344 us -> 301 us
  other arithmetic: 135 us -> 92.8 us
  starting transfers between devices: 1.38 us -> 29.8 us
  between operations: 28 us -> 8.48 us
    all_gather x12 -> x0, blocking collectives: 393 us -> none  [the longest x3 103 us: per_device(): lax.all_gather(w_down[layer_id].astype(jnp.bfloat16), 'fsdp', axis=0, til...]
    ppermute x0 -> x18, waiting for transfers between devices: none -> 301 us  [swap(): return lax.ppermute(x, AXES, partners(sizes, fsdp_mask, dp_mask))]
    reduce_scatter x6 -> x0, waiting for transfers between devices: 292 us -> none  [the longest x1 98.4 us: per_device(): lax.psum_scatter(stacks[2].astype(jnp.bfloat16), 'fsdp', scatter_dimensio...]
    dot_general x118 -> x0, matrix products: 204 us -> none  [the longest x26 44.3 us: dot_right(): lax.dot_general(left_side, right_side, (((1,), (1,)), ((), ())), preferre...]
    pallas_call x0 -> x7, Pallas kernels: none -> 193 us  [the longest x3 109 us: backward_layer(): pl.pallas_call(functools.partial(backward_body, first), grid=(rows // TIL...]
    psum x4 -> x0, blocking collectives: 111 us -> none  [the longest x1 40.3 us: per_device(): loss_sum, bias_grad = lax.psum((loss_local, grad_bias_acc), ('fsdp', 'dp'))]
    reshape x36 -> x4, local copies, waits for them, and re-layouts: 79.9 us -> 0.36 us  [the longest x3 0.27 us: per_device(): bias_grad.reshape(2, PAIRS, 8, 2, HD)]
    mul x17 -> x1, local copies, waits for them, and re-layouts: 42.4 us -> 0.09 us  [per_device(): clipped = [g.astype(F32) * scale for g in gradients] + [bias_grad * factor]]
  transfers between devices with their start and end apart: 11 -> 18, of which waited for: 6 -> 14; matrix products, arithmetic and copies ran while one was open for 22% -> 6% of each run, Pallas kernels for 0% -> 0%
where the time goes in v1:
time: 764 us; the launch traced here: 753 us
  waiting for transfers between devices  301 us (39%)
  Pallas kernels  193 us (25%)
  local copies, waits for them, and re-layouts  128 us (17%)
  other arithmetic  92.8 us (12%)
  starting transfers between devices  29.8 us (4%)
  between operations  8.48 us (1%)
    ppermute x18, waiting for transfers between devices, swap(): return lax.ppermute(x, AXES, partners(sizes, fsdp_mask, dp_mask))  301 us
    pallas_call x3, Pallas kernels, backward_layer(): pl.pallas_call(functools.partial(backward_body, first), grid=(rows // TIL...  109 us
    pallas_call x3, Pallas kernels, forward_layer(): pl.pallas_call(functools.partial(forward_body, first), grid=(rows // TILE...  75.3 us
    unnamed x234, local copies, waits for them, and re-layouts  51.9 us
    ppermute x18, starting transfers between devices, swap(): return lax.ppermute(x, AXES, partners(sizes, fsdp_mask, dp_mask))  29.8 us
    convert_element_type x4, other arithmetic, add(): return (a.astype(F32) + b.astype(F32)).astype(BF)  23.6 us
    ppermute x5, local copies, waits for them, and re-layouts, swap(): return lax.ppermute(x, AXES, partners(sizes, fsdp_mask, dp_mask))  18 us
  transfers between devices with their start and end apart: 18, of which 14 were waited for; matrix products, arithmetic and copies ran while one was open for 6% of the time, Pallas kernels for 0%

profile of v1, /device:TPU:0, one launch (start us, length us, event | category | flops | bytes accessed | tf_op | source)
XLA Modules:
  0.0 752.5 jit_solution(7503493708635705828)
XLA Ops:
  7.1 4.1 collective-permute-start
  11.2 33.9 %collective-permute-done = bf16[1,48,8064]{2,1,0:T(8,128)(2,1)S(1)} collective-permute-done((bf16[1,48,8064]{2,1,0:T(8,128)(2,1)S(1)}, bf16[1,48,8064]{2,1,0:T(8,128)(2,1)S(1)}, u32[]{:S(2)}, u32[]{:S(2)}) %collective-permute-start) | collective-permute-done | bytes 774176 | tf_op jit(solution)/shard_map/ppermute | solution.py:495
  46.0 34.3 %collective-permute-done.1 = bf16[2,48,8064]{2,1,0:T(8,128)(2,1)S(1)} collective-permute-done((bf16[2,48,8064]{2,1,0:T(8,128)(2,1)S(1)}, bf16[2,48,8064]{2,1,0:T(8,128)(2,1)S(1)}, u32[]{:S(2)}, u32[]{:S(2)}) %collective-permute-start.1) | collective-permute-done | bytes 1548320 | tf_op jit(solution)/shard_map/ppermute | solution.py:495
  82.1 66.0 %collective-permute-done.2 = bf16[4,48,8064]{2,1,0:T(8,128)(2,1)S(1)} collective-permute-done((bf16[4,48,8064]{2,1,0:T(8,128)(2,1)S(1)}, bf16[4,48,8064]{2,1,0:T(8,128)(2,1)S(1)}, u32[]{:S(2)}, u32[]{:S(2)}) %collective-permute-start.2) | collective-permute-done | bytes 3096608 | tf_op jit(solution)/shard_map/ppermute | solution.py:495
  164.3 4.3 broadcast_select_fusion.1
  183.5 26.6 %shard_map.493 = (f32[1024,384]{1,0:T(8,128)}, f32[1024,384]{1,0:T(8,128)}, bf16[1024,1152]{1,0:T(8,128)(2,1)}, bf16[1024,384]{1,0:T(8,128)(2,1)S(1)}, bf16[1024...) custom-call(bf16[1024,256]{1,0:T(8,128)(2,1)S(1)} %copy-done.10, ...), custom_call_target="tpu_custom_call" | custom-call | flops 3623878656 | bytes 16777216 | tf_op jit(solution)/shard_map/pallas_call | solution.py:223
  210.2 24.5 %shard_map.494 = (f32[1024,384]{1,0:T(8,128)}, bf16[1024,1152]{1,0:T(8,128)(2,1)}, bf16[1024,384]{1,0:T(8,128)(2,1)S(1)}, bf16[1024,384]{1,0:T(8,128)(2,1)S(1)},...) custom-call(f32[1024,384]{1,0:T(8,128)} %get-tuple-element.71.refs_0_.refs_1_, bf16[384,1152]{1,0:T(8,128)(2,1)S(1)} %bitcast.126, ...), custom_call_target="tpu_custom_call" | custom-call | flops 3623878656 | bytes 16777216 | tf_op jit(solution)/shard_map/pallas_call | solution.py:223
  235.6 24.2 %shard_map.495 = (f32[1024,384]{1,0:T(8,128)}, bf16[1024,1152]{1,0:T(8,128)(2,1)}, bf16[1024,384]{1,0:T(8,128)(2,1)S(1)}, bf16[1024,384]{1,0:T(8,128)(2,1)S(1)},...) custom-call(f32[1024,384]{1,0:T(8,128)} %get-tuple-element.72.refs_0_.refs_1_, bf16[384,1152]{1,0:T(8,128)(2,1)S(1)} %bitcast.128, ...), custom_call_target="tpu_custom_call" | custom-call | flops 3623878656 | bytes 16777216 | tf_op jit(solution)/shard_map/pallas_call | solution.py:223
  262.4 8.4 %shard_map.496 = (f32[1024,384]{1,0:T(8,128)S(1)}, bf16[384,1152]{1,0:T(8,128)(2,1)S(1)}, f32[8,384]{1,0:T(8,128)S(1)}, f32[8,128]{1,0:T(8,128)S(1)}) custom-call(f32[1024,384]{1,0:T(8,128)S(1)} %copy-done.19, f32[1024,128]{1,0:T(8,128)S(1)} %copy-done.17, f32[1024,128]{1,0:T(8,128)S(1)} %copy-done.9, bf16[384,1152]{1,0:T(8,128)(2,1)S(1)} %bitcast.121, ...), custom_call_target="tpu_custom_call" | custom-call | flops 2717908992 | bytes 8388608 | tf_op jit(solution)/shard_map/pallas_call | solution.py:278
  272.0 36.3 %shard_map.497 = (f32[1024,384]{1,0:T(8,128)}, bf16[384,1152]{1,0:T(8,128)(2,1)}, bf16[384,384]{1,0:T(8,128)(2,1)}, bf16[384,2048]{1,0:T(8,128)(2,1)}, bf16[1024...) custom-call(f32[1024,384]{1,0:T(8,128)} %copy-done.18, f32[1024,384]{1,0:T(8,128)} %get-tuple-element.72.refs_0_.refs_1_, ...), custom_call_target="tpu_custom_call" | custom-call | flops 7247757312 | bytes 25165824 | tf_op jit(solution)/shard_map/pallas_call | solution.py:459
  308.3 35.9 %shard_map.498 = (f32[1024,384]{1,0:T(8,128)}, bf16[384,1152]{1,0:T(8,128)(2,1)}, bf16[384,384]{1,0:T(8,128)(2,1)}, bf16[384,2048]{1,0:T(8,128)(2,1)}, bf16[1024...) custom-call(f32[1024,384]{1,0:T(8,128)} %get-tuple-element.81.refs_0_, ...), custom_call_target="tpu_custom_call" | custom-call | flops 7247757312 | bytes 25165824 | tf_op jit(solution)/shard_map/pallas_call | solution.py:459
  344.2 37.1 %shard_map.499 = (bf16[384,256]{1,0:T(8,128)(2,1)}, bf16[384,1152]{1,0:T(8,128)(2,1)}, bf16[384,384]{1,0:T(8,128)(2,1)}, bf16[384,2048]{1,0:T(8,128)(2,1)}, bf16...) custom-call(bf16[1024,256]{1,0:T(8,128)(2,1)} %concatenate.109.refs_0_, ...), custom_call_target="tpu_custom_call" | custom-call | flops 7247757312 | bytes 25165824 | tf_op jit(solution)/shard_map/pallas_call | solution.py:459
  411.9 6.1 broadcast_select_fusion
  418.4 10.0 %collective-permute-done.9 = bf16[8,48,8064]{2,1,0:T(8,128)(2,1)} collective-permute-done((bf16[8,48,8064]{2,1,0:T(8,128)(2,1)}, bf16[8,48,8064]{2,1,0:T(8,128)(2,1)}, u32[]{:S(2)}, u32[]{:S(2)}) %collective-permute-start.9) | collective-permute-done | bytes 6193184 | tf_op jit(solution)/shard_map/ppermute | solution.py:495
  428.4 9.4 %add_convert_fusion.1 = bf16[8,48,8064]{2,1,0:T(8,128)(2,1)} fusion(bf16[8,48,8064]{2,1,0:T(8,128)(2,1)} %collective-permute-done.9, bf16[8,48,8064]{2,1,0:T(8,128)(2,1)} %slice_dynamic-update-slice_fusion, bf16[8,48,8064]{2,1,0:T(8,128)(2,1)} %constant_dynamic-update-slice_fusion.31, pred[]{:T(512)S(6)} %eq.63), kind=kLoop, calls=%fused_computation.1 | loop fusion | flops 15482880 | bytes 24772608 | tf_op jit(solution)/shard_map/convert_element_type | solution.py:521
  445.0 6.1 copy.260
  451.1 61.8 %collective-permute-done.10 = bf16[4,48,8064]{2,1,0:T(8,128)(2,1)} collective-permute-done((bf16[4,48,8064]{2,1,0:T(8,128)(2,1)}, bf16[4,48,8064]{2,1,0:T(8,128)(2,1)}, u32[]{:S(2)}, u32[]{:S(2)}) %collective-permute-start.10) | collective-permute-done | bytes 3096608 | tf_op jit(solution)/shard_map/ppermute | solution.py:495
  512.9 8.1 %copy.261 = bf16[4,48,8064]{1,2,0:T(8,128)(2,1)} copy(bf16[4,48,8064]{2,1,0:T(8,128)(2,1)} %collective-permute-done.10) | data formatting | bytes 6193152 | tf_op jit(solution)/shard_map/ppermute | solution.py:495
  521.0 6.9 add_convert_fusion
  539.6 33.6 %collective-permute-done.11 = bf16[2,48,8064]{2,1,0:T(8,128)(2,1)S(1)} collective-permute-done((bf16[2,48,8064]{2,1,0:T(8,128)(2,1)S(1)}, bf16[2,48,8064]{2,1,0:T(8,128)(2,1)S(1)}, u32[]{:S(2)}, u32[]{:S(2)}) %collective-permute-start.11) | collective-permute-done | bytes 1548320 | tf_op jit(solution)/shard_map/ppermute | solution.py:495
  576.5 4.5 add_convert_fusion.2
  588.6 32.8 %collective-permute-done.12 = bf16[1,48,8064]{2,1,0:T(8,128)(2,1)S(1)} collective-permute-done((bf16[1,48,8064]{2,1,0:T(8,128)(2,1)S(1)}, bf16[1,48,8064]{2,1,0:T(8,128)(2,1)S(1)}, u32[]{:S(2)}, u32[]{:S(2)}) %collective-permute-start.12) | collective-permute-done | bytes 774176 | tf_op jit(solution)/shard_map/ppermute | solution.py:495
  629.7 17.2 %collective-permute-done.13 = bf16[48,8064]{1,0:T(8,128)(2,1)S(1)} collective-permute-done((bf16[48,8064]{1,0:T(8,128)(2,1)}, bf16[48,8064]{1,0:T(8,128)(2,1)S(1)}, u32[]{:S(2)}, u32[]{:S(2)}) %collective-permute-start.13) | collective-permute-done | bytes 774176 | tf_op jit(solution)/shard_map/ppermute | solution.py:495
  663.6 4.4 collective-permute-done.6
  (399 shorter events, 207.4 us)
Async XLA Ops:
  7.1 38.0 %collective-permute-start = (bf16[1,48,8064]{2,1,0:T(8,128)(2,1)S(1)}, bf16[1,48,8064]{2,1,0:T(8,128)(2,1)S(1)}, u32[]{:S(2)}, u32[]{:S(2)}) collective-permute-start(bf16[1,48,8064]{2,1,0:T(8,128)(2,1)S(1)} %broadcast_select_fusion.5), channel_id=1, source_target_pairs={{0,16},{1,17},{2,18},{3,19},{4,20},{5,21},{6,22},{7,23},{8,24},{9,... | collective-permute-start | bytes 2322440 | tf_op jit(solution)/shard_map/ppermute | solution.py:495
  45.0 106.6 %copy-start.32 = (bf16[1,48,8064]{2,1,0:T(8,128)(2,1)}, bf16[1,48,8064]{2,1,0:T(8,128)(2,1)S(1)}, u32[]{:S(2)}) copy-start(bf16[1,48,8064]{2,1,0:T(8,128)(2,1)S(1)} %collective-permute-done) | copy-start | bytes 2322436
  45.2 35.1 %collective-permute-start.1 = (bf16[2,48,8064]{2,1,0:T(8,128)(2,1)S(1)}, bf16[2,48,8064]{2,1,0:T(8,128)(2,1)S(1)}, u32[]{:S(2)}, u32[]{:S(2)}) collective-permute-start(bf16[2,48,8064]{2,1,0:T(8,128)(2,1)S(1)} %pad_maximum_fusion.4), channel_id=1, source_target_pairs={{0,8},{1,9},{2,10},{3,11},{4,12},{5,13},{6,14},{7,15},{8,0},{9,1},... | collective-permute-start | bytes 4644872 | tf_op jit(solution)/shard_map/ppermute | solution.py:495
  80.7 71.2 %copy-start.80 = (s32[16]{0:T(128)S(1)}, s32[16]{0:T(128)}, u32[]{:S(2)}) copy-start(s32[16]{0:T(128)} %param.35) | copy-start | bytes 196
  80.7 71.5 %copy-start.77 = (f32[3,2,6]{2,1,0:T(2,128)S(1)}, f32[3,2,6]{2,1,0:T(2,128)}, u32[]{:S(2)}) copy-start(f32[3,2,6]{2,1,0:T(2,128)} %param.43) | copy-start | bytes 436
  80.7 71.7 %copy-start.74 = (s32[1024]{0:T(1024)S(1)}, s32[1024]{0:T(1024)}, u32[]{:S(2)}) copy-start(s32[1024]{0:T(1024)} %param.32) | copy-start | bytes 12292
  80.7 71.7 %copy-start.35 = (bf16[1024,128]{1,0:T(8,128)(2,1)S(1)}, bf16[1024,128]{1,0:T(8,128)(2,1)}, u32[]{:S(2)}) copy-start(bf16[1024,128]{1,0:T(8,128)(2,1)} %param.30) | copy-start | bytes 786436
  80.8 67.4 %collective-permute-start.2 = (bf16[4,48,8064]{2,1,0:T(8,128)(2,1)S(1)}, bf16[4,48,8064]{2,1,0:T(8,128)(2,1)S(1)}, u32[]{:S(2)}, u32[]{:S(2)}) collective-permute-start(bf16[4,48,8064]{2,1,0:T(8,128)(2,1)S(1)} %pad_maximum_fusion.1), channel_id=1, source_target_pairs={{0,4},{1,5},{2,6},{3,7},{4,0},{5,1},{6,2},{7,3},{8,12},{9,13},{10,... | collective-permute-start | bytes 9289736 | tf_op jit(solution)/shard_map/ppermute | solution.py:495
  151.6 12.7 %collective-permute-start.3 = (bf16[8,48,8064]{2,1,0:T(8,128)(2,1)}, bf16[8,48,8064]{2,1,0:T(8,128)(2,1)}, u32[]{:S(2)}, u32[]{:S(2)}) collective-permute-start(bf16[8,48,8064]{2,1,0:T(8,128)(2,1)} %pad_maximum_fusion), channel_id=1, source_target_pairs={{0,1},{1,0},{2,3},{3,2},{4,5},{5,4},{6,7},{7,6},{8,9},{9,8},{10,11... | collective-permute-start | bytes 18579464 | tf_op jit(solution)/shard_map/ppermute | solution.py:495
  163.3 72.2 %copy-start.6 = (f32[1024,128]{1,0:T(8,128)}, f32[1024,128]{1,0:T(8,128)S(1)}, u32[]{:S(2)}) copy-start(f32[1024,128]{1,0:T(8,128)S(1)} %get-tuple-element.327.refs_8_.refs_7_.refs_12_.refs_13_) | copy-start | bytes 1572868
  418.1 10.4 %collective-permute-start.9 = (bf16[8,48,8064]{2,1,0:T(8,128)(2,1)}, bf16[8,48,8064]{2,1,0:T(8,128)(2,1)}, u32[]{:S(2)}, u32[]{:S(2)}) collective-permute-start(bf16[8,48,8064]{2,1,0:T(8,128)(2,1)} %broadcast_select_fusion), channel_id=1, source_target_pairs={{0,1},{1,0},{2,3},{3,2},{4,5},{5,4},{6,7},{7,6},{8,9},{9,8},{10,11... | collective-permute-start | bytes 18579464 | tf_op jit(solution)/shard_map/ppermute | solution.py:495
  443.1 69.7 %collective-permute-start.10 = (bf16[4,48,8064]{2,1,0:T(8,128)(2,1)}, bf16[4,48,8064]{2,1,0:T(8,128)(2,1)}, u32[]{:S(2)}, u32[]{:S(2)}) collective-permute-start(bf16[4,48,8064]{2,1,0:T(8,128)(2,1)} %pad_maximum_fusion.3), channel_id=1, source_target_pairs={{0,4},{1,5},{2,6},{3,7},{4,0},{5,1},{6,2},{7,3},{8,12},{9,13},{10,... | collective-permute-start | bytes 9289736 | tf_op jit(solution)/shard_map/ppermute | solution.py:495
  537.3 35.9 %collective-permute-start.11 = (bf16[2,48,8064]{2,1,0:T(8,128)(2,1)S(1)}, bf16[2,48,8064]{2,1,0:T(8,128)(2,1)S(1)}, u32[]{:S(2)}, u32[]{:S(2)}) collective-permute-start(bf16[2,48,8064]{2,1,0:T(8,128)(2,1)S(1)} %copy.262), channel_id=1, source_target_pairs={{0,8},{1,9},{2,10},{3,11},{4,12},{5,13},{6,14},{7,15},{8,0},{9,1},... | collective-permute-start | bytes 4644872 | tf_op jit(solution)/shard_map/ppermute | solution.py:495
  584.6 36.8 %collective-permute-start.12 = (bf16[1,48,8064]{2,1,0:T(8,128)(2,1)S(1)}, bf16[1,48,8064]{2,1,0:T(8,128)(2,1)S(1)}, u32[]{:S(2)}, u32[]{:S(2)}) collective-permute-start(bf16[1,48,8064]{2,1,0:T(8,128)(2,1)S(1)} %copy.264), channel_id=1, source_target_pairs={{0,16},{1,17},{2,18},{3,19},{4,20},{5,21},{6,22},{7,23},{8,24},{9,... | collective-permute-start | bytes 2322440 | tf_op jit(solution)/shard_map/ppermute | solution.py:495
  628.2 18.7 %collective-permute-start.13 = (bf16[48,8064]{1,0:T(8,128)(2,1)}, bf16[48,8064]{1,0:T(8,128)(2,1)S(1)}, u32[]{:S(2)}, u32[]{:S(2)}) collective-permute-start(bf16[48,8064]{1,0:T(8,128)(2,1)} %copy.266), channel_id=1, source_target_pairs={{0,2},{1,3},{2,0},{3,1},{4,6},{5,7},{6,4},{7,5},{8,10},{9,11},{10,... | collective-permute-start | bytes 2322440 | tf_op jit(solution)/shard_map/ppermute | solution.py:495
  653.6 27.6 %collective-permute-start.14 = (bf16[48,8064]{1,0:T(8,128)(2,1)}, bf16[48,8064]{1,0:T(8,128)(2,1)}, u32[]{:S(2)}, u32[]{:S(2)}) collective-permute-start(bf16[48,8064]{1,0:T(8,128)(2,1)} %copy.268), channel_id=1, source_target_pairs={{0,1},{1,0},{2,3},{3,2},{4,5},{5,4},{6,7},{7,6},{8,9},{9,8},{10,11... | collective-permute-start | bytes 2322440 | tf_op jit(solution)/shard_map/ppermute | solution.py:495
  657.3 1.3 collective-permute-start.4
  660.0 3.5 collective-permute-start.5
  663.6 4.4 collective-permute-start.6
  668.0 3.5 collective-permute-start.7
  671.6 7.6 %collective-permute-start.8 = (f32[1,128]{1,0:T(1,128)S(1)}, f32[1,128]{1,0:T(1,128)S(1)}, u32[]{:S(2)}, u32[]{:S(2)}) collective-permute-start(f32[1,128]{1,0:T(1,128)S(1)} %add.326), channel_id=1, source_target_pairs={{0,4},{1,5},{2,6},{3,7},{4,0},{5,1},{6,2},{7,3},{8,12},{9,13},{10,... | collective-permute-start | bytes 1544 | tf_op jit(solution)/shard_map/ppermute | solution.py:495
  693.8 20.6 %collective-permute-start.15 = (f32[1,1]{1,0:T(1,128)}, f32[1,1]{1,0:T(1,128)}, u32[]{:S(2)}, u32[]{:S(2)}) collective-permute-start(f32[1,1]{1,0:T(1,128)} %bitcast.51), channel_id=1, source_target_pairs={{0,16},{1,17},{2,18},{3,19},{4,20},{5,21},{6,22},{7,23},{8,24},{9,... | collective-permute-start | bytes 20 | tf_op jit(solution)/shard_map/ppermute | solution.py:495
  715.1 3.7 collective-permute-start.16
  719.4 3.7 collective-permute-start.17
  (75 other events, 1582.4 us)

commit v2 on v1

v2 whole, which is shorter than its diff:
```python
import functools

import jax
import jax.numpy as jnp
from jax import lax
from jax.experimental import pallas as pl
from jax.experimental.pallas import tpu as pltpu
from jax.sharding import PartitionSpec as P

D = 384
H = 6
HD = 64
FF = 1024
PMAX = 128
NQ = 9
BUCKET = 64
L = 3
STEP_NUM = 10
IN_CAT = 248
NGAIN = 7
QKV = 3 * D
HEADW = NQ * PMAX
PAIRS = H // 2
LANES = 2 * HD

TILE = 256

EPS_NORM = 1e-05
SMOOTH = 0.5
THETA = 10000.0
MASKED_SCORE = -1e30
CLIP_NORM = 0.001
BETA_ONE = 0.9
BETA_TWO = 0.95
ADAM_EPS = 1e-08
WEIGHT_DECAY = 0.1
RATE_MATRIX = 0.15
RATE_GAIN = 0.8

BF = jnp.bfloat16
F32 = jnp.float32
AXES = ("fsdp", "dp")


def dot_nn(a, b):
    return lax.dot_general(a, b, (((1,), (0,)), ((), ())), preferred_element_type=F32)


def dot_nt(a, b):
    return lax.dot_general(a, b, (((1,), (1,)), ((), ())), preferred_element_type=F32)


def dot_tn(a, b):
    return lax.dot_general(a, b, (((0,), (0,)), ((), ())), preferred_element_type=F32)


def unit(x):
    inverse = lax.rsqrt(jnp.mean(x * x, axis=-1, keepdims=True) + EPS_NORM)
    return x * inverse, inverse


def rms_backward(u, inverse, gain_row, grad):
    grad_unit = grad * gain_row
    grad_x = inverse * (grad_unit - u * jnp.mean(grad_unit * u, axis=-1, keepdims=True))
    return grad_x, rows_to_eight(grad * u)


def rows_to_eight(x):
    return jnp.sum(x.reshape(x.shape[0] // 8, 8, x.shape[1]), axis=0)


def lane_of(shape):
    return lax.broadcasted_iota(jnp.int32, shape, len(shape) - 1)


def swap_halves(x):
    lane = lane_of(x.shape)
    return jnp.where((lane & 32) == 0, pltpu.roll(x, 96, 1), pltpu.roll(x, 32, 1))


def low_lanes(shape):
    return lane_of(shape) < HD


def two_blocks(x):
    keep = low_lanes(x.shape)
    zero = jnp.zeros_like(x)
    return jnp.concatenate([jnp.where(keep, x, zero), jnp.where(keep, zero, x)], axis=0)


def fold_blocks(x):
    return jnp.where(low_lanes((BUCKET, LANES)), x[:BUCKET], x[BUCKET:])


def sigmoid_of(x):
    return 0.5 * jnp.tanh(0.5 * x) + 0.5


class Group:
    def __init__(self, extra, shards, rows, down_rows):
        self.shards, self.rows, self.down_rows = shards, rows, down_rows
        fields = [("qkv", QKV), ("o", D), ("d0", D), ("d1", D), ("gu", 2 * FF), ("d2", D)] + extra
        used = sum(width for _, width in fields)
        self.half = -(-used // (2 * LANES)) * LANES
        self.pad = 2 * self.half - used
        self.fields = fields
        self.pieces = []
        at = 0
        for name, width in fields:
            done = 0
            while done < width:
                half = (at + done) // self.half
                take = min(width - done, (half + 1) * self.half - at - done)
                self.pieces.append((half, at + done - half * self.half, name, done, take))
                done += take
            at += width

    def row_span(self, name):
        if name[0] == "d":
            first = int(name[1]) * self.rows
            return first, min(self.rows, self.down_rows - first), self.down_rows
        return 0, self.rows, self.rows

    def pack(self, parts):
        parts = dict(parts)
        if "d" in parts:
            down = parts.pop("d")
            for i in range(3):
                part = down[..., i * self.rows : (i + 1) * self.rows, :]
                parts[f"d{i}"] = pad_rows(part, self.rows)
        halves = [[], []]
        for half, _, name, start, width in self.pieces:
            halves[half].append(parts[name][..., start : start + width])
        if self.pad:
            like = halves[1][0]
            halves[1].append(jnp.zeros(like.shape[:-1] + (self.pad,), like.dtype))
        return tuple(jnp.concatenate(h, axis=-1) for h in halves)

    def unpack(self, halves):
        found = {}
        for half, at, name, _, width in self.pieces:
            part = halves[half][..., at : at + width]
            found[name] = jnp.concatenate([found[name], part], axis=-1) if name in found else part
        downs = [found.pop(f"d{i}") for i in range(3)]
        downs[2] = downs[2][..., : self.row_span("d2")[1], :]
        found["d"] = jnp.concatenate(downs, axis=-2)
        return found


def place(group):
    if group.shards == 1:
        return 0, 0
    return lax.axis_index("fsdp"), lax.axis_index("dp") & 1


def copies(group, halves, core, me, targets, sems, outward):
    masks = masks_of(group.shards)
    made = {}
    for n, (half, at, name, start, width) in enumerate(group.pieces):
        if name not in targets:
            continue
        first, count, stride = group.row_span(name)
        for v in range(group.shards):
            row = (me ^ v) * stride + first if group.shards > 1 else first
            if group.shards > 1:
                row = pl.multiple_of(row, 16)
            whole = targets[name].at[pl.ds(row, count), pl.ds(start, width)]
            slots = [h.at[slot_index(v, masks), pl.ds(0, count), pl.ds(at, width)] for h in halves]
            ends = [(whole, slot) if outward else (slot, whole) for slot in slots]
            pair = [
                functools.partial(pltpu.make_async_copy, a, b, sems.at[n, v]) for a, b in ends
            ]
            made.setdefault(name, []).append((half, pair))
    return made


def start_copies(group, made, core):
    def go(which):
        for items in made.values():
            for half, pair in items:
                pair[0 if half == which else 1]().start()

    if group.shards == 1:
        go(0)
    else:
        pl.when(core == 0)(functools.partial(go, 0))
        pl.when(core == 1)(functools.partial(go, 1))


def wait_copies(made, names):
    for name in names:
        for _, pair in made.get(name, []):
            pair[0]().wait()


def slot_index(v, masks):
    return sum((1 << bit) for bit, mask in enumerate(masks) if v & mask)


def masks_of(size):
    masks = []
    size //= 2
    while size:
        masks.append(size)
        size //= 2
    return masks


def any_spec():
    return pl.BlockSpec(memory_space=pl.ANY)


WEIGHTS = {"qkv": (D, QKV), "o": (D, D), "gu": (D, 2 * FF), "d": (FF, D)}


def weight_scratch(group, more=()):
    shapes = [WEIGHTS[name] for name in WEIGHTS] + list(more)
    return [pltpu.VMEM(shape, BF) for shape in shapes] + [
        pltpu.SemaphoreType.DMA((len(group.pieces), group.shards))
    ]


def down_fields(targets):
    targets = dict(targets)
    down = targets.pop("d")
    return {**targets, "d0": down, "d1": down, "d2": down}


def forward_body(first, group, *refs):
    refs = list(refs)
    x_ref, mine_ref, other_ref = refs[:3]
    refs = refs[3:]
    gain_ref = None if first else refs.pop(0)
    bias_ref, cos_ref, sin_ref, code_ref = refs[:4]
    refs = refs[4:]
    if first:
        base_ref, rows_ref = refs[:2]
        refs = refs[2:]
    out_ref, qkv_ref, prob_ref, mixed_ref, mid_ref, gu_ref = refs[:6]
    wqkv_ref, wo_ref, wgu_ref, wdown_ref = refs[6:10]
    sems = refs[-1]
    targets = {"qkv": wqkv_ref, "o": wo_ref, "gu": wgu_ref, "d": wdown_ref}
    if first:
        win_ref, gain_ref = refs[10], refs[11]
        targets["in"] = win_ref
    me, core = place(group)
    made = copies(
        group, (mine_ref, other_ref), core, me, down_fields(targets), sems, outward=False
    )
    opening = pl.program_id(0) == 0

    @pl.when(opening)
    def _():
        start_copies(group, made, core)
        wait_copies(made, ("in", "qkv"))
        if first:
            turned = win_ref[:, PMAX:].astype(F32).T
            gain_ref[...] = turned[IN_CAT - PMAX : IN_CAT - PMAX + 8, :]
            rows_ref[...] = gain_ref[...]

    if first:
        stream = dot_nt(x_ref[...], win_ref[...])
        base_ref[...] = stream
        gains = (gain_ref[0:1, :], gain_ref[1:2, :])
    else:
        stream = x_ref[...]
        gains = (gain_ref[0:1, :], gain_ref[1:2, :])
    rows = stream.shape[0]
    normed = (unit(stream)[0] * gains[0]).astype(BF)
    cos = cos_ref[...]
    sin = sin_ref[...]
    qk = dot_nn(normed, wqkv_ref[:, : 2 * D])
    for j in range(2 * PAIRS):
        part = qk[:, j * LANES : (j + 1) * LANES]
        qkv_ref[:, j * LANES : (j + 1) * LANES] = (part * cos + swap_halves(part) * sin).astype(BF)
    qkv_ref[:, 2 * D :] = dot_nn(normed, wqkv_ref[:, 2 * D :]).astype(BF)
    spots = [(b, p) for b in range(rows // BUCKET) for p in range(PAIRS)]
    scores = []
    for b, p in spots:
        here = slice(b * BUCKET, (b + 1) * BUCKET)
        q = qkv_ref[here, p * LANES : (p + 1) * LANES]
        k = qkv_ref[here, D + p * LANES : D + (p + 1) * LANES]
        scores.append(dot_nt(k, two_blocks(q)))
    probs = []
    for (b, p), score in zip(spots, scores):
        code = code_ref[b * BUCKET : (b + 1) * BUCKET, :]
        bias = jnp.where(code > 0.5, bias_ref[p + 8 : p + 9, :], bias_ref[p : p + 1, :])
        score = jnp.where(code < -0.5, MASKED_SCORE, score * HD ** (-0.5) + bias)
        e = jnp.exp(score - jnp.max(score, axis=0, keepdims=True))
        probs.append((e * (1.0 / jnp.sum(e, axis=0, keepdims=True))).astype(BF))
    for (b, p), prob in zip(spots, probs):
        here = slice(b * BUCKET, (b + 1) * BUCKET)
        cols = slice(p * LANES, (p + 1) * LANES)
        v = qkv_ref[here, 2 * D + p * LANES : 2 * D + (p + 1) * LANES]
        prob_ref[here, cols] = prob
        mixed_ref[here, cols] = fold_blocks(dot_tn(prob, v)).astype(BF)

    @pl.when(opening)
    def _():
        wait_copies(made, ("o", "d0", "d1", "gu", "d2"))

    middle = stream + dot_nn(mixed_ref[...], wo_ref[...])
    mid_ref[...] = middle
    ffn_in = (unit(middle)[0] * gains[1]).astype(BF)
    gate_up = dot_nn(ffn_in, wgu_ref[...])
    gu_ref[...] = gate_up.astype(BF)
    gate = gate_up[:, :FF]
    hidden = (gate * sigmoid_of(gate) * gate_up[:, FF:]).astype(BF)
    out_ref[...] = middle + dot_nn(hidden, wdown_ref[...])


def rows_spec(width):
    return pl.BlockSpec((TILE, width), lambda i: (i, 0))


def whole_spec(shape):
    zeros = (0,) * len(shape)
    return pl.BlockSpec(shape, lambda i: zeros)


def params(limit):
    return pltpu.CompilerParams(
        dimension_semantics=("arbitrary",), vmem_limit_bytes=limit * 1024 * 1024
    )


def forward_layer(x, first, group, halves, gain_pair, bias_rows, tables):
    rows = x.shape[0]
    args = [x, *halves] + ([] if first else [gain_pair]) + [bias_rows, *tables]
    in_specs = [rows_spec(x.shape[1]), any_spec(), any_spec()]
    in_specs += [] if first else [whole_spec(gain_pair.shape)]
    in_specs += [whole_spec(bias_rows.shape)] + [rows_spec(LANES)] * 3
    outs = [(D, F32), (QKV, BF), (D, BF), (D, BF), (D, F32), (2 * FF, BF)]
    out_specs = [rows_spec(w) for w, _ in outs]
    out_shape = [jax.ShapeDtypeStruct((rows, w), t) for w, t in outs]
    scratch = weight_scratch(group, [(D, 2 * PMAX)] if first else [])
    if first:
        out_specs = [rows_spec(D), whole_spec((8, D))] + out_specs
        out_shape = [
            jax.ShapeDtypeStruct((rows, D), F32),
            jax.ShapeDtypeStruct((8, D), F32),
        ] + out_shape
        scratch.insert(-1, pltpu.VMEM((8, D), F32))
    flops = 2 * rows * (D * QKV + D * D + 3 * D * FF)
    got = pl.pallas_call(
        functools.partial(forward_body, first, group),
        grid=(rows // TILE,),
        in_specs=in_specs,
        out_specs=out_specs,
        out_shape=out_shape,
        scratch_shapes=scratch,
        compiler_params=params(48),
        cost_estimate=pl.CostEstimate(flops=flops, bytes_accessed=40 << 20, transcendentals=0),
    )(*args)
    if first:
        return got[2], [got[0]] + list(got[3:]), got[1]
    return got[0], [x] + list(got[1:]), None


def head_body(
    group,
    x_ref,
    target_ref,
    mask_ref,
    mine_ref,
    other_ref,
    gain_ref,
    dx_ref,
    dw_ref,
    dg_ref,
    loss_ref,
    acc_ref,
    whead_ref,
    sems,
):
    step = pl.program_id(0)
    me, core = place(group)
    made = copies(
        group, (mine_ref, other_ref), core, me, {"head": whead_ref}, sems, outward=False
    )

    @pl.when(step == 0)
    def _():
        acc_ref[...] = jnp.zeros_like(acc_ref)
        dg_ref[...] = jnp.zeros_like(dg_ref)
        loss_ref[...] = jnp.zeros_like(loss_ref)
        start_copies(group, made, core)
        wait_copies(made, ("head",))

    u, inverse = unit(x_ref[...])
    gain_row = gain_ref[0:1, :]
    final_in = (u * gain_row).astype(BF)
    predicted = dot_nn(final_in, whead_ref[...])
    target = target_ref[...]
    mask = mask_ref[...]
    loss = jnp.zeros((8, PMAX), F32)
    grads = []
    for q in range(NQ):
        level = (q + 1.0) / (NQ + 1)
        r = target - predicted[:, q * PMAX : (q + 1) * PMAX]
        a = r * (-1.0 / SMOOTH)
        e = jnp.exp(-jnp.abs(a))
        recip = 1.0 / (1.0 + e)
        sigmoid = jnp.where(a >= 0, recip, e * recip)
        softplus = jnp.maximum(a, 0.0) + jnp.log(1.0 + e)
        loss = loss + rows_to_eight((level * r + SMOOTH * softplus) * mask)
        grads.append(((sigmoid - level) * mask).astype(BF))
    loss_ref[...] += loss
    grad_pred = jnp.concatenate(grads, axis=1)
    acc_ref[...] += dot_tn(final_in, grad_pred)
    grad_x, grad_gain = rms_backward(u, inverse, gain_row, dot_nt(grad_pred, whead_ref[...]))
    dx_ref[...] = grad_x
    dg_ref[...] += grad_gain

    @pl.when(step == pl.num_programs(0) - 1)
    def _():
        dw_ref[...] = acc_ref[...].astype(BF)


def head(x, targets, mask, group, halves, gain):
    rows = x.shape[0]
    return pl.pallas_call(
        functools.partial(head_body, group),
        grid=(rows // TILE,),
        in_specs=[
            rows_spec(D),
            rows_spec(PMAX),
            rows_spec(PMAX),
            any_spec(),
            any_spec(),
            whole_spec(gain.shape),
        ],
        out_specs=[
            rows_spec(D),
            whole_spec((D, HEADW)),
            whole_spec((8, D)),
            whole_spec((8, PMAX)),
        ],
        out_shape=[
            jax.ShapeDtypeStruct((rows, D), F32),
            jax.ShapeDtypeStruct((D, HEADW), BF),
            jax.ShapeDtypeStruct((8, D), F32),
            jax.ShapeDtypeStruct((8, PMAX), F32),
        ],
        scratch_shapes=[
            pltpu.VMEM((D, HEADW), F32),
            pltpu.VMEM((D, HEADW), BF),
            pltpu.SemaphoreType.DMA((len(group.pieces), group.shards)),
        ],
        compiler_params=params(40),
        cost_estimate=pl.CostEstimate(
            flops=6 * rows * D * HEADW, bytes_accessed=8 << 20, transcendentals=0
        ),
    )(x, targets, mask, *halves, gain)


def backward_body(extra, group, *refs):
    refs = list(refs)
    extra_ref = refs.pop(0) if extra else None
    dout_ref, x_ref, qkv_ref, prob_ref, mixed_ref, mid_ref, gu_ref = refs[:7]
    mine_ref, other_ref, gain_ref, cos_ref, sin_ref, code_ref = refs[7:13]
    refs = refs[13:]
    dx_ref = None if extra == "in" else refs.pop(0)
    keep_ref, give_ref, dg_ref, db_ref = refs[:4]
    aqkv_ref, ao_ref, agu_ref, adown_ref, dgu_ref, dqkv_ref = refs[4:10]
    wqkv_ref, wo_ref, wgu_ref, wdown_ref, gqkv_ref, go_ref, ggu_ref, gdown_ref = refs[10:18]
    sems, out_sems = refs[18:20]
    if extra == "in":
        ain_ref, gin_ref = refs[20:]
    step = pl.program_id(0)
    me, core = place(group)
    made = copies(
        group,
        (mine_ref, other_ref),
        core,
        me,
        down_fields({"qkv": wqkv_ref, "o": wo_ref, "gu": wgu_ref, "d": wdown_ref}),
        sems,
        outward=False,
    )
    grads = {"qkv": gqkv_ref, "o": go_ref, "gu": ggu_ref, "d": gdown_ref}
    if extra == "in":
        grads["in"] = gin_ref
    if extra == "head":
        grads["head"] = extra_ref
    sent = copies(
        group, (keep_ref, give_ref), core, me, down_fields(grads), out_sems, outward=True
    )

    @pl.when(step == 0)
    def _():
        start_copies(group, made, core)
        aqkv_ref[...] = jnp.zeros_like(aqkv_ref)
        ao_ref[...] = jnp.zeros_like(ao_ref)
        agu_ref[...] = jnp.zeros_like(agu_ref)
        adown_ref[...] = jnp.zeros_like(adown_ref)
        dg_ref[...] = jnp.zeros_like(dg_ref)
        db_ref[...] = jnp.zeros_like(db_ref)
        if extra == "in":
            ain_ref[...] = jnp.zeros_like(ain_ref)
        wait_copies(made, ("qkv", "o", "d0", "d1", "gu", "d2"))

    dout = dout_ref[...]
    rows = dout.shape[0]
    dout_low = dout.astype(BF)
    gate = gu_ref[:, :FF].astype(F32)
    up = gu_ref[:, FF:].astype(F32)
    sig = sigmoid_of(gate)
    silu = gate * sig
    adown_ref[...] += dot_tn((silu * up).astype(BF), dout_low)
    grad_hidden = dot_nt(dout_low, wdown_ref[...])
    dgu_ref[:, :FF] = (grad_hidden * up * (sig + silu * (1.0 - sig))).astype(BF)
    dgu_ref[:, FF:] = (grad_hidden * silu).astype(BF)
    u_mid, inverse_mid = unit(mid_ref[...])
    gain_mid = gain_ref[1:2, :]
    agu_ref[...] += dot_tn((u_mid * gain_mid).astype(BF), dgu_ref[...])
    grad_mid, dgain_mid = rms_backward(
        u_mid, inverse_mid, gain_mid, dot_nt(dgu_ref[...], wgu_ref[...])
    )
    dg_ref[8:16, :] += dgain_mid
    grad_mid = grad_mid + dout
    grad_attn_low = grad_mid.astype(BF)
    ao_ref[...] += dot_tn(mixed_ref[...], grad_attn_low)
    grad_mixed = dot_nt(grad_attn_low, wo_ref[...]).astype(BF)
    spots = [(b, p) for p in range(PAIRS) for b in range(rows // BUCKET)]
    dprobs = []
    for b, p in spots:
        here = slice(b * BUCKET, (b + 1) * BUCKET)
        dm2 = two_blocks(grad_mixed[here, p * LANES : (p + 1) * LANES])
        v = qkv_ref[here, 2 * D + p * LANES : 2 * D + (p + 1) * LANES]
        dprobs.append(dot_nt(v, dm2))
    dscores = []
    for (b, p), dprob in zip(spots, dprobs):
        prob = prob_ref[b * BUCKET : (b + 1) * BUCKET, p * LANES : (p + 1) * LANES].astype(F32)
        ds = prob * (dprob - jnp.sum(prob * dprob, axis=0, keepdims=True))
        dscores.append(ds.astype(BF))
    for p in range(PAIRS):
        other_sum = jnp.zeros((8, LANES), F32)
        same_sum = jnp.zeros((8, LANES), F32)
        for b in range(rows // BUCKET):
            ds = dscores[p * (rows // BUCKET) + b].astype(F32)
            same = code_ref[b * BUCKET : (b + 1) * BUCKET, :] > 0.5
            same_sum = same_sum + rows_to_eight(jnp.where(same, ds, 0.0))
            other_sum = other_sum + rows_to_eight(jnp.where(same, 0.0, ds))
        db_ref[p * 8 : (p + 1) * 8, :] += other_sum
        db_ref[(PAIRS + p) * 8 : (PAIRS + p + 1) * 8, :] += same_sum
    for (b, p), ds in zip(spots, dscores):
        here = slice(b * BUCKET, (b + 1) * BUCKET)
        cols = slice(p * LANES, (p + 1) * LANES)
        kcols = slice(D + p * LANES, D + (p + 1) * LANES)
        vcols = slice(2 * D + p * LANES, 2 * D + (p + 1) * LANES)
        cos = cos_ref[here, :] * HD ** (-0.5)
        sin = sin_ref[here, :] * HD ** (-0.5)
        dm2 = two_blocks(grad_mixed[here, cols])
        dq = fold_blocks(dot_tn(ds, qkv_ref[here, kcols]))
        dk = dot_nn(ds, two_blocks(qkv_ref[here, cols]))
        dv = dot_nn(prob_ref[here, cols], dm2)
        dqkv_ref[here, cols] = (dq * cos + swap_halves(dq * sin)).astype(BF)
        dqkv_ref[here, kcols] = (dk * cos + swap_halves(dk * sin)).astype(BF)
        dqkv_ref[here, vcols] = dv.astype(BF)
    u, inverse = unit(x_ref[...])
    gain_row = gain_ref[0:1, :]
    aqkv_ref[...] += dot_tn((u * gain_row).astype(BF), dqkv_ref[...])
    grad_x, dgain = rms_backward(u, inverse, gain_row, dot_nt(dqkv_ref[...], wqkv_ref[...]))
    dg_ref[0:8, :] += dgain
    grad_x = grad_x + grad_mid
    if extra == "in":
        ain_ref[...] += dot_tn(grad_x.astype(BF), extra_ref[...])
    else:
        dx_ref[...] = grad_x

    @pl.when(step == pl.num_programs(0) - 1)
    def _():
        gqkv_ref[...] = aqkv_ref[...].astype(BF)
        go_ref[...] = ao_ref[...].astype(BF)
        ggu_ref[...] = agu_ref[...].astype(BF)
        gdown_ref[...] = adown_ref[...].astype(BF)
        if extra == "in":
            gin_ref[...] = ain_ref[...].astype(BF)
        start_copies(group, sent, core)
        wait_copies(sent, list(sent))


def backward_layer(extra, extra_array, dout, saved, group, halves, gain_pair, tables):
    rows = dout.shape[0]
    args = ([extra_array] if extra else []) + [dout, *saved, *halves, gain_pair, *tables]
    in_specs = []
    if extra:
        in_specs = [rows_spec(2 * PMAX) if extra == "in" else whole_spec((D, HEADW))]
    in_specs += (
        [rows_spec(D)]
        + [rows_spec(s.shape[1]) for s in saved]
        + [any_spec(), any_spec(), whole_spec(gain_pair.shape)]
        + [rows_spec(LANES)] * 3
    )
    slots = (group.shards, group.rows, group.half)
    out_specs = [any_spec(), any_spec(), whole_spec((16, D)), whole_spec((48, LANES))]
    out_shape = [
        jax.ShapeDtypeStruct(slots, BF),
        jax.ShapeDtypeStruct(slots, BF),
        jax.ShapeDtypeStruct((16, D), F32),
        jax.ShapeDtypeStruct((48, LANES), F32),
    ]
    if extra != "in":
        out_specs = [rows_spec(D)] + out_specs
        out_shape = [jax.ShapeDtypeStruct((rows, D), F32)] + out_shape
    shapes = list(WEIGHTS.values())
    semaphores = pltpu.SemaphoreType.DMA((len(group.pieces), group.shards))
    scratch = [pltpu.VMEM(s, F32) for s in shapes]
    scratch += [pltpu.VMEM((TILE, 2 * FF), BF), pltpu.VMEM((TILE, QKV), BF)]
    scratch += [pltpu.VMEM(s, BF) for s in shapes * 2] + [semaphores, semaphores]
    if extra == "in":
        scratch += [pltpu.VMEM((D, 2 * PMAX), F32), pltpu.VMEM((D, 2 * PMAX), BF)]
    flops = 4 * rows * (D * QKV + D * D + 3 * D * FF)
    got = pl.pallas_call(
        functools.partial(backward_body, extra, group),
        grid=(rows // TILE,),
        in_specs=in_specs,
        out_specs=out_specs,
        out_shape=out_shape,
        scratch_shapes=scratch,
        compiler_params=params(56),
        cost_estimate=pl.CostEstimate(flops=flops, bytes_accessed=80 << 20, transcendentals=0),
    )(*args)
    return ([None] if extra == "in" else []) + list(got)


def partners(sizes, fsdp_mask, dp_mask):
    fsdp, dp = sizes
    return [
        (f * dp + d, (f ^ fsdp_mask) * dp + (d ^ dp_mask)) for f in range(fsdp) for d in range(dp)
    ]


def slot_of(offset, masks):
    slot = 0
    for bit, mask in enumerate(masks):
        slot = slot + jnp.where((offset & mask) != 0, 1 << bit, 0)
    return slot


def swap(x, sizes, fsdp_mask, dp_mask):
    return lax.ppermute(x, AXES, partners(sizes, fsdp_mask, dp_mask))


def reorder(slots, masks):
    me = lax.axis_index("fsdp")
    return jnp.stack(
        [
            lax.dynamic_index_in_dim(slots, slot_of(me ^ j, masks), 0, keepdims=False)
            for j in range(slots.shape[0])
        ]
    )


class Gather:
    def __init__(self, halves, sizes):
        core = lax.axis_index("dp") & 1
        self.sizes = sizes
        self.mine = jnp.where(core == 0, halves[0], halves[1])[None]
        self.masks = masks_of(sizes[0])

    def step(self, mask):
        self.mine = jnp.concatenate([self.mine, swap(self.mine, self.sizes, mask, 0)], axis=0)

    def along(self):
        for mask in self.masks[:-1]:
            self.step(mask)

    def last(self):
        self.got = swap(self.mine, self.sizes, self.masks[-1], 0)

    def pair(self):
        self.mine = jnp.concatenate([self.mine, self.got], axis=0)
        return self.mine, swap(self.mine, self.sizes, 0, 1)


def by_core(mine, other):
    core = lax.axis_index("dp") & 1
    return jnp.where(core == 0, mine, other), jnp.where(core == 0, other, mine)


def add(a, b):
    return (a.astype(F32) + b.astype(F32)).astype(BF)


def to_slots(shards, masks):
    me = lax.axis_index("fsdp")
    slots = [None] * shards.shape[0]
    for v in range(shards.shape[0]):
        slots[slot_index(v, masks)] = lax.dynamic_index_in_dim(shards, me ^ v, 0, keepdims=False)
    return jnp.stack(slots)


class Scatter:
    def __init__(self, keep, give, sizes):
        self.sizes = sizes
        self.keep = keep
        self.got = swap(give, sizes, 0, 1)
        self.moves = [(mask, 0) for mask in reversed(masks_of(sizes[0]))]
        dp_mask = 2
        while dp_mask < sizes[1]:
            self.moves.append((0, dp_mask))
            dp_mask *= 2

    def ready(self):
        if self.moves and self.moves[0][0]:
            half = self.keep.shape[0] // 2
            self.away = add(self.keep[half:], self.got[half:])
            self.keep = add(self.keep[:half], self.got[:half])
        else:
            self.keep = add(self.keep, self.got)
            self.away = self.keep

    def move(self):
        self.got = swap(self.away, self.sizes, *self.moves.pop(0))

    def end(self):
        while self.moves:
            self.ready()
            self.move()
        total = add(self.keep, self.got)[0]
        return by_core(total, swap(total, self.sizes, 0, 1))


def hold(x, *scatters):
    for one in scatters:
        one.ready()
    held = lax.optimization_barrier((x, [(one.keep, one.away) for one in scatters]))
    for one, (keep, away) in zip(scatters, held[1]):
        one.keep, one.away = keep, away
        one.move()
    return held[0]


def pad_rows(x, rows):
    return jnp.pad(x, ((0, 0),) * (x.ndim - 2) + ((0, rows - x.shape[-2]), (0, 0)))


def to_whole(group, whole, mine, other, sizes):
    masks = masks_of(sizes[0])
    low, high = by_core(mine, other)
    parts = group.unpack((reorder(low, masks), reorder(high, masks)))
    parts = {n: p.reshape(1, p.shape[0] * p.shape[1], p.shape[2]) for n, p in parts.items()}
    return whole.pack(parts)


def from_whole(group, whole, low, high, sizes):
    parts = whole.unpack((low, high))
    fsdp = sizes[0]
    parts = {n: p.reshape(fsdp, p.shape[1] // fsdp, p.shape[2]) for n, p in parts.items()}
    low, high = group.pack(parts)
    masks = masks_of(fsdp)
    return by_core(to_slots(low, masks), to_slots(high, masks))


def rotary_tables(time_ids):
    frequency = THETA ** (-2.0 * jnp.arange(HD // 2, dtype=F32) / HD)
    phase = time_ids.astype(F32)[:, None] * frequency[None, :]
    cos, sin = jnp.cos(phase), jnp.sin(phase)
    return jnp.concatenate([cos] * 4, axis=1), jnp.concatenate([-sin, sin, -sin, sin], axis=1)


def token_tables(size_ids, variate_ids, lengths):
    rows = size_ids.shape[0]
    buckets = rows // BUCKET
    live = jnp.arange(BUCKET, dtype=jnp.int32)[None, :] < lengths[:, None]
    widths = jnp.where(live.reshape(rows), PMAX >> (4 - size_ids), 0)
    mask = (jnp.arange(PMAX, dtype=jnp.int32)[None, :] < widths[:, None]).astype(F32)
    variates = variate_ids.reshape(buckets, BUCKET)
    same = (variates[:, :, None] == variates[:, None, :]).astype(F32)
    code = jnp.where(live[:, :, None], same, -1.0).reshape(rows, BUCKET)
    return mask, jnp.concatenate([code, code], axis=1)


def patch_concat(patches, size_ids):
    pieces = []
    for size_id in range(5):
        span = PMAX >> 4 - size_id
        chosen = (size_ids == size_id)[:, None]
        pieces.append(jnp.where(chosen, patches[:, :span], jnp.zeros((), BF)))
    pieces.append(jnp.zeros((patches.shape[0], 2 * PMAX - IN_CAT), BF))
    return jnp.concatenate(pieces, axis=1)


def adam_update(master, clipped, first_old, second_old, matrix):
    first_new = BETA_ONE * first_old + (1.0 - BETA_ONE) * clipped
    second_new = BETA_TWO * second_old + (1.0 - BETA_TWO) * clipped * clipped
    first_hat = first_new / (1.0 - BETA_ONE**STEP_NUM)
    second_hat = second_new / (1.0 - BETA_TWO**STEP_NUM)
    direction = first_hat / (jnp.sqrt(second_hat) + ADAM_EPS)
    if matrix:
        master_new = master - RATE_MATRIX * (direction + WEIGHT_DECAY * master)
    else:
        master_new = master - RATE_GAIN * direction
    return (master_new, first_new, second_new)


def all_sum(x, sizes, dp_from=1):
    dp_mask = dp_from
    while dp_mask < sizes[1]:
        x = x + swap(x, sizes, 0, dp_mask)
        dp_mask *= 2
    for mask in masks_of(sizes[0]):
        x = x + swap(x, sizes, mask, 0)
    return x


def per_device(sizes, *args):
    patches, targets, size_ids, time_ids, variate_ids, lengths = args[:6]
    masters = args[6:14]
    firsts = args[14:22]
    seconds = args[22:30]
    w_in, w_qkv, w_o, w_gu, w_down, w_head, gains, var_bias = masters
    own = w_head.shape[0]
    down_rows = w_down.shape[1]
    direct = own % 16 == 0 and down_rows % 16 == 0
    extras = [[("in", 2 * PMAX)], [], [("head", HEADW)]]
    groups = [Group(extra, sizes[0], own, down_rows) for extra in extras]
    wholes = groups if direct else [Group(extra, 1, D, FF) for extra in extras]

    in_rows = jnp.concatenate(
        [w_in.T, gains.T, jnp.zeros((own, 2 * PMAX - IN_CAT - NGAIN), F32)], axis=1
    ).astype(BF)
    weights = []
    for layer in range(L):
        parts = {"qkv": w_qkv, "o": w_o, "gu": w_gu, "d": w_down}
        parts = {name: w[layer].astype(BF) for name, w in parts.items()}
        if layer == 0:
            parts["in"] = in_rows
        if layer == L - 1:
            parts["head"] = w_head.astype(BF)
        weights.append(Gather(groups[layer].pack(parts), sizes))

    def arrived(layer):
        pair = weights[layer].pair()
        return pair if direct else to_whole(groups[layer], wholes[layer], *pair, sizes)

    for layer in range(L):
        weights[layer].along()
    weights[0].last()

    cos, sin = rotary_tables(time_ids)
    mask, code = token_tables(size_ids, variate_ids, lengths)
    tables = (cos, sin, code)
    concat = patch_concat(patches, size_ids)
    count = jnp.sum(mask)
    bias_lanes = jnp.repeat(var_bias, HD, axis=2).reshape(L, 2, PAIRS, LANES)
    bias_lanes = jnp.pad(bias_lanes, ((0, 0), (0, 0), (0, 8 - PAIRS), (0, 0)))
    bias_lanes = bias_lanes.reshape(L, 16, LANES)

    stream = concat
    kept = []
    gain_pairs = []
    halves = []
    for layer in range(L):
        halves.append(arrived(layer))
        if layer + 1 < L:
            weights[layer + 1].last()
        stream, saved, found = forward_layer(
            stream,
            layer == 0,
            wholes[layer],
            halves[layer],
            None if layer == 0 else gain_pairs[layer],
            bias_lanes[layer],
            tables,
        )
        if layer == 0:
            gain_pairs = [found[0:2], found[2:4], found[4:6], found[6:8]]
        kept.append(saved)
        if layer + 1 < L:
            held = lax.optimization_barrier((stream, weights[layer + 1].got))
            stream, weights[layer + 1].got = held
    grad, head_grad, gain_grad, loss = head(
        stream, targets, mask, wholes[-1], halves[-1], gain_pairs[L]
    )
    gain_grads = {2 * L: jnp.sum(gain_grad, axis=0)}
    bias_grads = [None] * L
    totals = [None] * L
    for layer in reversed(range(L)):
        extra, extra_array = None, None
        if layer == 0:
            extra, extra_array = "in", concat
        elif layer == L - 1:
            extra, extra_array = "head", head_grad
        grad, keep, give, gain_grad, bias_grad = backward_layer(
            extra,
            extra_array,
            grad,
            kept[layer],
            wholes[layer],
            halves[layer],
            gain_pairs[layer],
            tables,
        )
        if not direct:
            keep, give = from_whole(groups[layer], wholes[layer], keep, give, sizes)
        flying = totals[layer + 1 :]
        give, landed = lax.optimization_barrier((give, [one.got for one in flying]))
        for one, got in zip(flying, landed):
            one.got = got
        totals[layer] = Scatter(keep, give, sizes)
        if layer:
            grad = hold(grad, *totals[layer:])
        gain_grads[2 * layer] = jnp.sum(gain_grad[:8], axis=0)
        gain_grads[2 * layer + 1] = jnp.sum(gain_grad[8:], axis=0)
        bias_grads[layer] = jnp.sum(bias_grad.reshape(2, PAIRS, 8, 2, HD), axis=(2, 4)).reshape(2, H)

    small = [jnp.sum(loss)[None], count[None], jnp.stack(bias_grads).reshape(-1)]
    small = jnp.concatenate(small)
    small = jnp.pad(small, (0, D - small.shape[0]))
    rows = [gain_grads[g] for g in range(NGAIN)] + [small]
    rows = all_sum(hold(jnp.stack(rows), totals[0]), sizes)
    loss_sum, total_count = rows[NGAIN, 0], rows[NGAIN, 1]
    inverse_count = 1.0 / total_count
    bias_grad = rows[NGAIN, 2 : 2 + var_bias.size].reshape(var_bias.shape) * inverse_count
    gain_all = rows[:NGAIN]
    gain_own = lax.dynamic_slice_in_dim(gain_all, lax.axis_index("fsdp") * own, own, axis=1)

    pieces = [groups[layer].unpack(totals[layer].end()) for layer in range(L)]
    in_piece = pieces[0]["in"][:, :IN_CAT]
    head_piece = pieces[-1]["head"]
    matrices = [[pieces[layer][m] for layer in range(L)] for m in ("qkv", "o", "gu", "d")]
    squares = 0.0
    for piece in [in_piece, head_piece] + sum(matrices, []):
        squares = squares + jnp.sum(jnp.square(piece.astype(F32)))
    squares = all_sum(squares.reshape(1, 1), sizes, dp_from=sizes[1])[0, 0]
    squares = squares + jnp.sum(jnp.square(gain_all))
    grad_norm = jnp.sqrt(
        squares * (inverse_count * inverse_count) + jnp.sum(bias_grad * bias_grad)
    )
    factor = jnp.minimum(1.0, CLIP_NORM / grad_norm)
    scale = factor * inverse_count

    gradients = [in_piece.T] + [jnp.stack(m) for m in matrices] + [head_piece, gain_own]
    clipped = [g.astype(F32) * scale for g in gradients] + [bias_grad * factor]
    fresh = [
        adam_update(masters[m], clipped[m], firsts[m], seconds[m], m < 6) for m in range(8)
    ]
    return (
        (loss_sum, total_count, grad_norm)
        + tuple(f[0] for f in fresh)
        + tuple(f[1] for f in fresh)
        + tuple(f[2] for f in fresh)
    )


def solution(mesh):
    sizes = (mesh.shape["fsdp"], mesh.shape["dp"])
    tokens = P(("fsdp", "dp"))
    tokens_two = P(("fsdp", "dp"), None)
    columns = P(None, "fsdp")
    stacked = P(None, "fsdp", None)
    states = (columns, stacked, stacked, stacked, stacked, P("fsdp", None), columns, P())
    in_specs = (tokens_two, tokens_two, tokens, tokens, tokens, tokens) + states * 3
    out_specs = (P(), P(), P()) + states * 3
    return jax.shard_map(
        functools.partial(per_device, sizes),
        mesh=mesh,
        in_specs=in_specs,
        out_specs=out_specs,
        check_vma=False,
    )
```

time: 764 us -> 435 us (0.57)
  waiting for transfers between devices: 301 us -> 162 us
  local copies, waits for them, and re-layouts: 128 us -> 19.9 us
  Pallas kernels: 193 us -> 132 us
  other arithmetic: 92.8 us -> 58.9 us
  starting transfers between devices: 29.8 us -> 41.6 us
  between operations: 8.48 us -> 16.4 us
    ppermute x18 -> x38, waiting for transfers between devices: 301 us -> 162 us  [swap(): return lax.ppermute(x, AXES, partners(sizes, fsdp_mask, dp_mask))]
    pallas_call x7, Pallas kernels: 193 us -> 132 us  [the longest x3 79.1 us: backward_layer(): pl.pallas_call(functools.partial(backward_body, extra, group), grid=(rows...]
    unnamed x234 -> x128, local copies, waits for them, and re-layouts: 51.9 us -> 11.9 us
    slice x24 -> x12, local copies, waits for them, and re-layouts: 22.3 us -> 1.24 us  [the longest x1 0.59 us: per_device(): loss_sum, total_count = (rows[NGAIN, 0], rows[NGAIN, 1])]
    another operation x24 -> x19, local copies, waits for them, and re-layouts: 21.9 us -> 1.73 us  [the longest x6 1.3 us: per_device(): jnp.stack(m)]
    ppermute x5 -> x0, local copies, waits for them, and re-layouts: 18 us -> none  [swap(): return lax.ppermute(x, AXES, partners(sizes, fsdp_mask, dp_mask))]
    convert_element_type x4 -> x12, other arithmetic: 23.6 us -> 11.1 us  [add(): return (a.astype(F32) + b.astype(F32)).astype(BF)]
    ppermute x18 -> x38, starting transfers between devices: 29.8 us -> 41.6 us  [swap(): return lax.ppermute(x, AXES, partners(sizes, fsdp_mask, dp_mask))]
  transfers between devices with their start and end apart: 18 -> 38, of which waited for: 14 -> 24; matrix products, arithmetic and copies ran while one was open for 6% -> 9% of each run, Pallas kernels for 0% -> 19%
where the time goes in v2:
time: 435 us; the launch traced here: 431 us
  waiting for transfers between devices  162 us (37%)
  Pallas kernels  132 us (30%)
  other arithmetic  58.9 us (14%)
  starting transfers between devices  41.6 us (10%)
  local copies, waits for them, and re-layouts  19.9 us (5%)
  between operations  16.4 us (4%)
    ppermute x38, waiting for transfers between devices, swap(): return lax.ppermute(x, AXES, partners(sizes, fsdp_mask, dp_mask))  162 us
    pallas_call x3, Pallas kernels, backward_layer(): pl.pallas_call(functools.partial(backward_body, extra, group), grid=(rows...  79.1 us
    pallas_call x3, Pallas kernels, forward_layer(): pl.pallas_call(functools.partial(forward_body, first, group), grid=(rows...  43.8 us
    ppermute x38, starting transfers between devices, swap(): return lax.ppermute(x, AXES, partners(sizes, fsdp_mask, dp_mask))  41.6 us
    unnamed x128, local copies, waits for them, and re-layouts  11.9 us
    sub x6, other arithmetic, adam_update(): master_new = master - RATE_MATRIX * (direction + WEIGHT_DECAY * master)  11.2 us
    convert_element_type x12, other arithmetic, add(): return (a.astype(F32) + b.astype(F32)).astype(BF)  11.1 us
    reduce_sum x14, other arithmetic, per_device(): squares = squares + jnp.sum(jnp.square(piece.astype(F32)))  9.14 us
  transfers between devices with their start and end apart: 38, of which 24 were waited for; matrix products, arithmetic and copies ran while one was open for 9% of the time, Pallas kernels for 19%

profile of v2, /device:TPU:0, one launch (start us, length us, event | category | flops | bytes accessed | tf_op | source)
XLA Modules:
  0.0 430.9 jit_solution(9224230867045794230)
XLA Ops:
  3.4 4.1 collective-permute-start.4
  8.3 20.4 %collective-permute-done = bf16[1,48,2560]{2,1,0:T(8,128)(2,1)S(1)} collective-permute-done((bf16[1,48,2560]{2,1,0:T(8,128)(2,1)S(1)}, bf16[1,48,2560]{2,1,0:T(8,128)(2,1)S(1)}, u32[]{:S(2)}, u32[]{:S(2)}) %collective-permute-start) | collective-permute-done | bytes 245792 | tf_op jit(solution)/shard_map/ppermute | solution.py:643
  29.6 11.6 %collective-permute-done.1 = bf16[2,48,2560]{2,1,0:T(8,128)(2,1)S(1)} collective-permute-done((bf16[2,48,2560]{2,1,0:T(8,128)(2,1)S(1)}, bf16[2,48,2560]{2,1,0:T(8,128)(2,1)S(1)}, u32[]{:S(2)}, u32[]{:S(2)}) %collective-permute-start.1) | collective-permute-done | bytes 491552 | tf_op jit(solution)/shard_map/ppermute | solution.py:643
  43.5 3.3 collective-permute-start.8
  48.9 14.6 %collective-permute-done.2 = bf16[4,48,2560]{2,1,0:T(8,128)(2,1)S(1)} collective-permute-done((bf16[4,48,2560]{2,1,0:T(8,128)(2,1)S(1)}, bf16[4,48,2560]{2,1,0:T(8,128)(2,1)S(1)}, u32[]{:S(2)}, u32[]{:S(2)}) %collective-permute-start.2) | collective-permute-done | bytes 983072 | tf_op jit(solution)/shard_map/ppermute | solution.py:643
  74.1 6.4 %collective-permute-done.5 = bf16[2,48,2432]{2,1,0:T(8,128)(2,1)S(1)} collective-permute-done((bf16[2,48,2432]{2,1,0:T(8,128)(2,1)}, bf16[2,48,2432]{2,1,0:T(8,128)(2,1)S(1)}, u32[]{:S(2)}, u32[]{:S(2)}) %collective-permute-start.5) | collective-permute-done | bytes 466976 | tf_op jit(solution)/shard_map/ppermute | solution.py:643
  85.3 15.5 %shard_map.493 = (f32[1024,384]{1,0:T(8,128)S(1)}, f32[8,384]{1,0:T(8,128)S(1)}, f32[1024,384]{1,0:T(8,128)}, bf16[1024,1152]{1,0:T(8,128)(2,1)}, bf16[1024,384]...) custom-call(bf16[1024,256]{1,0:T(8,128)(2,1)S(1)} %concatenate.160.refs_0_, ...), custom_call_target="tpu_custom_call" | custom-call | flops 3623878656 | bytes 41943040 | tf_op jit(solution)/shard_map/pallas_call | solution.py:345
  106.7 13.2 %collective-permute-done.9 = bf16[2,48,2944]{2,1,0:T(8,128)(2,1)S(1)} collective-permute-done((bf16[2,48,2944]{2,1,0:T(8,128)(2,1)S(1)}, bf16[2,48,2944]{2,1,0:T(8,128)(2,1)S(1)}, u32[]{:S(2)}, u32[]{:S(2)}) %collective-permute-start.9) | collective-permute-done | bytes 565280 | tf_op jit(solution)/shard_map/ppermute | solution.py:643
  124.6 14.0 %shard_map.494 = (f32[1024,384]{1,0:T(8,128)S(1)}, bf16[1024,1152]{1,0:T(8,128)(2,1)}, bf16[1024,384]{1,0:T(8,128)(2,1)S(1)}, bf16[1024,384]{1,0:T(8,128)(2,1)S(...) custom-call(f32[1024,384]{1,0:T(8,128)} %get-tuple-element.86.refs_0_.refs_1_, bf16[8,48,2432]{2,1,0:T(8,128)(2,1)} %copy-done.32, ...), custom_call_target="tpu_custom_call" | custom-call | flops 3623878656 | bytes 41943040 | tf_op jit(solution)/shard_map/pallas_call | solution.py:345
  138.7 8.6 %collective-permute-done.10 = bf16[4,48,2944]{2,1,0:T(8,128)(2,1)S(1)} collective-permute-done((bf16[4,48,2944]{2,1,0:T(8,128)(2,1)S(1)}, bf16[4,48,2944]{2,1,0:T(8,128)(2,1)S(1)}, u32[]{:S(2)}, u32[]{:S(2)}) %collective-permute-start.10) | collective-permute-done | bytes 1130528 | tf_op jit(solution)/shard_map/ppermute | solution.py:643
  149.0 4.2 collective-permute-done.11.refs_2_.other_ref.refs_9_
  154.5 14.3 %shard_map.495 = (f32[1024,384]{1,0:T(8,128)S(1)}, bf16[1024,1152]{1,0:T(8,128)(2,1)}, bf16[1024,384]{1,0:T(8,128)(2,1)S(1)}, bf16[1024,384]{1,0:T(8,128)(2,1)S(...) custom-call(f32[1024,384]{1,0:T(8,128)} %copy-done.13, bf16[8,48,2944]{2,1,0:T(8,128)(2,1)} %copy-done, ...), custom_call_target="tpu_custom_call" | custom-call | flops 3623878656 | bytes 41943040 | tf_op jit(solution)/shard_map/pallas_call | solution.py:345
  173.3 9.1 %shard_map.496 = (f32[1024,384]{1,0:T(8,128)S(1)}, bf16[384,1152]{1,0:T(8,128)(2,1)S(1)}, f32[8,384]{1,0:T(8,128)S(1)}, f32[8,128]{1,0:T(8,128)S(1)}) custom-call(f32[1024,384]{1,0:T(8,128)S(1)} %get-tuple-element.92.x_ref, f32[1024,128]{1,0:T(8,128)S(1)} %copy-done.10, f32[1024,128]{1,0:T(8,128)S(1)} %fusion.3.mask_ref, bf16[8,48,2944]{2,1,0:T(8,128)(2,1)S(1)} %copy-done.1, ...), custom_call_target="tpu_custom_call" | custom-call | flops 2717908992 | bytes 8388608 | tf_op jit(solution)/shard_map/pallas_call | solution.py:422
  184.4 26.3 %shard_map.497 = (f32[1024,384]{1,0:T(8,128)}, bf16[8,48,2944]{2,1,0:T(8,128)(2,1)}, bf16[8,48,2944]{2,1,0:T(8,128)(2,1)}, f32[16,384]{1,0:T(8,128)}, f32[48,128]{1,0:T(8,128)}) custom-call(bf16[384,1152]{1,0:T(8,128)(2,1)} %copy-done.12, f32[1024,384]{1,0:T(8,128)} %copy-done.11, f32[1024,384]{1,0:T(8,128)} %copy-done.13, ...), custom_call_target="tpu_custom_call" | custom-call | flops 7247757312 | bytes 83886080 | tf_op jit(solution)/shard_map/pallas_call | solution.py:615
  211.0 4.4 %collective-permute-done.12 = bf16[8,48,2944]{2,1,0:T(8,128)(2,1)S(1)} collective-permute-done((bf16[8,48,2944]{2,1,0:T(8,128)(2,1)}, bf16[8,48,2944]{2,1,0:T(8,128)(2,1)S(1)}, u32[]{:S(2)}, u32[]{:S(2)}) %collective-permute-start.12) | collective-permute-done | bytes 2261024 | tf_op jit(solution)/shard_map/ppermute | solution.py:643
  219.1 25.9 %shard_map.498 = (f32[1024,384]{1,0:T(8,128)}, bf16[8,48,2432]{2,1,0:T(8,128)(2,1)}, bf16[8,48,2432]{2,1,0:T(8,128)(2,1)}, f32[16,384]{1,0:T(8,128)}, f32[48,128]{1,0:T(8,128)}) custom-call(f32[1024,384]{1,0:T(8,128)} %get-tuple-element.103.refs_0_, f32[1024,384]{1,0:T(8,128)} %get-tuple-element.86.refs_0_.refs_1_, ...), custom_call_target="tpu_custom_call" | custom-call | flops 7247757312 | bytes 83886080 | tf_op jit(solution)/shard_map/pallas_call | solution.py:615
  256.9 26.9 %shard_map.499 = (bf16[8,48,2560]{2,1,0:T(8,128)(2,1)}, bf16[8,48,2560]{2,1,0:T(8,128)(2,1)}, f32[16,384]{1,0:T(8,128)}, f32[48,128]{1,0:T(8,128)}) custom-call(bf16[1024,256]{1,0:T(8,128)(2,1)} %copy-done.5, f32[1024,384]{1,0:T(8,128)} %get-tuple-element.116.refs_1_, f32[1024,384]{1,0:T(8,128)} %copy-done.14, ...), custom_call_target="tpu_custom_call" | custom-call | flops 7247757312 | bytes 83886080 | tf_op jit(solution)/shard_map/pallas_call | solution.py:615
  288.1 3.4 collective-permute-start.28
  293.6 11.0 %collective-permute-done.28 = bf16[1,48,2944]{2,1,0:T(8,128)(2,1)S(1)} collective-permute-done((bf16[1,48,2944]{2,1,0:T(8,128)(2,1)S(1)}, bf16[1,48,2944]{2,1,0:T(8,128)(2,1)S(1)}, u32[]{:S(2)}, u32[]{:S(2)}) %collective-permute-start.28) | collective-permute-done | bytes 282656 | tf_op jit(solution)/shard_map/ppermute | solution.py:643
  307.3 4.0 collective-permute-done.31
  314.5 8.2 %collective-permute-done.32 = bf16[1,48,2432]{2,1,0:T(8,128)(2,1)S(1)} collective-permute-done((bf16[1,48,2432]{2,1,0:T(8,128)(2,1)S(1)}, bf16[1,48,2432]{2,1,0:T(8,128)(2,1)S(1)}, u32[]{:S(2)}, u32[]{:S(2)}) %collective-permute-start.32) | collective-permute-done | bytes 233504 | tf_op jit(solution)/shard_map/ppermute | solution.py:643
  332.2 19.6 %collective-permute-done.23 = bf16[4,48,2560]{2,1,0:T(8,128)(2,1)S(1)} collective-permute-done((bf16[4,48,2560]{2,1,0:T(8,128)(2,1)S(1)}, bf16[4,48,2560]{2,1,0:T(8,128)(2,1)S(1)}, u32[]{:S(2)}, u32[]{:S(2)}) %collective-permute-start.23) | collective-permute-done | bytes 983072 | tf_op jit(solution)/shard_map/ppermute | solution.py:643
  352.2 11.8 %collective-permute-done.24 = bf16[2,48,2560]{2,1,0:T(8,128)(2,1)S(1)} collective-permute-done((bf16[2,48,2560]{2,1,0:T(8,128)(2,1)S(1)}, bf16[2,48,2560]{2,1,0:T(8,128)(2,1)S(1)}, u32[]{:S(2)}, u32[]{:S(2)}) %collective-permute-start.24) | collective-permute-done | bytes 491552 | tf_op jit(solution)/shard_map/ppermute | solution.py:643
  372.0 4.6 %collective-permute-done.20 = f32[8,384]{1,0:T(8,128)S(1)} collective-permute-done((f32[8,384]{1,0:T(8,128)S(1)}, f32[8,384]{1,0:T(8,128)S(1)}, u32[]{:S(2)}, u32[]{:S(2)}) %collective-permute-start.20) | collective-permute-done | bytes 12320 | tf_op jit(solution)/shard_map/ppermute | solution.py:643
  (342 shorter events, 129.0 us)
Async XLA Ops:
  3.4 62.4 %collective-permute-start.4 = (bf16[1,48,2432]{2,1,0:T(8,128)(2,1)S(1)}, bf16[1,48,2432]{2,1,0:T(8,128)(2,1)S(1)}, u32[]{:S(2)}, u32[]{:S(2)}) collective-permute-start(bf16[1,48,2432]{2,1,0:T(8,128)(2,1)S(1)} %maximum_select_fusion.2), channel_id=1, source_target_pairs={{0,16},{1,17},{2,18},{3,19},{4,20},{5,21},{6,22},{7,23},{8,24},{9,... | collective-permute-start | bytes 700424 | tf_op jit(solution)/shard_map/ppermute | solution.py:643
  7.9 20.8 %collective-permute-start = (bf16[1,48,2560]{2,1,0:T(8,128)(2,1)S(1)}, bf16[1,48,2560]{2,1,0:T(8,128)(2,1)S(1)}, u32[]{:S(2)}, u32[]{:S(2)}) collective-permute-start(bf16[1,48,2560]{2,1,0:T(8,128)(2,1)S(1)} %maximum_select_fusion.1), channel_id=1, source_target_pairs={{0,16},{1,17},{2,18},{3,19},{4,20},{5,21},{6,22},{7,23},{8,24},{9,... | collective-permute-start | bytes 737288 | tf_op jit(solution)/shard_map/ppermute | solution.py:643
  28.8 12.5 %collective-permute-start.1 = (bf16[2,48,2560]{2,1,0:T(8,128)(2,1)S(1)}, bf16[2,48,2560]{2,1,0:T(8,128)(2,1)S(1)}, u32[]{:S(2)}, u32[]{:S(2)}) collective-permute-start(bf16[2,48,2560]{2,1,0:T(8,128)(2,1)S(1)} %pad_maximum_fusion.11), channel_id=1, source_target_pairs={{0,8},{1,9},{2,10},{3,11},{4,12},{5,13},{6,14},{7,15},{8,0},{9,1},... | collective-permute-start | bytes 1474568 | tf_op jit(solution)/shard_map/ppermute | solution.py:643
  41.3 22.1 %collective-permute-start.2 = (bf16[4,48,2560]{2,1,0:T(8,128)(2,1)S(1)}, bf16[4,48,2560]{2,1,0:T(8,128)(2,1)S(1)}, u32[]{:S(2)}, u32[]{:S(2)}) collective-permute-start(bf16[4,48,2560]{2,1,0:T(8,128)(2,1)S(1)} %pad_maximum_fusion.4), channel_id=1, source_target_pairs={{0,4},{1,5},{2,6},{3,7},{4,0},{5,1},{6,2},{7,3},{8,12},{9,13},{10,... | collective-permute-start | bytes 2949128 | tf_op jit(solution)/shard_map/ppermute | solution.py:643
  43.5 60.1 %collective-permute-start.8 = (bf16[1,48,2944]{2,1,0:T(8,128)(2,1)}, bf16[1,48,2944]{2,1,0:T(8,128)(2,1)}, u32[]{:S(2)}, u32[]{:S(2)}) collective-permute-start(bf16[1,48,2944]{2,1,0:T(8,128)(2,1)} %maximum_select_fusion), channel_id=1, source_target_pairs={{0,16},{1,17},{2,18},{3,19},{4,20},{5,21},{6,22},{7,23},{8,24},{9,... | collective-permute-start | bytes 847880 | tf_op jit(solution)/shard_map/ppermute | solution.py:643
  64.9 20.4 %collective-permute-start.3 = (bf16[8,48,2560]{2,1,0:T(8,128)(2,1)}, bf16[8,48,2560]{2,1,0:T(8,128)(2,1)}, u32[]{:S(2)}, u32[]{:S(2)}) collective-permute-start(bf16[8,48,2560]{2,1,0:T(8,128)(2,1)} %pad_maximum_fusion.1.refs_1_.refs_8_), channel_id=1, source_target_pairs={{0,1},{1,0},{2,3},{3,2},{4,5},{5,4},{6,7},{7,6},{8,9},{9,8},{10,11... | collective-permute-start | bytes 5898248 | tf_op jit(solution)/shard_map/ppermute | solution.py:643
  66.7 13.8 %collective-permute-start.5 = (bf16[2,48,2432]{2,1,0:T(8,128)(2,1)}, bf16[2,48,2432]{2,1,0:T(8,128)(2,1)S(1)}, u32[]{:S(2)}, u32[]{:S(2)}) collective-permute-start(bf16[2,48,2432]{2,1,0:T(8,128)(2,1)} %pad_maximum_fusion.12), channel_id=1, source_target_pairs={{0,8},{1,9},{2,10},{3,11},{4,12},{5,13},{6,14},{7,15},{8,0},{9,1},... | collective-permute-start | bytes 1400840 | tf_op jit(solution)/shard_map/ppermute | solution.py:643
  80.6 22.6 %collective-permute-start.6 = (bf16[4,48,2432]{2,1,0:T(8,128)(2,1)S(1)}, bf16[4,48,2432]{2,1,0:T(8,128)(2,1)S(1)}, u32[]{:S(2)}, u32[]{:S(2)}) collective-permute-start(bf16[4,48,2432]{2,1,0:T(8,128)(2,1)S(1)} %pad_maximum_fusion.5), channel_id=1, source_target_pairs={{0,4},{1,5},{2,6},{3,7},{4,0},{5,1},{6,2},{7,3},{8,12},{9,13},{10,... | collective-permute-start | bytes 2801672 | tf_op jit(solution)/shard_map/ppermute | solution.py:643
  103.5 19.8 %collective-permute-start.7 = (bf16[8,48,2432]{2,1,0:T(8,128)(2,1)S(1)}, bf16[8,48,2432]{2,1,0:T(8,128)(2,1)S(1)}, u32[]{:S(2)}, u32[]{:S(2)}) collective-permute-start(bf16[8,48,2432]{2,1,0:T(8,128)(2,1)S(1)} %pad_maximum_fusion.2.refs_1_.refs_7_), channel_id=1, source_target_pairs={{0,1},{1,0},{2,3},{3,2},{4,5},{5,4},{6,7},{7,6},{8,9},{9,8},{10,11... | collective-permute-start | bytes 5603336 | tf_op jit(solution)/shard_map/ppermute | solution.py:643
  105.1 14.8 %collective-permute-start.9 = (bf16[2,48,2944]{2,1,0:T(8,128)(2,1)S(1)}, bf16[2,48,2944]{2,1,0:T(8,128)(2,1)S(1)}, u32[]{:S(2)}, u32[]{:S(2)}) collective-permute-start(bf16[2,48,2944]{2,1,0:T(8,128)(2,1)S(1)} %pad_maximum_fusion.7), channel_id=1, source_target_pairs={{0,8},{1,9},{2,10},{3,11},{4,12},{5,13},{6,14},{7,15},{8,0},{9,1},... | collective-permute-start | bytes 1695752 | tf_op jit(solution)/shard_map/ppermute | solution.py:643
  121.2 26.1 %collective-permute-start.10 = (bf16[4,48,2944]{2,1,0:T(8,128)(2,1)S(1)}, bf16[4,48,2944]{2,1,0:T(8,128)(2,1)S(1)}, u32[]{:S(2)}, u32[]{:S(2)}) collective-permute-start(bf16[4,48,2944]{2,1,0:T(8,128)(2,1)S(1)} %pad_maximum_fusion.3), channel_id=1, source_target_pairs={{0,4},{1,5},{2,6},{3,7},{4,0},{5,1},{6,2},{7,3},{8,12},{9,13},{10,... | collective-permute-start | bytes 3391496 | tf_op jit(solution)/shard_map/ppermute | solution.py:643
  217.5 27.5 %collective-permute-start.13 = (bf16[4,48,2944]{2,1,0:T(8,128)(2,1)S(1)}, bf16[4,48,2944]{2,1,0:T(8,128)(2,1)S(1)}, u32[]{:S(2)}, u32[]{:S(2)}) collective-permute-start(bf16[4,48,2944]{2,1,0:T(8,128)(2,1)S(1)} %get-tuple-element.112), channel_id=1, source_target_pairs={{0,4},{1,5},{2,6},{3,7},{4,0},{5,1},{6,2},{7,3},{8,12},{9,13},{10,... | collective-permute-start | bytes 3391496 | tf_op jit(solution)/shard_map/ppermute | solution.py:643
  254.3 32.7 %collective-permute-start.16 = (bf16[2,48,2944]{2,1,0:T(8,128)(2,1)S(1)}, bf16[2,48,2944]{2,1,0:T(8,128)(2,1)}, u32[]{:S(2)}, u32[]{:S(2)}) collective-permute-start(bf16[2,48,2944]{2,1,0:T(8,128)(2,1)S(1)} %get-tuple-element.134), channel_id=1, source_target_pairs={{0,8},{1,9},{2,10},{3,11},{4,12},{5,13},{6,14},{7,15},{8,0},{9,1},... | collective-permute-start | bytes 1695752 | tf_op jit(solution)/shard_map/ppermute | solution.py:643
  255.9 31.2 %collective-permute-start.15 = (bf16[4,48,2432]{2,1,0:T(8,128)(2,1)}, bf16[4,48,2432]{2,1,0:T(8,128)(2,1)}, u32[]{:S(2)}, u32[]{:S(2)}) collective-permute-start(bf16[4,48,2432]{2,1,0:T(8,128)(2,1)} %get-tuple-element.133), channel_id=1, source_target_pairs={{0,4},{1,5},{2,6},{3,7},{4,0},{5,1},{6,2},{7,3},{8,12},{9,13},{10,... | collective-permute-start | bytes 2801672 | tf_op jit(solution)/shard_map/ppermute | solution.py:643
  288.1 16.5 %collective-permute-start.28 = (bf16[1,48,2944]{2,1,0:T(8,128)(2,1)S(1)}, bf16[1,48,2944]{2,1,0:T(8,128)(2,1)S(1)}, u32[]{:S(2)}, u32[]{:S(2)}) collective-permute-start(bf16[1,48,2944]{2,1,0:T(8,128)(2,1)S(1)} %add_convert_fusion.14), channel_id=1, source_target_pairs={{0,16},{1,17},{2,18},{3,19},{4,20},{5,21},{6,22},{7,23},{8,24},{9,... | collective-permute-start | bytes 847880 | tf_op jit(solution)/shard_map/ppermute | solution.py:643
  293.0 18.3 %collective-permute-start.31 = (bf16[2,48,2432]{2,1,0:T(8,128)(2,1)S(1)}, bf16[2,48,2432]{2,1,0:T(8,128)(2,1)S(1)}, u32[]{:S(2)}, u32[]{:S(2)}) collective-permute-start(bf16[2,48,2432]{2,1,0:T(8,128)(2,1)S(1)} %get-tuple-element.184), channel_id=1, source_target_pairs={{0,8},{1,9},{2,10},{3,11},{4,12},{5,13},{6,14},{7,15},{8,0},{9,1},... | collective-permute-start | bytes 1400840 | tf_op jit(solution)/shard_map/ppermute | solution.py:643
  293.6 34.1 %collective-permute-start.17 = (bf16[8,48,2560]{2,1,0:T(8,128)(2,1)S(1)}, bf16[8,48,2560]{2,1,0:T(8,128)(2,1)S(1)}, u32[]{:S(2)}, u32[]{:S(2)}) collective-permute-start(bf16[8,48,2560]{2,1,0:T(8,128)(2,1)S(1)} %copy-done.60), channel_id=1, source_target_pairs={{0,1},{1,0},{2,3},{3,2},{4,5},{5,4},{6,7},{7,6},{8,9},{9,8},{10,11... | collective-permute-start | bytes 5898248 | tf_op jit(solution)/shard_map/ppermute | solution.py:643
  305.7 8.6 %collective-permute-start.29 = (bf16[1,48,2944]{2,1,0:T(8,128)(2,1)S(1)}, bf16[1,48,2944]{2,1,0:T(8,128)(2,1)S(1)}, u32[]{:S(2)}, u32[]{:S(2)}) collective-permute-start(bf16[1,48,2944]{2,1,0:T(8,128)(2,1)S(1)} %add_convert_fusion.13), channel_id=1, source_target_pairs={{0,2},{1,3},{2,0},{3,1},{4,6},{5,7},{6,4},{7,5},{8,10},{9,11},{10,... | collective-permute-start | bytes 847880 | tf_op jit(solution)/shard_map/ppermute | solution.py:643
  311.3 11.4 %collective-permute-start.32 = (bf16[1,48,2432]{2,1,0:T(8,128)(2,1)S(1)}, bf16[1,48,2432]{2,1,0:T(8,128)(2,1)S(1)}, u32[]{:S(2)}, u32[]{:S(2)}) collective-permute-start(bf16[1,48,2432]{2,1,0:T(8,128)(2,1)S(1)} %add_convert_fusion.22), channel_id=1, source_target_pairs={{0,16},{1,17},{2,18},{3,19},{4,20},{5,21},{6,22},{7,23},{8,24},{9,... | collective-permute-start | bytes 700424 | tf_op jit(solution)/shard_map/ppermute | solution.py:643
  314.4 9.9 %collective-permute-start.30 = (bf16[48,2944]{1,0:T(8,128)(2,1)S(1)}, bf16[48,2944]{1,0:T(8,128)(2,1)S(1)}, u32[]{:S(2)}, u32[]{:S(2)}) collective-permute-start(bf16[48,2944]{1,0:T(8,128)(2,1)S(1)} %fusion.4), channel_id=1, source_target_pairs={{0,1},{1,0},{2,3},{3,2},{4,5},{5,4},{6,7},{7,6},{8,9},{9,8},{10,11... | collective-permute-start | bytes 847880 | tf_op jit(solution)/shard_map/ppermute | solution.py:643
  328.3 23.5 %collective-permute-start.23 = (bf16[4,48,2560]{2,1,0:T(8,128)(2,1)S(1)}, bf16[4,48,2560]{2,1,0:T(8,128)(2,1)S(1)}, u32[]{:S(2)}, u32[]{:S(2)}) collective-permute-start(bf16[4,48,2560]{2,1,0:T(8,128)(2,1)S(1)} %get-tuple-element.138), channel_id=1, source_target_pairs={{0,4},{1,5},{2,6},{3,7},{4,0},{5,1},{6,2},{7,3},{8,12},{9,13},{10,... | collective-permute-start | bytes 2949128 | tf_op jit(solution)/shard_map/ppermute | solution.py:643
  352.0 12.0 %collective-permute-start.24 = (bf16[2,48,2560]{2,1,0:T(8,128)(2,1)S(1)}, bf16[2,48,2560]{2,1,0:T(8,128)(2,1)S(1)}, u32[]{:S(2)}, u32[]{:S(2)}) collective-permute-start(bf16[2,48,2560]{2,1,0:T(8,128)(2,1)S(1)} %get-tuple-element.182), channel_id=1, source_target_pairs={{0,8},{1,9},{2,10},{3,11},{4,12},{5,13},{6,14},{7,15},{8,0},{9,1},... | collective-permute-start | bytes 1474568 | tf_op jit(solution)/shard_map/ppermute | solution.py:643
  352.1 12.7 %collective-permute-start.18 = (f32[8,384]{1,0:T(8,128)S(1)}, f32[8,384]{1,0:T(8,128)S(1)}, u32[]{:S(2)}, u32[]{:S(2)}) collective-permute-start(f32[8,384]{1,0:T(8,128)S(1)} %stack.87), channel_id=1, source_target_pairs={{0,1},{1,0},{2,3},{3,2},{4,5},{5,4},{6,7},{7,6},{8,9},{9,8},{10,11... | collective-permute-start | bytes 36872 | tf_op jit(solution)/shard_map/ppermute | solution.py:643
  364.1 12.6 %collective-permute-start.25 = (bf16[1,48,2560]{2,1,0:T(8,128)(2,1)S(1)}, bf16[1,48,2560]{2,1,0:T(8,128)(2,1)S(1)}, u32[]{:S(2)}, u32[]{:S(2)}) collective-permute-start(bf16[1,48,2560]{2,1,0:T(8,128)(2,1)S(1)} %add_convert_fusion.18), channel_id=1, source_target_pairs={{0,16},{1,17},{2,18},{3,19},{4,20},{5,21},{6,22},{7,23},{8,24},{9,... | collective-permute-start | bytes 737288 | tf_op jit(solution)/shard_map/ppermute | solution.py:643
  (76 other events, 1024.3 us)

commit v3 on v2

v3 whole, which is shorter than its diff:
```python
import functools

import jax
import jax.numpy as jnp
from jax import lax
from jax.experimental import pallas as pl
from jax.experimental.pallas import tpu as pltpu
from jax.sharding import PartitionSpec as P

D = 384
H = 6
HD = 64
FF = 1024
PMAX = 128
NQ = 9
BUCKET = 64
L = 3
STEP_NUM = 10
IN_CAT = 248
NGAIN = 7
QKV = 3 * D
HEADW = NQ * PMAX
PAIRS = H // 2
LANES = 2 * HD

TILE = 256

EPS_NORM = 1e-05
SMOOTH = 0.5
THETA = 10000.0
MASKED_SCORE = -1e30
CLIP_NORM = 0.001
BETA_ONE = 0.9
BETA_TWO = 0.95
ADAM_EPS = 1e-08
WEIGHT_DECAY = 0.1
RATE_MATRIX = 0.15
RATE_GAIN = 0.8

BF = jnp.bfloat16
F32 = jnp.float32
AXES = ("fsdp", "dp")


def dot_nn(a, b):
    return lax.dot_general(a, b, (((1,), (0,)), ((), ())), preferred_element_type=F32)


def dot_nt(a, b):
    return lax.dot_general(a, b, (((1,), (1,)), ((), ())), preferred_element_type=F32)


def dot_tn(a, b):
    return lax.dot_general(a, b, (((0,), (0,)), ((), ())), preferred_element_type=F32)


def unit(x):
    inverse = lax.rsqrt(jnp.mean(x * x, axis=-1, keepdims=True) + EPS_NORM)
    return x * inverse, inverse


def rms_backward(u, inverse, gain_row, grad):
    grad_unit = grad * gain_row
    grad_x = inverse * (grad_unit - u * jnp.mean(grad_unit * u, axis=-1, keepdims=True))
    return grad_x, rows_to_eight(grad * u)


def rows_to_eight(x):
    return jnp.sum(x.reshape(x.shape[0] // 8, 8, x.shape[1]), axis=0)


def lane_of(shape):
    return lax.broadcasted_iota(jnp.int32, shape, len(shape) - 1)


def swap_halves(x):
    lane = lane_of(x.shape)
    return jnp.where((lane & 32) == 0, pltpu.roll(x, 96, 1), pltpu.roll(x, 32, 1))


def low_lanes(shape):
    return lane_of(shape) < HD


def two_blocks(x):
    keep = low_lanes(x.shape)
    zero = jnp.zeros_like(x)
    return jnp.concatenate([jnp.where(keep, x, zero), jnp.where(keep, zero, x)], axis=0)


def fold_blocks(x):
    return jnp.where(low_lanes((BUCKET, LANES)), x[:BUCKET], x[BUCKET:])


def sigmoid_of(x):
    return 0.5 * jnp.tanh(0.5 * x) + 0.5


class Group:
    def __init__(self, fields, parts, shards, rows, down_rows):
        self.parts, self.shards, self.rows, self.down_rows = parts, shards, rows, down_rows
        used = sum(width for _, width in fields)
        self.width = -(-used // (parts * LANES)) * LANES
        self.pad = parts * self.width - used
        self.fields = fields
        self.pieces = []
        at = 0
        for name, width in fields:
            done = 0
            while done < width:
                part = (at + done) // self.width
                take = min(width - done, (part + 1) * self.width - at - done)
                self.pieces.append((part, at + done - part * self.width, name, done, take))
                done += take
            at += width
        masks = masks_of(shards)
        self.slots = [slot_index(v, masks) if parts > 1 else v for v in range(shards)]

    def row_span(self, name):
        if name[0] == "d":
            first = int(name[1]) * self.rows
            return first, min(self.rows, self.down_rows - first), self.down_rows
        return 0, self.rows, self.rows

    def pack(self, fields):
        fields = dict(fields)
        if "d" in fields:
            down = fields.pop("d")
            for i in range(3):
                part = down[..., i * self.rows : (i + 1) * self.rows, :]
                fields[f"d{i}"] = pad_rows(part, self.rows)
        parts = [[] for _ in range(self.parts)]
        for part, _, name, start, width in self.pieces:
            parts[part].append(fields[name][..., start : start + width])
        if self.pad:
            like = parts[-1][0]
            parts[-1].append(jnp.zeros(like.shape[:-1] + (self.pad,), like.dtype))
        return tuple(jnp.concatenate(p, axis=-1) for p in parts)

    def unpack(self, parts):
        found = {}
        for part, at, name, _, width in self.pieces:
            got = parts[part][..., at : at + width]
            found[name] = jnp.concatenate([found[name], got], axis=-1) if name in found else got
        if "d0" in found:
            downs = [found.pop(f"d{i}") for i in range(3)]
            downs[2] = downs[2][..., : self.row_span("d2")[1], :]
            found["d"] = jnp.concatenate(downs, axis=-2)
        return found


    def squares(self, own):
        row = lax.broadcasted_iota(jnp.int32, own.shape, 0)
        col = lax.broadcasted_iota(jnp.int32, own.shape, 1)
        used = [jnp.zeros(own.shape, bool)] * 2
        for part, at, name, _, width in self.pieces:
            inside = (col >= at) & (col < at + width) & (row < self.row_span(name)[1])
            used[part] = used[part] | inside
        core = lax.axis_index("dp") & 1
        used = (used[0] & (core == 0)) | (used[1] & (core == 1))
        return jnp.sum(jnp.where(used, jnp.square(own.astype(F32)), 0.0)).reshape(1, 1)


def place(group):
    if group.shards == 1:
        return 0, 0
    return lax.axis_index("fsdp"), lax.axis_index("dp") & 1


def copies(group, arrays, me, targets, sems, outward):
    made = {}
    for n, (part, at, name, start, width) in enumerate(group.pieces):
        if name not in targets:
            continue
        first, count, stride = group.row_span(name)
        for v in range(group.shards):
            owner = v if group.parts == 1 else me ^ v
            row = owner * stride + first
            if not isinstance(row, int):
                row = pl.multiple_of(row, 16)
            whole = targets[name].at[pl.ds(row, count), pl.ds(start, width)]
            slots = [
                a.at[group.slots[v], pl.ds(0, count), pl.ds(at, width)] for a in arrays
            ]
            ends = [(whole, slot) if outward else (slot, whole) for slot in slots]
            pair = [functools.partial(pltpu.make_async_copy, a, b, sems.at[n, v]) for a, b in ends]
            made.setdefault(name, []).append((part, pair))
    return made


def start_copies(group, made, core):
    def go(which):
        for items in made.values():
            for part, pair in items:
                pair[part ^ which]().start()

    if group.shards == 1 or group.parts == 1:
        go(0)
    else:
        pl.when(core == 0)(functools.partial(go, 0))
        pl.when(core == 1)(functools.partial(go, 1))


def wait_copies(made, names):
    for name in names:
        for _, pair in made.get(name, []):
            pair[0]().wait()


def slot_index(v, masks):
    return sum((1 << bit) for bit, mask in enumerate(masks) if v & mask)


def masks_of(size):
    masks = []
    size //= 2
    while size:
        masks.append(size)
        size //= 2
    return masks


def any_spec():
    return pl.BlockSpec(memory_space=pl.ANY)


WEIGHTS = {"in": (D, 2 * PMAX), "qkv": (D, QKV), "o": (D, D), "gu": (D, 2 * FF), "d": (FF, D)}


def semaphores(group):
    return pltpu.SemaphoreType.DMA((len(group.pieces), group.shards))


class Taker:
    def __init__(self, refs):
        self.refs = list(refs)

    def __call__(self, count=1):
        taken, self.refs = self.refs[:count], self.refs[count:]
        return taken[0] if count == 1 else taken

    def named(self, names):
        return dict(zip(names, [self() for _ in names]))


def down_fields(targets):
    targets = dict(targets)
    if "d" in targets:
        down = targets.pop("d")
        targets.update(d0=down, d1=down, d2=down)
    return targets


ATTN, FFN = ("qkv", "o"), ("gu", "d")


def forward_body(names, group, *refs):
    first, attn, ffn = "in" in names, "qkv" in names, "gu" in names
    take = Taker(refs)
    x_ref = take()
    arrays = take.refs[: group.parts]
    take(group.parts)
    gain_ref = None if first else take()
    if attn:
        bias_ref, cos_ref, sin_ref, code_ref = take(4)
    if first:
        base_ref, rows_ref = take(2)
    if attn:
        qkv_ref, prob_ref, mixed_ref, mid_ref = take(4)
    if ffn:
        out_ref, gu_ref = take(2)
    w = take.named(names)
    sems = take()
    if first:
        gain_ref = take()
    me, core = place(group)
    made = copies(group, arrays, me, down_fields(w), sems, outward=False)
    opening = pl.program_id(0) == 0
    early = [n for n in made if n in ("in", "qkv")]
    late = [n for n in made if n not in early]

    @pl.when(opening)
    def _():
        start_copies(group, made, core)
        wait_copies(made, early)
        if first:
            turned = w["in"][:, PMAX:].astype(F32).T
            gain_ref[...] = turned[IN_CAT - PMAX : IN_CAT - PMAX + 8, :]
            rows_ref[...] = gain_ref[...]

    def rest():
        pl.when(opening)(functools.partial(wait_copies, made, late))

    if attn:
        if first:
            stream = dot_nt(x_ref[...], w["in"][...])
            base_ref[...] = stream
        else:
            stream = x_ref[...]
        rows = stream.shape[0]
        normed = (unit(stream)[0] * gain_ref[0:1, :]).astype(BF)
        cos = cos_ref[...]
        sin = sin_ref[...]
        qk = dot_nn(normed, w["qkv"][:, : 2 * D])
        for j in range(2 * PAIRS):
            cols = slice(j * LANES, (j + 1) * LANES)
            qkv_ref[:, cols] = (qk[:, cols] * cos + swap_halves(qk[:, cols]) * sin).astype(BF)
        qkv_ref[:, 2 * D :] = dot_nn(normed, w["qkv"][:, 2 * D :]).astype(BF)
        spots = [(b, p) for b in range(rows // BUCKET) for p in range(PAIRS)]
        scores = []
        for b, p in spots:
            here = slice(b * BUCKET, (b + 1) * BUCKET)
            q = qkv_ref[here, p * LANES : (p + 1) * LANES]
            k = qkv_ref[here, D + p * LANES : D + (p + 1) * LANES]
            scores.append(dot_nt(k, two_blocks(q)))
        probs = []
        for (b, p), score in zip(spots, scores):
            code = code_ref[b * BUCKET : (b + 1) * BUCKET, :]
            bias = jnp.where(code > 0.5, bias_ref[p + 8 : p + 9, :], bias_ref[p : p + 1, :])
            score = jnp.where(code < -0.5, MASKED_SCORE, score * HD ** (-0.5) + bias)
            e = jnp.exp(score - jnp.max(score, axis=0, keepdims=True))
            probs.append((e * (1.0 / jnp.sum(e, axis=0, keepdims=True))).astype(BF))
        for (b, p), prob in zip(spots, probs):
            here = slice(b * BUCKET, (b + 1) * BUCKET)
            cols = slice(p * LANES, (p + 1) * LANES)
            v = qkv_ref[here, 2 * D + p * LANES : 2 * D + (p + 1) * LANES]
            prob_ref[here, cols] = prob
            mixed_ref[here, cols] = fold_blocks(dot_tn(prob, v)).astype(BF)
        rest()
        middle = stream + dot_nn(mixed_ref[...], w["o"][...])
        mid_ref[...] = middle
    else:
        rest()
        middle = x_ref[...]
    if ffn:
        ffn_in = (unit(middle)[0] * gain_ref[1:2, :]).astype(BF)
        gate_up = dot_nn(ffn_in, w["gu"][...])
        gu_ref[...] = gate_up.astype(BF)
        gate = gate_up[:, :FF]
        hidden = (gate * sigmoid_of(gate) * gate_up[:, FF:]).astype(BF)
        out_ref[...] = middle + dot_nn(hidden, w["d"][...])


def rows_spec(width):
    return pl.BlockSpec((TILE, width), lambda i: (i, 0))


def whole_spec(shape):
    zeros = (0,) * len(shape)
    return pl.BlockSpec(shape, lambda i: zeros)


def params(limit):
    return pltpu.CompilerParams(
        dimension_semantics=("arbitrary",), vmem_limit_bytes=limit * 1024 * 1024
    )


def forward_layer(x, names, group, arrays, gain_pair, bias_rows, tables):
    first, attn, ffn = "in" in names, "qkv" in names, "gu" in names
    rows = x.shape[0]
    args = [x, *arrays]
    in_specs = [rows_spec(x.shape[1])] + [any_spec()] * group.parts
    if not first:
        args.append(gain_pair)
        in_specs.append(whole_spec(gain_pair.shape))
    if attn:
        args += [bias_rows, *tables]
        in_specs += [whole_spec(bias_rows.shape)] + [rows_spec(LANES)] * 3
    outs = [(D, F32)] if first else []
    outs += [(QKV, BF), (D, BF), (D, BF), (D, F32)] if attn else []
    outs += [(D, F32), (2 * FF, BF)] if ffn else []
    out_specs = [rows_spec(w) for w, _ in outs]
    out_shape = [jax.ShapeDtypeStruct((rows, w), t) for w, t in outs]
    scratch = [pltpu.VMEM(WEIGHTS[n], BF) for n in names] + [semaphores(group)]
    if first:
        out_specs.insert(1, whole_spec((8, D)))
        out_shape.insert(1, jax.ShapeDtypeStruct((8, D), F32))
        scratch.append(pltpu.VMEM((8, D), F32))
    size = sum(WEIGHTS[n][0] * WEIGHTS[n][1] for n in names)
    return pl.pallas_call(
        functools.partial(forward_body, names, group),
        grid=(rows // TILE,),
        in_specs=in_specs,
        out_specs=out_specs,
        out_shape=out_shape,
        scratch_shapes=scratch,
        compiler_params=params(48),
        cost_estimate=pl.CostEstimate(
            flops=2 * rows * size, bytes_accessed=24 * size, transcendentals=0
        ),
    )(*args)


def head_body(
    group,
    x_ref,
    target_ref,
    mask_ref,
    *refs,
):
    take = Taker(refs)
    arrays = take.refs[: group.parts]
    take(group.parts)
    gain_ref, dx_ref, dw_ref, dg_ref, loss_ref, acc_ref, whead_ref, sems = take(8)
    step = pl.program_id(0)
    me, core = place(group)
    made = copies(group, arrays, me, {"head": whead_ref}, sems, outward=False)

    @pl.when(step == 0)
    def _():
        acc_ref[...] = jnp.zeros_like(acc_ref)
        dg_ref[...] = jnp.zeros_like(dg_ref)
        loss_ref[...] = jnp.zeros_like(loss_ref)
        start_copies(group, made, core)
        wait_copies(made, ("head",))

    u, inverse = unit(x_ref[...])
    gain_row = gain_ref[0:1, :]
    final_in = (u * gain_row).astype(BF)
    predicted = dot_nn(final_in, whead_ref[...])
    target = target_ref[...]
    mask = mask_ref[...]
    loss = jnp.zeros((8, PMAX), F32)
    grads = []
    for q in range(NQ):
        level = (q + 1.0) / (NQ + 1)
        r = target - predicted[:, q * PMAX : (q + 1) * PMAX]
        a = r * (-1.0 / SMOOTH)
        e = jnp.exp(-jnp.abs(a))
        recip = 1.0 / (1.0 + e)
        sigmoid = jnp.where(a >= 0, recip, e * recip)
        softplus = jnp.maximum(a, 0.0) + jnp.log(1.0 + e)
        loss = loss + rows_to_eight((level * r + SMOOTH * softplus) * mask)
        grads.append(((sigmoid - level) * mask).astype(BF))
    loss_ref[...] += loss
    grad_pred = jnp.concatenate(grads, axis=1)
    acc_ref[...] += dot_tn(final_in, grad_pred)
    grad_x, grad_gain = rms_backward(u, inverse, gain_row, dot_nt(grad_pred, whead_ref[...]))
    dx_ref[...] = grad_x
    dg_ref[...] += grad_gain

    @pl.when(step == pl.num_programs(0) - 1)
    def _():
        dw_ref[...] = acc_ref[...].astype(BF)


def head(x, targets, mask, group, arrays, gain):
    rows = x.shape[0]
    return pl.pallas_call(
        functools.partial(head_body, group),
        grid=(rows // TILE,),
        in_specs=[
            rows_spec(D),
            rows_spec(PMAX),
            rows_spec(PMAX),
        ]
        + [any_spec()] * group.parts
        + [whole_spec(gain.shape)],
        out_specs=[
            rows_spec(D),
            whole_spec((D, HEADW)),
            whole_spec((8, D)),
            whole_spec((8, PMAX)),
        ],
        out_shape=[
            jax.ShapeDtypeStruct((rows, D), F32),
            jax.ShapeDtypeStruct((D, HEADW), BF),
            jax.ShapeDtypeStruct((8, D), F32),
            jax.ShapeDtypeStruct((8, PMAX), F32),
        ],
        scratch_shapes=[
            pltpu.VMEM((D, HEADW), F32),
            pltpu.VMEM((D, HEADW), BF),
            semaphores(group),
        ],
        compiler_params=params(40),
        cost_estimate=pl.CostEstimate(
            flops=6 * rows * D * HEADW, bytes_accessed=8 << 20, transcendentals=0
        ),
    )(x, targets, mask, *arrays, gain)


def backward_body(names, extra, group, out_group, *refs):
    first, attn, ffn = "in" in names, "qkv" in names, "gu" in names
    take = Taker(refs)
    dout_ref = take()
    if attn:
        x_ref, qkv_ref, prob_ref, mixed_ref = take(4)
    if ffn:
        mid_ref, gu_ref = take(2)
    concat_ref = take() if first else None
    extras = {extra: take()} if extra else {}
    arrays = take.refs[: group.parts]
    take(group.parts)
    gain_ref = take()
    if attn:
        cos_ref, sin_ref, code_ref = take(3)
    dx_ref = None if first else take()
    out_arrays = take.refs[: out_group.parts]
    take(out_group.parts)
    if attn:
        dg_attn, db_ref = take(2)
    if ffn:
        dg_ffn = take()
    loads = [n for n in names if n != "in"]
    w = take.named(loads)
    acc = take.named(names)
    grads = take.named(names)
    sems, out_sems = take(2)
    if attn:
        dqkv_ref = take()
    if ffn:
        dgu_ref = take()
    step = pl.program_id(0)
    me, core = place(group)
    made = copies(group, arrays, me, down_fields(w), sems, outward=False)
    sent = copies(
        out_group, out_arrays, me, {**down_fields(grads), **extras}, out_sems, outward=True
    )

    @pl.when(step == 0)
    def _():
        start_copies(group, made, core)
        for ref in acc.values():
            ref[...] = jnp.zeros_like(ref)
        if attn:
            dg_attn[...] = jnp.zeros_like(dg_attn)
            db_ref[...] = jnp.zeros_like(db_ref)
        if ffn:
            dg_ffn[...] = jnp.zeros_like(dg_ffn)
        wait_copies(made, list(made))

    dout = dout_ref[...]
    rows = dout.shape[0]
    grad_mid = dout
    if ffn:
        dout_low = dout.astype(BF)
        gate = gu_ref[:, :FF].astype(F32)
        up = gu_ref[:, FF:].astype(F32)
        sig = sigmoid_of(gate)
        silu = gate * sig
        acc["d"][...] += dot_tn((silu * up).astype(BF), dout_low)
        grad_hidden = dot_nt(dout_low, w["d"][...])
        dgu_ref[:, :FF] = (grad_hidden * up * (sig + silu * (1.0 - sig))).astype(BF)
        dgu_ref[:, FF:] = (grad_hidden * silu).astype(BF)
        u_mid, inverse_mid = unit(mid_ref[...])
        gain_mid = gain_ref[1:2, :]
        acc["gu"][...] += dot_tn((u_mid * gain_mid).astype(BF), dgu_ref[...])
        grad_mid, dgain_mid = rms_backward(
            u_mid, inverse_mid, gain_mid, dot_nt(dgu_ref[...], w["gu"][...])
        )
        dg_ffn[...] += dgain_mid
        grad_mid = grad_mid + dout
    grad_x = grad_mid
    if attn:
        grad_attn_low = grad_mid.astype(BF)
        acc["o"][...] += dot_tn(mixed_ref[...], grad_attn_low)
        grad_mixed = dot_nt(grad_attn_low, w["o"][...]).astype(BF)
        spots = [(b, p) for p in range(PAIRS) for b in range(rows // BUCKET)]
        dprobs = []
        for b, p in spots:
            here = slice(b * BUCKET, (b + 1) * BUCKET)
            dm2 = two_blocks(grad_mixed[here, p * LANES : (p + 1) * LANES])
            v = qkv_ref[here, 2 * D + p * LANES : 2 * D + (p + 1) * LANES]
            dprobs.append(dot_nt(v, dm2))
        dscores = []
        for (b, p), dprob in zip(spots, dprobs):
            prob = prob_ref[b * BUCKET : (b + 1) * BUCKET, p * LANES : (p + 1) * LANES].astype(F32)
            ds = prob * (dprob - jnp.sum(prob * dprob, axis=0, keepdims=True))
            dscores.append(ds.astype(BF))
        for p in range(PAIRS):
            other_sum = jnp.zeros((8, LANES), F32)
            same_sum = jnp.zeros((8, LANES), F32)
            for b in range(rows // BUCKET):
                ds = dscores[p * (rows // BUCKET) + b].astype(F32)
                same = code_ref[b * BUCKET : (b + 1) * BUCKET, :] > 0.5
                same_sum = same_sum + rows_to_eight(jnp.where(same, ds, 0.0))
                other_sum = other_sum + rows_to_eight(jnp.where(same, 0.0, ds))
            db_ref[p * 8 : (p + 1) * 8, :] += other_sum
            db_ref[(PAIRS + p) * 8 : (PAIRS + p + 1) * 8, :] += same_sum
        for (b, p), ds in zip(spots, dscores):
            here = slice(b * BUCKET, (b + 1) * BUCKET)
            cols = slice(p * LANES, (p + 1) * LANES)
            kcols = slice(D + p * LANES, D + (p + 1) * LANES)
            vcols = slice(2 * D + p * LANES, 2 * D + (p + 1) * LANES)
            cos = cos_ref[here, :] * HD ** (-0.5)
            sin = sin_ref[here, :] * HD ** (-0.5)
            dm2 = two_blocks(grad_mixed[here, cols])
            dq = fold_blocks(dot_tn(ds, qkv_ref[here, kcols]))
            dk = dot_nn(ds, two_blocks(qkv_ref[here, cols]))
            dv = dot_nn(prob_ref[here, cols], dm2)
            dqkv_ref[here, cols] = (dq * cos + swap_halves(dq * sin)).astype(BF)
            dqkv_ref[here, kcols] = (dk * cos + swap_halves(dk * sin)).astype(BF)
            dqkv_ref[here, vcols] = dv.astype(BF)
        u, inverse = unit(x_ref[...])
        gain_row = gain_ref[0:1, :]
        acc["qkv"][...] += dot_tn((u * gain_row).astype(BF), dqkv_ref[...])
        grad_x, dgain = rms_backward(u, inverse, gain_row, dot_nt(dqkv_ref[...], w["qkv"][...]))
        dg_attn[...] += dgain
        grad_x = grad_x + grad_mid
    if first:
        acc["in"][...] += dot_tn(grad_x.astype(BF), concat_ref[...])
    else:
        dx_ref[...] = grad_x

    @pl.when(step == pl.num_programs(0) - 1)
    def _():
        for name in names:
            grads[name][...] = acc[name][...].astype(BF)
        start_copies(out_group, sent, core)
        wait_copies(sent, list(sent))


def backward_layer(names, dout, saved, concat, extra, group, arrays, out_group, gain_pair, tables):
    first, attn, ffn = "in" in names, "qkv" in names, "gu" in names
    rows = dout.shape[0]
    args = [dout, *saved] + ([concat] if first else [])
    in_specs = [rows_spec(a.shape[1]) for a in args]
    if extra:
        args.append(extra[1])
        in_specs.append(whole_spec(extra[1].shape))
    args += [*arrays, gain_pair]
    in_specs += [any_spec()] * group.parts + [whole_spec(gain_pair.shape)]
    if attn:
        args += list(tables)
        in_specs += [rows_spec(LANES)] * 3
    out_specs, out_shape = [], []
    if not first:
        out_specs.append(rows_spec(D))
        out_shape.append(jax.ShapeDtypeStruct((rows, D), F32))
    slots = (out_group.shards, out_group.rows, out_group.width)
    out_specs += [any_spec()] * out_group.parts
    out_shape += [jax.ShapeDtypeStruct(slots, BF)] * out_group.parts
    small = ([(8, D), (48, LANES)] if attn else []) + ([(8, D)] if ffn else [])
    out_specs += [whole_spec(shape) for shape in small]
    out_shape += [jax.ShapeDtypeStruct(shape, F32) for shape in small]
    scratch = [pltpu.VMEM(WEIGHTS[n], BF) for n in names if n != "in"]
    scratch += [pltpu.VMEM(WEIGHTS[n], F32) for n in names]
    scratch += [pltpu.VMEM(WEIGHTS[n], BF) for n in names]
    scratch += [semaphores(group), semaphores(out_group)]
    scratch += [pltpu.VMEM((TILE, QKV), BF)] if attn else []
    scratch += [pltpu.VMEM((TILE, 2 * FF), BF)] if ffn else []
    size = sum(WEIGHTS[n][0] * WEIGHTS[n][1] for n in names)
    got = pl.pallas_call(
        functools.partial(backward_body, names, extra[0] if extra else None, group, out_group),
        grid=(rows // TILE,),
        in_specs=in_specs,
        out_specs=out_specs,
        out_shape=out_shape,
        scratch_shapes=scratch,
        compiler_params=params(56),
        cost_estimate=pl.CostEstimate(
            flops=4 * rows * size, bytes_accessed=48 * size, transcendentals=0
        ),
    )(*args)
    got = list(got)
    grad = None if first else got.pop(0)
    return grad, got[: out_group.parts], got[out_group.parts :]


def partners(sizes, fsdp_mask, dp_mask):
    fsdp, dp = sizes
    return [
        (f * dp + d, (f ^ fsdp_mask) * dp + (d ^ dp_mask)) for f in range(fsdp) for d in range(dp)
    ]


def slot_of(offset, masks):
    slot = 0
    for bit, mask in enumerate(masks):
        slot = slot + jnp.where((offset & mask) != 0, 1 << bit, 0)
    return slot


def swap(x, sizes, fsdp_mask, dp_mask):
    return lax.ppermute(x, AXES, partners(sizes, fsdp_mask, dp_mask))


def reorder(slots, masks):
    me = lax.axis_index("fsdp")
    return jnp.stack(
        [
            lax.dynamic_index_in_dim(slots, slot_of(me ^ j, masks), 0, keepdims=False)
            for j in range(slots.shape[0])
        ]
    )


class Gather:
    def __init__(self, halves, sizes):
        core = lax.axis_index("dp") & 1
        self.sizes = sizes
        self.mine = jnp.where(core == 0, halves[0], halves[1])[None]
        self.masks = masks_of(sizes[0])
        self.got = None

    def move(self, after=None):
        mine = self.land()
        if after is not None:
            mine, after.got = lax.optimization_barrier((mine, after.got))
        self.mine = mine
        self.got = swap(mine, self.sizes, self.masks.pop(0), 0)

    def land(self):
        if self.got is not None:
            self.mine = jnp.concatenate([self.mine, self.got], axis=0)
            self.got = None
        return self.mine

    def hold(self, x):
        x, self.got = lax.optimization_barrier((x, self.got))
        return x

    def pair(self):
        mine = self.land()
        return mine, swap(mine, self.sizes, 0, 1)


def by_core(mine, other):
    core = lax.axis_index("dp") & 1
    return jnp.where(core == 0, mine, other), jnp.where(core == 0, other, mine)


def add(a, b):
    return (a.astype(F32) + b.astype(F32)).astype(BF)


def to_slots(shards, masks):
    me = lax.axis_index("fsdp")
    slots = [None] * shards.shape[0]
    for v in range(shards.shape[0]):
        slots[slot_index(v, masks)] = lax.dynamic_index_in_dim(shards, me ^ v, 0, keepdims=False)
    return jnp.stack(slots)


class Scatter:
    def __init__(self, keep, give, sizes):
        self.sizes = sizes
        self.keep = keep
        self.got = swap(give, sizes, 0, 1)
        self.moves = [(mask, 0) for mask in reversed(masks_of(sizes[0]))]
        dp_mask = 2
        while dp_mask < sizes[1]:
            self.moves.append((0, dp_mask))
            dp_mask *= 2

    def ready(self):
        if self.moves and self.moves[0][0]:
            half = self.keep.shape[0] // 2
            self.away = add(self.keep[half:], self.got[half:])
            self.keep = add(self.keep[:half], self.got[:half])
        else:
            self.keep = add(self.keep, self.got)
            self.away = self.keep

    def move(self):
        self.got = swap(self.away, self.sizes, *self.moves.pop(0))

    def total(self):
        return add(self.keep, self.got)[0]


def hold(x, *scatters):
    for one in scatters:
        one.ready()
    held = lax.optimization_barrier((x, [(one.keep, one.away) for one in scatters]))
    for one, (keep, away) in zip(scatters, held[1]):
        one.keep, one.away = keep, away
        one.move()
    return held[0]


def after_landing(x, scatters):
    x, landed = lax.optimization_barrier((x, [one.got for one in scatters]))
    for one, got in zip(scatters, landed):
        one.got = got
    return x


def pad_rows(x, rows):
    return jnp.pad(x, ((0, 0),) * (x.ndim - 2) + ((0, rows - x.shape[-2]), (0, 0)))


def to_whole(group, whole, arrays, sizes):
    if group.parts == 2:
        masks = masks_of(sizes[0])
        arrays = [reorder(a, masks) for a in by_core(*arrays)]
    fields = group.unpack(arrays)
    fields = {n: p.reshape(1, p.shape[0] * p.shape[1], p.shape[2]) for n, p in fields.items()}
    return whole.pack(fields)


def from_whole(group, whole, arrays, sizes):
    fsdp = sizes[0]
    fields = whole.unpack(arrays)
    fields = {n: p.reshape(fsdp, p.shape[1] // fsdp, p.shape[2]) for n, p in fields.items()}
    arrays = group.pack(fields)
    if group.parts == 1:
        return arrays
    masks = masks_of(fsdp)
    return by_core(*[to_slots(a, masks) for a in arrays])


def rotary_tables(time_ids):
    frequency = THETA ** (-2.0 * jnp.arange(HD // 2, dtype=F32) / HD)
    phase = time_ids.astype(F32)[:, None] * frequency[None, :]
    cos, sin = jnp.cos(phase), jnp.sin(phase)
    return jnp.concatenate([cos] * 4, axis=1), jnp.concatenate([-sin, sin, -sin, sin], axis=1)


def live_slots(lengths):
    return jnp.arange(BUCKET, dtype=jnp.int32)[None, :] < lengths[:, None]


def target_mask(size_ids, lengths):
    widths = jnp.where(live_slots(lengths).reshape(size_ids.shape), PMAX >> (4 - size_ids), 0)
    return (jnp.arange(PMAX, dtype=jnp.int32)[None, :] < widths[:, None]).astype(F32)


def code_table(variate_ids, lengths):
    variates = variate_ids.reshape(-1, BUCKET)
    same = (variates[:, :, None] == variates[:, None, :]).astype(F32)
    code = jnp.where(live_slots(lengths)[:, :, None], same, -1.0).reshape(-1, BUCKET)
    return jnp.concatenate([code, code], axis=1)


def patch_concat(patches, size_ids):
    pieces = []
    for size_id in range(5):
        span = PMAX >> 4 - size_id
        chosen = (size_ids == size_id)[:, None]
        pieces.append(jnp.where(chosen, patches[:, :span], jnp.zeros((), BF)))
    pieces.append(jnp.zeros((patches.shape[0], 2 * PMAX - IN_CAT), BF))
    return jnp.concatenate(pieces, axis=1)


def adam_update(master, clipped, first_old, second_old, matrix):
    first_new = BETA_ONE * first_old + (1.0 - BETA_ONE) * clipped
    second_new = BETA_TWO * second_old + (1.0 - BETA_TWO) * clipped * clipped
    first_hat = first_new / (1.0 - BETA_ONE**STEP_NUM)
    second_hat = second_new / (1.0 - BETA_TWO**STEP_NUM)
    direction = first_hat / (jnp.sqrt(second_hat) + ADAM_EPS)
    if matrix:
        master_new = master - RATE_MATRIX * (direction + WEIGHT_DECAY * master)
    else:
        master_new = master - RATE_GAIN * direction
    return (master_new, first_new, second_new)


def sum_moves(sizes, dp_from=1):
    moves = []
    dp_mask = dp_from
    while dp_mask < sizes[1]:
        moves.append((0, dp_mask))
        dp_mask *= 2
    return moves + [(mask, 0) for mask in masks_of(sizes[0])]


def per_device(sizes, *args):
    patches, targets, size_ids, time_ids, variate_ids, lengths = args[:6]
    masters = args[6:14]
    firsts = args[14:22]
    seconds = args[22:30]
    w_in, w_qkv, w_o, w_gu, w_down, w_head, gains, var_bias = masters
    own = w_head.shape[0]
    down_rows = w_down.shape[1]
    direct = own % 16 == 0 and down_rows % 16 == 0
    attn_fields = [("qkv", QKV), ("o", D)]
    ffn_fields = [("d0", D), ("d1", D), ("gu", 2 * FF), ("d2", D)]
    plan = [
        (("in",) + ATTN, [("in", 2 * PMAX)] + attn_fields),
        (FFN, ffn_fields),
        (ATTN + FFN, attn_fields + ffn_fields),
        (ATTN + FFN, attn_fields + ffn_fields + [("head", HEADW)]),
    ]
    layers = [0, 0, 1, 2]
    count = len(plan)
    def groups_of(fields, parts):
        many = [Group(f, p, sizes[0], own, down_rows) for f, p in zip(fields, parts)]
        if direct:
            return many, many
        return many, [Group(f, p, 1, D, FF) for f, p in zip(fields, parts)]

    fields = [f for _, f in plan]
    groups, wholes = groups_of(fields, [2] * count)

    in_rows = jnp.concatenate(
        [w_in.T, gains.T, jnp.zeros((own, 2 * PMAX - IN_CAT - NGAIN), F32)], axis=1
    ).astype(BF)
    def packed(n, stacks, head_w=None):
        fields = {m: w[layers[n]].astype(BF) for m, w in zip(("qkv", "o", "gu", "d"), stacks)}
        if n == count - 1:
            fields["head"] = head_w.astype(BF)
        return groups[n].pack({**fields, "in": in_rows})

    stacks = (w_qkv, w_o, w_gu, w_down)
    gathers = [Gather(packed(0, stacks), sizes)]
    steps = len(gathers[0].masks)
    gathers[0].move()
    stacks, head_w, time_ids = gathers[0].hold((stacks, w_head, time_ids))
    gathers += [Gather(packed(n, stacks, head_w), sizes) for n in range(1, count)]
    cos, sin = rotary_tables(time_ids)
    for _ in range(steps - 2):
        gathers[0].move()
    early = (patches, size_ids, variate_ids, lengths)
    early, gathers[1].mine = gathers[0].hold((early, gathers[1].mine))
    patches, size_ids, variate_ids, lengths = early
    gathers[0].move()
    for _ in range(steps - 2):
        gathers[1].move()
    gathers[2].move(gathers[1])
    gathers[1].move()
    gathers[3].move(gathers[2])
    for _ in range(steps - 2):
        gathers[2].move()
    gathers[1].move()
    for _ in range(steps - 3):
        gathers[3].move()

    def arrived(n):
        arrays = gathers[n].pair()
        return arrays if direct else to_whole(groups[n], wholes[n], arrays, sizes)

    tables = (cos, sin, code_table(variate_ids, lengths))
    concat = patch_concat(patches, size_ids)
    bias_lanes = jnp.repeat(var_bias, HD, axis=2).reshape(L, 2, PAIRS, LANES)
    bias_lanes = jnp.pad(bias_lanes, ((0, 0), (0, 0), (0, 8 - PAIRS), (0, 0)))
    bias_lanes = bias_lanes.reshape(L, 16, LANES)

    stream = concat
    kept = [None] * count
    loaded = []
    gain_pairs = [None] * (L + 1)
    for n, layer in enumerate(layers):
        names = plan[n][0]
        loaded.append(arrived(n))
        for one in gathers[n + 1 :]:
            if n and one.masks:
                one.move()
        got = list(
            forward_layer(
                stream, names, wholes[n], loaded[n], gain_pairs[layer], bias_lanes[layer], tables
            )
        )
        if n == 0:
            stream, found = got[:2]
            got = got[2:]
            gain_pairs = [found[0:2], found[2:4], found[4:6], found[6:8]]
            kept[0] = [stream, *got[:3]]
            stream = got[3]
        elif n == 1:
            kept[1] = [stream, got[1]]
            stream = got[0]
        else:
            kept[n] = [stream, *got[:4], got[5]]
            stream = got[4]
        for one in gathers[n + 1 :]:
            stream = one.hold(stream)
        if n == 0:
            stream, size_ids, lengths = lax.optimization_barrier((stream, size_ids, lengths))
            mask = target_mask(size_ids, lengths)
            live = jnp.sum(mask)
    grad, head_grad, gain_grad, loss = head(
        stream, targets, mask, wholes[-1], loaded[-1], gain_pairs[L]
    )
    raw = [gain_grad, loss]
    totals = [None] * count
    for n in reversed(range(count)):
        names = plan[n][0]
        layer = layers[n]
        grad, arrays, small = backward_layer(
            names,
            grad,
            kept[n],
            concat,
            ("head", head_grad) if n == count - 1 else None,
            wholes[n],
            loaded[n],
            wholes[n],
            gain_pairs[layer],
            tables,
        )
        raw += small
        if not direct:
            arrays = from_whole(groups[n], wholes[n], arrays, sizes)
        keep, give = arrays
        flying = totals[n + 1 :]
        give = after_landing(give, flying)
        totals[n] = Scatter(keep, give, sizes)
        if n:
            grad = hold(grad, totals[n], *flying)

    gain_grad, loss, *raw = raw
    gain_grads, bias_grads = {2 * L: gain_grad}, [None] * L
    for n in reversed(range(count)):
        names = plan[n][0]
        layer = layers[n]
        if "qkv" in names:
            gain_grads[2 * layer] = raw.pop(0)
            bias_grads[layer] = raw.pop(0).reshape(2, PAIRS, 8, 2, HD)
        if "gu" in names:
            gain_grads[2 * layer + 1] = raw.pop(0)
    gain_grads = [jnp.sum(gain_grads[g], axis=0) for g in range(NGAIN)]
    bias_grads = jnp.sum(jnp.stack(bias_grads), axis=(3, 5)).reshape(L, 2, H)

    small = jnp.concatenate([jnp.sum(loss)[None], live[None], bias_grads.reshape(-1)])
    small = jnp.pad(small, (0, D - small.shape[0]))
    rows = jnp.stack(gain_grads + [small])
    orders = sum_moves(sizes)
    rows = rows + swap(rows, sizes, *orders.pop(0))
    own_parts = [None] * count
    active = list(range(count))
    while active:
        for n in active:
            if not totals[n].moves:
                own_parts[n] = totals[n].total()
        active = [n for n in active if own_parts[n] is None]
        if not active:
            break
        moving = [totals[n] for n in active]
        rows = hold(rows, *moving)
        if orders:
            rows = rows + swap(rows, sizes, *orders.pop(0))
    while orders:
        rows = rows + swap(rows, sizes, *orders.pop(0))
    loss_sum, total_count = rows[NGAIN, 0], rows[NGAIN, 1]
    inverse_count = 1.0 / total_count
    bias_grad = rows[NGAIN, 2 : 2 + var_bias.size].reshape(var_bias.shape) * inverse_count
    gain_all = rows[:NGAIN]
    gain_own = lax.dynamic_slice_in_dim(gain_all, lax.axis_index("fsdp") * own, own, axis=1)

    squares = jnp.zeros((1, 1), F32)
    for n in range(count):
        squares = squares + groups[n].squares(own_parts[n])
    for fsdp_mask, dp_mask in sum_moves(sizes):
        if dp_mask < 2:
            squares = squares + swap(squares, sizes, fsdp_mask, dp_mask)
    squares = squares[0, 0]

    pieces = []
    for n in range(count):
        low, high = by_core(own_parts[n], swap(own_parts[n], sizes, 0, 1))
        pieces.append(groups[n].unpack((low, high)))
    in_piece = pieces[0]["in"][:, :IN_CAT]
    head_piece = pieces[-1]["head"]
    matrices = [[piece[m] for piece in pieces if m in piece] for m in ("qkv", "o", "gu", "d")]
    squares = squares + jnp.sum(jnp.square(gain_all))
    grad_norm = jnp.sqrt(
        squares * (inverse_count * inverse_count) + jnp.sum(bias_grad * bias_grad)
    )
    factor = jnp.minimum(1.0, CLIP_NORM / grad_norm)
    scale = factor * inverse_count

    gradients = [in_piece.T] + [jnp.stack(m) for m in matrices] + [head_piece, gain_own]
    clipped = [g.astype(F32) * scale for g in gradients] + [bias_grad * factor]
    fresh = [
        adam_update(masters[m], clipped[m], firsts[m], seconds[m], m < 6) for m in range(8)
    ]
    return (
        (loss_sum, total_count, grad_norm)
        + tuple(f[0] for f in fresh)
        + tuple(f[1] for f in fresh)
        + tuple(f[2] for f in fresh)
    )


def solution(mesh):
    sizes = (mesh.shape["fsdp"], mesh.shape["dp"])
    tokens = P(("fsdp", "dp"))
    tokens_two = P(("fsdp", "dp"), None)
    columns = P(None, "fsdp")
    stacked = P(None, "fsdp", None)
    states = (columns, stacked, stacked, stacked, stacked, P("fsdp", None), columns, P())
    in_specs = (tokens_two, tokens_two, tokens, tokens, tokens, tokens) + states * 3
    out_specs = (P(), P(), P()) + states * 3
    return jax.shard_map(
        functools.partial(per_device, sizes),
        mesh=mesh,
        in_specs=in_specs,
        out_specs=out_specs,
        check_vma=False,
    )
```

time: 435 us -> 365 us (0.84)
  waiting for transfers between devices: 162 us -> 85.3 us
  local copies, waits for them, and re-layouts: 19.9 us -> 26.4 us
  starting transfers between devices: 41.6 us -> 47.5 us
  other arithmetic: 58.9 us -> 53.2 us
  between operations: 16.4 us -> 11.1 us
    ppermute x38 -> x49, waiting for transfers between devices: 162 us -> 85.3 us  [swap(): return lax.ppermute(x, AXES, partners(sizes, fsdp_mask, dp_mask))]
    ppermute x38 -> x49, starting transfers between devices: 41.6 us -> 47.5 us  [swap(): return lax.ppermute(x, AXES, partners(sizes, fsdp_mask, dp_mask))]
    unnamed x128 -> x209, local copies, waits for them, and re-layouts: 11.9 us -> 16.5 us
    reduce_sum x22 -> x13, other arithmetic: 11.8 us -> 8.46 us  [the longest x4 3.73 us: squares(): jnp.sum(jnp.where(used, jnp.square(own.astype(F32)), 0.0)).reshape(1, 1)]
    pallas_call x6 -> x8, Pallas kernels: 123 us -> 126 us  [the longest x4 82.2 us: backward_layer(): pl.pallas_call(functools.partial(backward_body, names, extra[0] if extra...]
    convert_element_type x12 -> x16, other arithmetic: 11.1 us -> 8.64 us  [add(): return (a.astype(F32) + b.astype(F32)).astype(BF)]
  transfers between devices with their start and end apart: 38 -> 49, of which waited for: 24 -> 23; matrix products, arithmetic and copies ran while one was open for 9% -> 15% of each run, Pallas kernels for 19% -> 24%
where the time goes in v3:
time: 365 us; the launch traced here: 359 us
  Pallas kernels  136 us (37%)
  waiting for transfers between devices  85.3 us (23%)
  other arithmetic  53.2 us (15%)
  starting transfers between devices  47.5 us (13%)
  local copies, waits for them, and re-layouts  26.4 us (7%)
  between operations  11.1 us (3%)
    ppermute x49, waiting for transfers between devices, swap(): return lax.ppermute(x, AXES, partners(sizes, fsdp_mask, dp_mask))  85.3 us
    pallas_call x4, Pallas kernels, backward_layer(): pl.pallas_call(functools.partial(backward_body, names, extra[0] if extra...  82.2 us
    ppermute x49, starting transfers between devices, swap(): return lax.ppermute(x, AXES, partners(sizes, fsdp_mask, dp_mask))  47.5 us
    pallas_call x4, Pallas kernels, forward_layer(): pl.pallas_call(functools.partial(forward_body, names, group), grid=(rows...  43.8 us
    unnamed x209, local copies, waits for them, and re-layouts  16.5 us
    pallas_call x1, Pallas kernels, head(): pl.pallas_call(functools.partial(head_body, group), grid=(rows // TILE,),...  9.94 us
    convert_element_type x16, other arithmetic, add(): return (a.astype(F32) + b.astype(F32)).astype(BF)  8.64 us
    sub x6, other arithmetic, adam_update(): master_new = master - RATE_MATRIX * (direction + WEIGHT_DECAY * master)  8.17 us
  transfers between devices with their start and end apart: 49, of which 23 were waited for; matrix products, arithmetic and copies ran while one was open for 15% of the time, Pallas kernels for 24%

profile of v3, /device:TPU:0, one launch (start us, length us, event | category | flops | bytes accessed | tf_op | source)
XLA Modules:
  0.0 359.4 jit_solution(18161718247893018831)
XLA Ops:
  4.3 4.1 %collective-permute-start = (bf16[1,48,896]{2,1,0:T(8,128)(2,1)S(1)}, bf16[1,48,896]{2,1,0:T(8,128)(2,1)S(1)}, u32[]{:S(2)}, u32[]{:S(2)}) collective-permute-start(bf16[1,48,896]{2,1,0:T(8,128)(2,1)S(1)} %maximum_select_fusion.3), channel_id=1, source_target_pairs={{0,16},{1,17},{2,18},{3,19},{4,20},{5,21},{6,22},{7,23},{8,24},{9,... | collective-permute-start | bytes 258056 | tf_op jit(solution)/shard_map/ppermute | solution.py:677
  9.3 3.5 collective-permute-done
  21.0 3.4 collective-permute-start.4
  38.0 8.6 %collective-permute-done.7 = bf16[1,48,2432]{2,1,0:T(8,128)(2,1)S(1)} collective-permute-done((bf16[1,48,2432]{2,1,0:T(8,128)(2,1)}, bf16[1,48,2432]{2,1,0:T(8,128)(2,1)S(1)}, u32[]{:S(2)}, u32[]{:S(2)}) %collective-permute-start.7) | collective-permute-done | bytes 233504 | tf_op jit(solution)/shard_map/ppermute | solution.py:677
  50.3 8.7 %shard_map.493 = (f32[1024,384]{1,0:T(8,128)}, f32[8,384]{1,0:T(8,128)S(1)}, bf16[1024,1152]{1,0:T(8,128)(2,1)}, bf16[1024,384]{1,0:T(8,128)(2,1)S(1)}, bf16[102...) custom-call(bf16[1024,256]{1,0:T(8,128)(2,1)S(1)} %concatenate.211.refs_0_.refs_5_, ...), custom_call_target="tpu_custom_call" | custom-call | flops 1409286144 | bytes 16515072 | tf_op jit(solution)/shard_map/pallas_call | solution.py:381
  59.1 6.1 %collective-permute-done.6 = bf16[4,48,1664]{2,1,0:T(8,128)(2,1)S(1)} collective-permute-done((bf16[4,48,1664]{2,1,0:T(8,128)(2,1)S(1)}, bf16[4,48,1664]{2,1,0:T(8,128)(2,1)S(1)}, u32[]{:S(2)}, u32[]{:S(2)}) %collective-permute-start.6) | collective-permute-done | bytes 639008 | tf_op jit(solution)/shard_map/ppermute | solution.py:677
  69.0 6.2 %shard_map.494 = (f32[1024,384]{1,0:T(8,128)S(1)}, bf16[1024,2048]{1,0:T(8,128)(2,1)}) custom-call(f32[1024,384]{1,0:T(8,128)S(1)} %copy-done.15, bf16[8,48,1664]{2,1,0:T(8,128)(2,1)S(1)} %constant_dynamic-update-slice_fusion.7.refs_1_.refs_3_, bf16[8,48,1664]{2,1,0:T(8,128)(2,1)S(1)} %collective-permute-done.10.refs_2_.refs_4_, ...), custom_call_target="tpu_custom_call" | custom-call | flops 2415919104 | bytes 28311552 | tf_op jit(solution)/shard_map/pallas_call | solution.py:381
  75.3 15.0 %collective-permute-done.11 = bf16[4,48,2432]{2,1,0:T(8,128)(2,1)S(1)} collective-permute-done((bf16[4,48,2432]{2,1,0:T(8,128)(2,1)S(1)}, bf16[4,48,2432]{2,1,0:T(8,128)(2,1)S(1)}, u32[]{:S(2)}, u32[]{:S(2)}) %collective-permute-start.11) | collective-permute-done | bytes 933920 | tf_op jit(solution)/shard_map/ppermute | solution.py:677
  95.6 14.3 %shard_map.495 = (bf16[1024,1152]{1,0:T(8,128)(2,1)}, bf16[1024,384]{1,0:T(8,128)(2,1)S(1)}, bf16[1024,384]{1,0:T(8,128)(2,1)S(1)}, f32[1024,384]{1,0:T(8,128)S(...) custom-call(f32[1024,384]{1,0:T(8,128)} %copy-done.19, bf16[8,48,2432]{2,1,0:T(8,128)(2,1)} %copy-done.59, ...), custom_call_target="tpu_custom_call" | custom-call | flops 3623878656 | bytes 42467328 | tf_op jit(solution)/shard_map/pallas_call | solution.py:381
  111.9 6.1 %collective-permute-done.14 = bf16[4,48,2944]{2,1,0:T(8,128)(2,1)S(1)} collective-permute-done((bf16[4,48,2944]{2,1,0:T(8,128)(2,1)S(1)}, bf16[4,48,2944]{2,1,0:T(8,128)(2,1)S(1)}, u32[]{:S(2)}, u32[]{:S(2)}) %collective-permute-start.14) | collective-permute-done | bytes 1130528 | tf_op jit(solution)/shard_map/ppermute | solution.py:677
  119.5 4.3 %collective-permute-done.15.refs_2_.refs_1_.refs_9_ = bf16[8,48,2944]{2,1,0:T(8,128)(2,1)} collective-permute-done((bf16[8,48,2944]{2,1,0:T(8,128)(2,1)}, bf16[8,48,2944]{2,1,0:T(8,128)(2,1)}, u32[]{:S(2)}, u32[]{:S(2)}) %collective-permute-start.15) | collective-permute-done | bytes 2261024 | tf_op jit(solution)/shard_map/ppermute | solution.py:677
  123.9 14.5 %shard_map.496 = (bf16[1024,1152]{1,0:T(8,128)(2,1)}, bf16[1024,384]{1,0:T(8,128)(2,1)S(1)}, bf16[1024,384]{1,0:T(8,128)(2,1)S(1)}, f32[1024,384]{1,0:T(8,128)S(...) custom-call(f32[1024,384]{1,0:T(8,128)} %get-tuple-element.183.refs_0_.refs_1_, ...), custom_call_target="tpu_custom_call" | custom-call | flops 3623878656 | bytes 42467328 | tf_op jit(solution)/shard_map/pallas_call | solution.py:381
  141.6 9.9 %shard_map.497 = (f32[1024,384]{1,0:T(8,128)S(1)}, bf16[384,1152]{1,0:T(8,128)(2,1)S(1)}, f32[8,384]{1,0:T(8,128)S(1)}, f32[8,128]{1,0:T(8,128)S(1)}) custom-call(f32[1024,384]{1,0:T(8,128)S(1)} %copy-done.17, f32[1024,128]{1,0:T(8,128)S(1)} %copy-done.14, f32[1024,128]{1,0:T(8,128)S(1)} %fusion.3.mask_ref, ...), custom_call_target="tpu_custom_call" | custom-call | flops 2717908992 | bytes 8388608 | tf_op jit(solution)/shard_map/pallas_call | solution.py:450
  153.6 26.3 %shard_map.498 = (f32[1024,384]{1,0:T(8,128)}, bf16[8,48,2944]{2,1,0:T(8,128)(2,1)}, bf16[8,48,2944]{2,1,0:T(8,128)(2,1)}, f32[8,384]{1,0:T(8,128)}, f32[48,128]{1,0:T(8,128)}, /*index=5*/f32[8,384]{1,0:T(8,128)}) custom-call(f32[1024,384]{1,0:T(8,128)} %copy-done.16, f32[1024,384]{1,0:T(8,128)} %get-tuple-element.183.refs_0_.refs_1_, ...), custom_call_target="tpu_custom_call" | custom-call | flops 7247757312 | bytes 84934656 | tf_op jit(solution)/shard_map/pallas_call | solution.py:645
  180.2 4.4 %collective-permute-done.16 = bf16[8,48,2944]{2,1,0:T(8,128)(2,1)S(1)} collective-permute-done((bf16[8,48,2944]{2,1,0:T(8,128)(2,1)}, bf16[8,48,2944]{2,1,0:T(8,128)(2,1)S(1)}, u32[]{:S(2)}, u32[]{:S(2)}) %collective-permute-start.16) | collective-permute-done | bytes 2261024 | tf_op jit(solution)/shard_map/ppermute | solution.py:677
  187.4 25.8 %shard_map.499 = (f32[1024,384]{1,0:T(8,128)}, bf16[8,48,2432]{2,1,0:T(8,128)(2,1)}, bf16[8,48,2432]{2,1,0:T(8,128)(2,1)}, f32[8,384]{1,0:T(8,128)}, f32[48,128]{1,0:T(8,128)}, /*index=5*/f32[8,384]{1,0:T(8,128)}) custom-call(f32[1024,384]{1,0:T(8,128)} %get-tuple-element.198.refs_0_, f32[1024,384]{1,0:T(8,128)} %copy-done.19, ...), custom_call_target="tpu_custom_call" | custom-call | flops 7247757312 | bytes 84934656 | tf_op jit(solution)/shard_map/pallas_call | solution.py:645
  221.9 14.9 %shard_map.500 = (f32[1024,384]{1,0:T(8,128)}, bf16[8,48,1664]{2,1,0:T(8,128)(2,1)}, bf16[8,48,1664]{2,1,0:T(8,128)(2,1)}, f32[8,384]{1,0:T(8,128)}) custom-call(f32[1024,384]{1,0:T(8,128)} %get-tuple-element.211.refs_0_, f32[1024,384]{1,0:T(8,128)} %get-tuple-element.172.refs_0_.refs_1_, bf16[1024,2048]{1,0:T(8,128)(2,1)} %get-tuple-element.212.refs_2_, ...), custom_call_target="tpu_custom_call" | custom-call | flops 4831838208 | bytes 56623104 | tf_op jit(solution)/shard_map/pallas_call | solution.py:645
  236.9 4.4 %collective-permute-done.19 = bf16[4,48,2432]{2,1,0:T(8,128)(2,1)S(1)} collective-permute-done((bf16[4,48,2432]{2,1,0:T(8,128)(2,1)S(1)}, bf16[4,48,2432]{2,1,0:T(8,128)(2,1)S(1)}, u32[]{:S(2)}, u32[]{:S(2)}) %collective-permute-start.19) | collective-permute-done | bytes 933920 | tf_op jit(solution)/shard_map/ppermute | solution.py:677
  252.6 15.1 %shard_map.501 = (bf16[8,48,896]{2,1,0:T(8,128)(2,1)}, bf16[8,48,896]{2,1,0:T(8,128)(2,1)}, f32[8,384]{1,0:T(8,128)}, f32[48,128]{1,0:T(8,128)}) custom-call(f32[1024,384]{1,0:T(8,128)} %get-tuple-element.223.refs_0_, f32[1024,384]{1,0:T(8,128)} %get-tuple-element.224.refs_1_, bf16[1024,1152]{1,0:T(8,128)(2,1)} %get-tuple-element.225.refs_2_, ...), custom_call_target="tpu_custom_call" | custom-call | flops 2818572288 | bytes 33030144 | tf_op jit(solution)/shard_map/pallas_call | solution.py:645
  284.5 7.4 %collective-permute-done.30 = bf16[1,48,2432]{2,1,0:T(8,128)(2,1)S(1)} collective-permute-done((bf16[1,48,2432]{2,1,0:T(8,128)(2,1)}, bf16[1,48,2432]{2,1,0:T(8,128)(2,1)S(1)}, u32[]{:S(2)}, u32[]{:S(2)}) %collective-permute-start.30) | collective-permute-done | bytes 233504 | tf_op jit(solution)/shard_map/ppermute | solution.py:677
  292.0 3.4 collective-permute-done.29
  299.8 5.0 %collective-permute-done.31 = f32[8,384]{1,0:T(8,128)S(1)} collective-permute-done((f32[8,384]{1,0:T(8,128)S(1)}, f32[8,384]{1,0:T(8,128)S(1)}, u32[]{:S(2)}, u32[]{:S(2)}) %collective-permute-start.31) | collective-permute-done | bytes 12320 | tf_op jit(solution)/shard_map/ppermute | solution.py:677
  304.9 3.5 collective-permute-done.32
  329.3 3.4 collective-permute-start.42
  (463 shorter events, 129.5 us)
Async XLA Ops:
  21.0 12.6 %collective-permute-start.4 = (bf16[1,48,1664]{2,1,0:T(8,128)(2,1)S(1)}, bf16[1,48,1664]{2,1,0:T(8,128)(2,1)S(1)}, u32[]{:S(2)}, u32[]{:S(2)}) collective-permute-start(bf16[1,48,1664]{2,1,0:T(8,128)(2,1)S(1)} %maximum_select_fusion.2), channel_id=1, source_target_pairs={{0,16},{1,17},{2,18},{3,19},{4,20},{5,21},{6,22},{7,23},{8,24},{9,... | collective-permute-start | bytes 479240 | tf_op jit(solution)/shard_map/ppermute | solution.py:677
  33.6 12.9 %collective-permute-start.7 = (bf16[1,48,2432]{2,1,0:T(8,128)(2,1)}, bf16[1,48,2432]{2,1,0:T(8,128)(2,1)S(1)}, u32[]{:S(2)}, u32[]{:S(2)}) collective-permute-start(bf16[1,48,2432]{2,1,0:T(8,128)(2,1)} %maximum_select_fusion.1), channel_id=1, source_target_pairs={{0,16},{1,17},{2,18},{3,19},{4,20},{5,21},{6,22},{7,23},{8,24},{9,... | collective-permute-start | bytes 700424 | tf_op jit(solution)/shard_map/ppermute | solution.py:677
  35.2 14.2 %collective-permute-start.5 = (bf16[2,48,1664]{2,1,0:T(8,128)(2,1)S(1)}, bf16[2,48,1664]{2,1,0:T(8,128)(2,1)S(1)}, u32[]{:S(2)}, u32[]{:S(2)}) collective-permute-start(bf16[2,48,1664]{2,1,0:T(8,128)(2,1)S(1)} %pad_maximum_fusion.12), channel_id=1, source_target_pairs={{0,8},{1,9},{2,10},{3,11},{4,12},{5,13},{6,14},{7,15},{8,0},{9,1},... | collective-permute-start | bytes 958472 | tf_op jit(solution)/shard_map/ppermute | solution.py:677
  37.9 12.4 %collective-permute-start.3 = (bf16[8,48,896]{2,1,0:T(8,128)(2,1)S(1)}, bf16[8,48,896]{2,1,0:T(8,128)(2,1)S(1)}, u32[]{:S(2)}, u32[]{:S(2)}) collective-permute-start(bf16[8,48,896]{2,1,0:T(8,128)(2,1)S(1)} %pad_maximum_fusion.2.refs_1_.refs_6_), channel_id=1, source_target_pairs={{0,1},{1,0},{2,3},{3,2},{4,5},{5,4},{6,7},{7,6},{8,9},{9,8},{10,11... | collective-permute-start | bytes 2064392 | tf_op jit(solution)/shard_map/ppermute | solution.py:677
  47.6 18.3 %collective-permute-start.8 = (bf16[2,48,2432]{2,1,0:T(8,128)(2,1)S(1)}, bf16[2,48,2432]{2,1,0:T(8,128)(2,1)S(1)}, u32[]{:S(2)}, u32[]{:S(2)}) collective-permute-start(bf16[2,48,2432]{2,1,0:T(8,128)(2,1)S(1)} %pad_maximum_fusion.9), channel_id=1, source_target_pairs={{0,8},{1,9},{2,10},{3,11},{4,12},{5,13},{6,14},{7,15},{8,0},{9,1},... | collective-permute-start | bytes 1400840 | tf_op jit(solution)/shard_map/ppermute | solution.py:677
  47.6 20.4 %collective-permute-start.9 = (bf16[1,48,2944]{2,1,0:T(8,128)(2,1)S(1)}, bf16[1,48,2944]{2,1,0:T(8,128)(2,1)S(1)}, u32[]{:S(2)}, u32[]{:S(2)}) collective-permute-start(bf16[1,48,2944]{2,1,0:T(8,128)(2,1)S(1)} %copy-done.28), channel_id=1, source_target_pairs={{0,16},{1,17},{2,18},{3,19},{4,20},{5,21},{6,22},{7,23},{8,24},{9,... | collective-permute-start | bytes 847880 | tf_op jit(solution)/shard_map/ppermute | solution.py:677
  49.6 15.7 %collective-permute-start.6 = (bf16[4,48,1664]{2,1,0:T(8,128)(2,1)S(1)}, bf16[4,48,1664]{2,1,0:T(8,128)(2,1)S(1)}, u32[]{:S(2)}, u32[]{:S(2)}) collective-permute-start(bf16[4,48,1664]{2,1,0:T(8,128)(2,1)S(1)} %pad_maximum_fusion.3), channel_id=1, source_target_pairs={{0,4},{1,5},{2,6},{3,7},{4,0},{5,1},{6,2},{7,3},{8,12},{9,13},{10,... | collective-permute-start | bytes 1916936 | tf_op jit(solution)/shard_map/ppermute | solution.py:677
  67.4 22.9 %collective-permute-start.11 = (bf16[4,48,2432]{2,1,0:T(8,128)(2,1)S(1)}, bf16[4,48,2432]{2,1,0:T(8,128)(2,1)S(1)}, u32[]{:S(2)}, u32[]{:S(2)}) collective-permute-start(bf16[4,48,2432]{2,1,0:T(8,128)(2,1)S(1)} %pad_maximum_fusion.1), channel_id=1, source_target_pairs={{0,4},{1,5},{2,6},{3,7},{4,0},{5,1},{6,2},{7,3},{8,12},{9,13},{10,... | collective-permute-start | bytes 2801672 | tf_op jit(solution)/shard_map/ppermute | solution.py:677
  68.1 22.4 %collective-permute-start.12 = (bf16[2,48,2944]{2,1,0:T(8,128)(2,1)S(1)}, bf16[2,48,2944]{2,1,0:T(8,128)(2,1)S(1)}, u32[]{:S(2)}, u32[]{:S(2)}) collective-permute-start(bf16[2,48,2944]{2,1,0:T(8,128)(2,1)S(1)} %pad_maximum_fusion.5), channel_id=1, source_target_pairs={{0,8},{1,9},{2,10},{3,11},{4,12},{5,13},{6,14},{7,15},{8,0},{9,1},... | collective-permute-start | bytes 1695752 | tf_op jit(solution)/shard_map/ppermute | solution.py:677
  90.7 27.4 %collective-permute-start.14 = (bf16[4,48,2944]{2,1,0:T(8,128)(2,1)S(1)}, bf16[4,48,2944]{2,1,0:T(8,128)(2,1)S(1)}, u32[]{:S(2)}, u32[]{:S(2)}) collective-permute-start(bf16[4,48,2944]{2,1,0:T(8,128)(2,1)S(1)} %pad_maximum_fusion), channel_id=1, source_target_pairs={{0,4},{1,5},{2,6},{3,7},{4,0},{5,1},{6,2},{7,3},{8,12},{9,13},{10,... | collective-permute-start | bytes 3391496 | tf_op jit(solution)/shard_map/ppermute | solution.py:677
  186.8 27.1 %collective-permute-start.17 = (bf16[4,48,2944]{2,1,0:T(8,128)(2,1)S(1)}, bf16[4,48,2944]{2,1,0:T(8,128)(2,1)S(1)}, u32[]{:S(2)}, u32[]{:S(2)}) collective-permute-start(bf16[4,48,2944]{2,1,0:T(8,128)(2,1)S(1)} %get-tuple-element.207), channel_id=1, source_target_pairs={{0,4},{1,5},{2,6},{3,7},{4,0},{5,1},{6,2},{7,3},{8,12},{9,13},{10,... | collective-permute-start | bytes 3391496 | tf_op jit(solution)/shard_map/ppermute | solution.py:677
  218.5 22.8 %collective-permute-start.19 = (bf16[4,48,2432]{2,1,0:T(8,128)(2,1)S(1)}, bf16[4,48,2432]{2,1,0:T(8,128)(2,1)S(1)}, u32[]{:S(2)}, u32[]{:S(2)}) collective-permute-start(bf16[4,48,2432]{2,1,0:T(8,128)(2,1)S(1)} %get-tuple-element.216), channel_id=1, source_target_pairs={{0,4},{1,5},{2,6},{3,7},{4,0},{5,1},{6,2},{7,3},{8,12},{9,13},{10,... | collective-permute-start | bytes 2801672 | tf_op jit(solution)/shard_map/ppermute | solution.py:677
  220.7 16.1 %collective-permute-start.20 = (bf16[2,48,2944]{2,1,0:T(8,128)(2,1)S(1)}, bf16[2,48,2944]{2,1,0:T(8,128)(2,1)S(1)}, u32[]{:S(2)}, u32[]{:S(2)}) collective-permute-start(bf16[2,48,2944]{2,1,0:T(8,128)(2,1)S(1)} %get-tuple-element.217), channel_id=1, source_target_pairs={{0,8},{1,9},{2,10},{3,11},{4,12},{5,13},{6,14},{7,15},{8,0},{9,1},... | collective-permute-start | bytes 1695752 | tf_op jit(solution)/shard_map/ppermute | solution.py:677
  244.8 28.8 %collective-permute-start.23 = (bf16[4,48,1664]{2,1,0:T(8,128)(2,1)S(1)}, bf16[4,48,1664]{2,1,0:T(8,128)(2,1)S(1)}, u32[]{:S(2)}, u32[]{:S(2)}) collective-permute-start(bf16[4,48,1664]{2,1,0:T(8,128)(2,1)S(1)} %get-tuple-element.241), channel_id=1, source_target_pairs={{0,4},{1,5},{2,6},{3,7},{4,0},{5,1},{6,2},{7,3},{8,12},{9,13},{10,... | collective-permute-start | bytes 1916936 | tf_op jit(solution)/shard_map/ppermute | solution.py:677
  250.3 23.3 %collective-permute-start.24 = (bf16[2,48,2432]{2,1,0:T(8,128)(2,1)S(1)}, bf16[2,48,2432]{2,1,0:T(8,128)(2,1)}, u32[]{:S(2)}, u32[]{:S(2)}) collective-permute-start(bf16[2,48,2432]{2,1,0:T(8,128)(2,1)S(1)} %get-tuple-element.242), channel_id=1, source_target_pairs={{0,8},{1,9},{2,10},{3,11},{4,12},{5,13},{6,14},{7,15},{8,0},{9,1},... | collective-permute-start | bytes 1400840 | tf_op jit(solution)/shard_map/ppermute | solution.py:677
  250.4 23.2 %collective-permute-start.25 = (bf16[1,48,2944]{2,1,0:T(8,128)(2,1)}, bf16[1,48,2944]{2,1,0:T(8,128)(2,1)}, u32[]{:S(2)}, u32[]{:S(2)}) collective-permute-start(bf16[1,48,2944]{2,1,0:T(8,128)(2,1)} %get-tuple-element.243), channel_id=1, source_target_pairs={{0,16},{1,17},{2,18},{3,19},{4,20},{5,21},{6,22},{7,23},{8,24},{9,... | collective-permute-start | bytes 847880 | tf_op jit(solution)/shard_map/ppermute | solution.py:677
  277.9 14.0 %collective-permute-start.30 = (bf16[1,48,2432]{2,1,0:T(8,128)(2,1)}, bf16[1,48,2432]{2,1,0:T(8,128)(2,1)S(1)}, u32[]{:S(2)}, u32[]{:S(2)}) collective-permute-start(bf16[1,48,2432]{2,1,0:T(8,128)(2,1)} %get-tuple-element.257), channel_id=1, source_target_pairs={{0,16},{1,17},{2,18},{3,19},{4,20},{5,21},{6,22},{7,23},{8,24},{9,... | collective-permute-start | bytes 700424 | tf_op jit(solution)/shard_map/ppermute | solution.py:677
  280.9 14.5 %collective-permute-start.29 = (bf16[2,48,1664]{2,1,0:T(8,128)(2,1)}, bf16[2,48,1664]{2,1,0:T(8,128)(2,1)S(1)}, u32[]{:S(2)}, u32[]{:S(2)}) collective-permute-start(bf16[2,48,1664]{2,1,0:T(8,128)(2,1)} %get-tuple-element.255), channel_id=1, source_target_pairs={{0,8},{1,9},{2,10},{3,11},{4,12},{5,13},{6,14},{7,15},{8,0},{9,1},... | collective-permute-start | bytes 958472 | tf_op jit(solution)/shard_map/ppermute | solution.py:677
  282.8 12.7 %collective-permute-start.28 = (bf16[4,48,896]{2,1,0:T(8,128)(2,1)S(1)}, bf16[4,48,896]{2,1,0:T(8,128)(2,1)S(1)}, u32[]{:S(2)}, u32[]{:S(2)}) collective-permute-start(bf16[4,48,896]{2,1,0:T(8,128)(2,1)S(1)} %get-tuple-element.253), channel_id=1, source_target_pairs={{0,4},{1,5},{2,6},{3,7},{4,0},{5,1},{6,2},{7,3},{8,12},{9,13},{10,... | collective-permute-start | bytes 1032200 | tf_op jit(solution)/shard_map/ppermute | solution.py:677
  283.9 14.7 %collective-permute-start.40 = (bf16[1,48,2944]{2,1,0:T(8,128)(2,1)S(1)}, bf16[1,48,2944]{2,1,0:T(8,128)(2,1)S(1)}, u32[]{:S(2)}, u32[]{:S(2)}) collective-permute-start(bf16[1,48,2944]{2,1,0:T(8,128)(2,1)S(1)} %add_convert_fusion.15), channel_id=1, source_target_pairs={{0,2},{1,3},{2,0},{3,1},{4,6},{5,7},{6,4},{7,5},{8,10},{9,11},{10,... | collective-permute-start | bytes 847880 | tf_op jit(solution)/shard_map/ppermute | solution.py:677
  299.8 13.5 %collective-permute-start.47 = (bf16[48,2944]{1,0:T(8,128)(2,1)S(1)}, bf16[48,2944]{1,0:T(8,128)(2,1)S(1)}, u32[]{:S(2)}, u32[]{:S(2)}) collective-permute-start(bf16[48,2944]{1,0:T(8,128)(2,1)S(1)} %get-tuple-element.300), channel_id=1, source_target_pairs={{0,1},{1,0},{2,3},{3,2},{4,5},{5,4},{6,7},{7,6},{8,9},{9,8},{10,11... | collective-permute-start | bytes 847880 | tf_op jit(solution)/shard_map/ppermute | solution.py:677
  318.7 29.1 %collective-permute-start.46 = (bf16[48,2432]{1,0:T(8,128)(2,1)S(1)}, bf16[48,2432]{1,0:T(8,128)(2,1)S(1)}, u32[]{:S(2)}, u32[]{:S(2)}) collective-permute-start(bf16[48,2432]{1,0:T(8,128)(2,1)S(1)} %get-tuple-element.302), channel_id=1, source_target_pairs={{0,1},{1,0},{2,3},{3,2},{4,5},{5,4},{6,7},{7,6},{8,9},{9,8},{10,11... | collective-permute-start | bytes 700424 | tf_op jit(solution)/shard_map/ppermute | solution.py:677
  323.7 27.6 %collective-permute-start.48 = (bf16[48,1664]{1,0:T(8,128)(2,1)S(1)}, bf16[48,1664]{1,0:T(8,128)(2,1)}, u32[]{:S(2)}, u32[]{:S(2)}) collective-permute-start(bf16[48,1664]{1,0:T(8,128)(2,1)S(1)} %get-tuple-element.304), channel_id=1, source_target_pairs={{0,1},{1,0},{2,3},{3,2},{4,5},{5,4},{6,7},{7,6},{8,9},{9,8},{10,11... | collective-permute-start | bytes 479240 | tf_op jit(solution)/shard_map/ppermute | solution.py:677
  328.6 18.4 %collective-permute-start.45 = (bf16[48,896]{1,0:T(8,128)(2,1)S(1)}, bf16[48,896]{1,0:T(8,128)(2,1)S(1)}, u32[]{:S(2)}, u32[]{:S(2)}) collective-permute-start(bf16[48,896]{1,0:T(8,128)(2,1)S(1)} %get-tuple-element.306), channel_id=1, source_target_pairs={{0,1},{1,0},{2,3},{3,2},{4,5},{5,4},{6,7},{7,6},{8,9},{9,8},{10,11... | collective-permute-start | bytes 258056 | tf_op jit(solution)/shard_map/ppermute | solution.py:677
  (123 other events, 1372.0 us)

commit v4 on v3

--- a/solution.py
+++ b/solution.py
@@ -24,6 +24,7 @@
 LANES = 2 * HD
 
 TILE = 256
+FORWARD_TILE = 512
 
 EPS_NORM = 1e-05
 SMOOTH = 0.5
@@ -164,7 +165,7 @@
 def place(group):
     if group.shards == 1:
         return 0, 0
-    return lax.axis_index("fsdp"), lax.axis_index("dp") & 1
+    return lax.axis_index("fsdp"), lax.axis_index("dp") & (group.parts - 1)
 
 
 def copies(group, arrays, me, targets, sems, outward):
@@ -197,8 +198,8 @@
     if group.shards == 1 or group.parts == 1:
         go(0)
     else:
-        pl.when(core == 0)(functools.partial(go, 0))
-        pl.when(core == 1)(functools.partial(go, 1))
+        for which in range(group.parts):
+            pl.when(core == which)(functools.partial(go, which))
 
 
 def wait_copies(made, names):
@@ -341,8 +342,8 @@
         out_ref[...] = middle + dot_nn(hidden, w["d"][...])
 
 
-def rows_spec(width):
-    return pl.BlockSpec((TILE, width), lambda i: (i, 0))
+def rows_spec(width, tile=TILE):
+    return pl.BlockSpec((tile, width), lambda i: (i, 0))
 
 
 def whole_spec(shape):
@@ -360,17 +361,17 @@
     first, attn, ffn = "in" in names, "qkv" in names, "gu" in names
     rows = x.shape[0]
     args = [x, *arrays]
-    in_specs = [rows_spec(x.shape[1])] + [any_spec()] * group.parts
+    in_specs = [rows_spec(x.shape[1], FORWARD_TILE)] + [any_spec()] * group.parts
     if not first:
         args.append(gain_pair)
         in_specs.append(whole_spec(gain_pair.shape))
     if attn:
         args += [bias_rows, *tables]
-        in_specs += [whole_spec(bias_rows.shape)] + [rows_spec(LANES)] * 3
+        in_specs += [whole_spec(bias_rows.shape)] + [rows_spec(LANES, FORWARD_TILE)] * 3
     outs = [(D, F32)] if first else []
     outs += [(QKV, BF), (D, BF), (D, BF), (D, F32)] if attn else []
     outs += [(D, F32), (2 * FF, BF)] if ffn else []
-    out_specs = [rows_spec(w) for w, _ in outs]
+    out_specs = [rows_spec(w, FORWARD_TILE) for w, _ in outs]
     out_shape = [jax.ShapeDtypeStruct((rows, w), t) for w, t in outs]
     scratch = [pltpu.VMEM(WEIGHTS[n], BF) for n in names] + [semaphores(group)]
     if first:
@@ -380,7 +381,7 @@
     size = sum(WEIGHTS[n][0] * WEIGHTS[n][1] for n in names)
     return pl.pallas_call(
         functools.partial(forward_body, names, group),
-        grid=(rows // TILE,),
+        grid=(rows // FORWARD_TILE,),
         in_specs=in_specs,
         out_specs=out_specs,
         out_shape=out_shape,
@@ -515,6 +516,7 @@
     step = pl.program_id(0)
     me, core = place(group)
     made = copies(group, arrays, me, down_fields(w), sems, outward=False)
+    out_core = place(out_group)[1]
     sent = copies(
         out_group, out_arrays, me, {**down_fields(grads), **extras}, out_sems, outward=True
     )
@@ -608,7 +610,7 @@
     def _():
         for name in names:
             grads[name][...] = acc[name][...].astype(BF)
-        start_copies(out_group, sent, core)
+        start_copies(out_group, sent, out_core)
         wait_copies(sent, list(sent))
 
 
@@ -688,33 +690,59 @@
 
 
 class Gather:
-    def __init__(self, halves, sizes):
-        core = lax.axis_index("dp") & 1
+    def __init__(self, parts, sizes):
         self.sizes = sizes
-        self.mine = jnp.where(core == 0, halves[0], halves[1])[None]
+        self.four = len(parts) == 4
+        self.mine = by_place(parts)[0][None]
         self.masks = masks_of(sizes[0])
-        self.got = None
+        self.last = self.masks.pop() if self.four else 0
+        self.got = ()
+
+    def land(self):
+        if self.got:
+            self.mine = jnp.concatenate([self.mine, *self.got], axis=0)
+            self.got = ()
+        return self.mine
 
     def move(self, after=None):
         mine = self.land()
         if after is not None:
             mine, after.got = lax.optimization_barrier((mine, after.got))
         self.mine = mine
-        self.got = swap(mine, self.sizes, self.masks.pop(0), 0)
-
-    def land(self):
-        if self.got is not None:
-            self.mine = jnp.concatenate([self.mine, self.got], axis=0)
-            self.got = None
-        return self.mine
+        self.got = (swap(mine, self.sizes, self.masks.pop(0), 0),)
+
+    def ring(self):
+        mine = self.land()
+        self.got = (swap(mine, self.sizes, self.last, 0), swap(mine, self.sizes, 0, 2))
 
     def hold(self, x):
         x, self.got = lax.optimization_barrier((x, self.got))
         return x
 
-    def pair(self):
-        mine = self.land()
-        return mine, swap(mine, self.sizes, 0, 1)
+    def arrays(self):
+        if not self.four:
+            mine = self.land()
+            return mine, swap(mine, self.sizes, 0, 1)
+        near, far = self.got
+        half = near.shape[0] // 2
+        corner = (
+            swap(far[:half], self.sizes, self.last, 0),
+            swap(near[half:], self.sizes, 0, 2),
+        )
+        mine = jnp.concatenate([self.mine, near], axis=0)
+        far = jnp.concatenate([far, *corner], axis=0)
+        return mine, swap(mine, self.sizes, 0, 1), far, swap(far, self.sizes, 0, 1)
+
+
+def by_place(parts):
+    place = lax.axis_index("dp") & (len(parts) - 1)
+    found = []
+    for distance in range(len(parts)):
+        one = parts[distance]
+        for other in range(1, len(parts)):
+            one = jnp.where(place == other, parts[other ^ distance], one)
+        found.append(one)
+    return found
 
 
 def by_core(mine, other):
@@ -783,9 +811,8 @@
 
 
 def to_whole(group, whole, arrays, sizes):
-    if group.parts == 2:
-        masks = masks_of(sizes[0])
-        arrays = [reorder(a, masks) for a in by_core(*arrays)]
+    masks = masks_of(sizes[0])
+    arrays = [reorder(a, masks) for a in by_place(arrays)]
     fields = group.unpack(arrays)
     fields = {n: p.reshape(1, p.shape[0] * p.shape[1], p.shape[2]) for n, p in fields.items()}
     return whole.pack(fields)
@@ -884,43 +911,41 @@
 
     fields = [f for _, f in plan]
     groups, wholes = groups_of(fields, [2] * count)
+    in_fields = [fields[0] + fields[1], fields[2], fields[3]]
+    in_groups, in_wholes = groups_of(in_fields, [4, 2, 4])
+    sources = [0, 0, 1, 2]
 
     in_rows = jnp.concatenate(
         [w_in.T, gains.T, jnp.zeros((own, 2 * PMAX - IN_CAT - NGAIN), F32)], axis=1
     ).astype(BF)
-    def packed(n, stacks, head_w=None):
-        fields = {m: w[layers[n]].astype(BF) for m, w in zip(("qkv", "o", "gu", "d"), stacks)}
-        if n == count - 1:
+    def packed(layer, stacks, head_w=None):
+        fields = {m: w[layer].astype(BF) for m, w in zip(("qkv", "o", "gu", "d"), stacks)}
+        if layer == L - 1:
             fields["head"] = head_w.astype(BF)
-        return groups[n].pack({**fields, "in": in_rows})
+        return in_groups[layer].pack({**fields, "in": in_rows})
 
     stacks = (w_qkv, w_o, w_gu, w_down)
-    gathers = [Gather(packed(0, stacks), sizes)]
-    steps = len(gathers[0].masks)
-    gathers[0].move()
-    stacks, head_w, time_ids = gathers[0].hold((stacks, w_head, time_ids))
-    gathers += [Gather(packed(n, stacks, head_w), sizes) for n in range(1, count)]
+    first = Gather(packed(0, stacks), sizes)
+    first.move()
+    stacks, head_w, time_ids = first.hold((stacks, w_head, time_ids))
+    second, third = [Gather(packed(layer, stacks, head_w), sizes) for layer in (1, 2)]
     cos, sin = rotary_tables(time_ids)
-    for _ in range(steps - 2):
-        gathers[0].move()
+    while first.masks:
+        first.move()
     early = (patches, size_ids, variate_ids, lengths)
-    early, gathers[1].mine = gathers[0].hold((early, gathers[1].mine))
+    early, second.mine = first.hold((early, second.mine))
     patches, size_ids, variate_ids, lengths = early
-    gathers[0].move()
-    for _ in range(steps - 2):
-        gathers[1].move()
-    gathers[2].move(gathers[1])
-    gathers[1].move()
-    gathers[3].move(gathers[2])
-    for _ in range(steps - 2):
-        gathers[2].move()
-    gathers[1].move()
-    for _ in range(steps - 3):
-        gathers[3].move()
-
-    def arrived(n):
-        arrays = gathers[n].pair()
-        return arrays if direct else to_whole(groups[n], wholes[n], arrays, sizes)
+    first.ring()
+    second.move()
+    third.move(second)
+    while second.masks:
+        second.move()
+    while len(third.masks) > 1:
+        third.move()
+
+    def arrived(layer):
+        arrays = (first, second, third)[layer].arrays()
+        return arrays if direct else to_whole(in_groups[layer], in_wholes[layer], arrays, sizes)
 
     tables = (cos, sin, code_table(variate_ids, lengths))
     concat = patch_concat(patches, size_ids)
@@ -932,37 +957,45 @@
     kept = [None] * count
     loaded = []
     gain_pairs = [None] * (L + 1)
-    for n, layer in enumerate(layers):
-        names = plan[n][0]
-        loaded.append(arrived(n))
-        for one in gathers[n + 1 :]:
-            if n and one.masks:
-                one.move()
+    for layer in range(L):
+        if layer == 1:
+            second.mine, third.got = lax.optimization_barrier((second.land(), third.got))
+        loaded.append(arrived(layer))
+        if layer == 0:
+            third.mine, stream = lax.optimization_barrier((third.land(), stream))
+            while third.masks:
+                third.move()
+        if layer == 1:
+            third.ring()
+        names = ATTN + FFN if layer else ("in",) + ATTN + FFN
         got = list(
             forward_layer(
-                stream, names, wholes[n], loaded[n], gain_pairs[layer], bias_lanes[layer], tables
+                stream,
+                names,
+                in_wholes[layer],
+                loaded[layer],
+                gain_pairs[layer],
+                bias_lanes[layer],
+                tables,
             )
         )
-        if n == 0:
+        if layer == 0:
             stream, found = got[:2]
             got = got[2:]
             gain_pairs = [found[0:2], found[2:4], found[4:6], found[6:8]]
             kept[0] = [stream, *got[:3]]
-            stream = got[3]
-        elif n == 1:
-            kept[1] = [stream, got[1]]
-            stream = got[0]
+            kept[1] = [got[3], got[5]]
         else:
-            kept[n] = [stream, *got[:4], got[5]]
-            stream = got[4]
-        for one in gathers[n + 1 :]:
+            kept[layer + 1] = [stream, *got[:4], got[5]]
+        stream = got[4]
+        for one in (second, third)[layer:]:
             stream = one.hold(stream)
-        if n == 0:
+        if layer == 0:
             stream, size_ids, lengths = lax.optimization_barrier((stream, size_ids, lengths))
             mask = target_mask(size_ids, lengths)
             live = jnp.sum(mask)
     grad, head_grad, gain_grad, loss = head(
-        stream, targets, mask, wholes[-1], loaded[-1], gain_pairs[L]
+        stream, targets, mask, in_wholes[-1], loaded[-1], gain_pairs[L]
     )
     raw = [gain_grad, loss]
     totals = [None] * count
@@ -975,8 +1008,8 @@
             kept[n],
             concat,
             ("head", head_grad) if n == count - 1 else None,
-            wholes[n],
-            loaded[n],
+            in_wholes[sources[n]],
+            loaded[sources[n]],
             wholes[n],
             gain_pairs[layer],
             tables,
@@ -991,6 +1024,7 @@
         if n:
             grad = hold(grad, totals[n], *flying)
 
+    raw = hold(raw, *totals)
     gain_grad, loss, *raw = raw
     gain_grads, bias_grads = {2 * L: gain_grad}, [None] * L
     for n in reversed(range(count)):
@@ -1007,36 +1041,35 @@
     small = jnp.concatenate([jnp.sum(loss)[None], live[None], bias_grads.reshape(-1)])
     small = jnp.pad(small, (0, D - small.shape[0]))
     rows = jnp.stack(gain_grads + [small])
-    orders = sum_moves(sizes)
-    rows = rows + swap(rows, sizes, *orders.pop(0))
+    pending = list(zip(range(count), totals))
     own_parts = [None] * count
-    active = list(range(count))
-    while active:
-        for n in active:
-            if not totals[n].moves:
-                own_parts[n] = totals[n].total()
-        active = [n for n in active if own_parts[n] is None]
-        if not active:
+    first = True
+    while pending:
+        for n, one in pending:
+            if not one.moves:
+                own_parts[n] = one.total()
+        pending = [(n, one) for n, one in pending if one.moves]
+        if not pending:
             break
-        moving = [totals[n] for n in active]
-        rows = hold(rows, *moving)
-        if orders:
-            rows = rows + swap(rows, sizes, *orders.pop(0))
-    while orders:
-        rows = rows + swap(rows, sizes, *orders.pop(0))
+        if not first:
+            hold((), *[one for _, one in pending])
+        first = False
+    squares = jnp.zeros((1, 1), F32)
+    for n in range(count):
+        squares = squares + groups[n].squares(own_parts[n])
+    rows = rows + jnp.pad(squares, ((NGAIN, 0), (D - 1, 0)))
+    for fsdp_mask, dp_mask in sum_moves(sizes):
+        rows = rows + swap(rows, sizes, fsdp_mask, dp_mask)
+    squares = rows[NGAIN, D - 1] / (sizes[1] // 2)
     loss_sum, total_count = rows[NGAIN, 0], rows[NGAIN, 1]
     inverse_count = 1.0 / total_count
     bias_grad = rows[NGAIN, 2 : 2 + var_bias.size].reshape(var_bias.shape) * inverse_count
+    at_row = lax.broadcasted_iota(jnp.int32, rows.shape, 0)
+    at_col = lax.broadcasted_iota(jnp.int32, rows.shape, 1)
+    counted = (at_row < NGAIN) | ((at_col >= 2) & (at_col < 2 + var_bias.size))
+    squares = squares + jnp.sum(jnp.where(counted, jnp.square(rows), 0.0))
     gain_all = rows[:NGAIN]
     gain_own = lax.dynamic_slice_in_dim(gain_all, lax.axis_index("fsdp") * own, own, axis=1)
-
-    squares = jnp.zeros((1, 1), F32)
-    for n in range(count):
-        squares = squares + groups[n].squares(own_parts[n])
-    for fsdp_mask, dp_mask in sum_moves(sizes):
-        if dp_mask < 2:
-            squares = squares + swap(squares, sizes, fsdp_mask, dp_mask)
-    squares = squares[0, 0]
 
     pieces = []
     for n in range(count):
@@ -1045,10 +1078,7 @@
     in_piece = pieces[0]["in"][:, :IN_CAT]
     head_piece = pieces[-1]["head"]
     matrices = [[piece[m] for piece in pieces if m in piece] for m in ("qkv", "o", "gu", "d")]
-    squares = squares + jnp.sum(jnp.square(gain_all))
-    grad_norm = jnp.sqrt(
-        squares * (inverse_count * inverse_count) + jnp.sum(bias_grad * bias_grad)
-    )
+    grad_norm = jnp.sqrt(squares) * inverse_count
     factor = jnp.minimum(1.0, CLIP_NORM / grad_norm)
     scale = factor * inverse_count
 

time: 365 us -> 343 us (0.940)
  starting transfers between devices: 47.5 us -> 41.3 us
  waiting for transfers between devices: 85.3 us -> 80.2 us
  Pallas kernels: 136 us -> 131 us
    pallas_call x4 -> x3, Pallas kernels: 43.8 us -> 37.6 us  [forward_layer(): pl.pallas_call(functools.partial(forward_body, names, group), grid=(rows...]
    ppermute x49, starting transfers between devices: 47.5 us -> 41.3 us  [swap(): return lax.ppermute(x, AXES, partners(sizes, fsdp_mask, dp_mask))]
    ppermute x49, waiting for transfers between devices: 85.3 us -> 80.2 us  [swap(): return lax.ppermute(x, AXES, partners(sizes, fsdp_mask, dp_mask))]
    unnamed x209 -> x178, local copies, waits for them, and re-layouts: 16.5 us -> 15.9 us
  transfers between devices with their start and end apart: 49 -> 49, of which waited for: 23 -> 25; matrix products, arithmetic and copies ran while one was open for 15% -> 16% of each run, Pallas kernels for 24% -> 24%
where the time goes in v4:
time: 343 us; the launch traced here: 337 us
  Pallas kernels  131 us (38%)
  waiting for transfers between devices  80.2 us (23%)
  other arithmetic  50.3 us (15%)
  starting transfers between devices  41.3 us (12%)
  local copies, waits for them, and re-layouts  25.8 us (8%)
  between operations  8.64 us (3%)
    pallas_call x4, Pallas kernels, backward_layer(): pl.pallas_call(functools.partial(backward_body, names, extra[0] if extra...  83.3 us
    ppermute x49, waiting for transfers between devices, swap(): return lax.ppermute(x, AXES, partners(sizes, fsdp_mask, dp_mask))  80.2 us
    ppermute x49, starting transfers between devices, swap(): return lax.ppermute(x, AXES, partners(sizes, fsdp_mask, dp_mask))  41.3 us
    pallas_call x3, Pallas kernels, forward_layer(): pl.pallas_call(functools.partial(forward_body, names, group), grid=(rows...  37.6 us
    unnamed x178, local copies, waits for them, and re-layouts  15.9 us
    pallas_call x1, Pallas kernels, head(): pl.pallas_call(functools.partial(head_body, group), grid=(rows // TILE,),...  10 us
    sub x6, other arithmetic, adam_update(): master_new = master - RATE_MATRIX * (direction + WEIGHT_DECAY * master)  8.18 us
    convert_element_type x16, other arithmetic, add(): return (a.astype(F32) + b.astype(F32)).astype(BF)  7.23 us
  transfers between devices with their start and end apart: 49, of which 25 were waited for; matrix products, arithmetic and copies ran while one was open for 16% of the time, Pallas kernels for 24%

profile of v4, /device:TPU:0, one launch (start us, length us, event | category | flops | bytes accessed | tf_op | source)
XLA Modules:
  0.0 337.2 jit_solution(16727788875189834115)
XLA Ops:
  3.4 4.1 %collective-permute-start = (bf16[1,48,1280]{2,1,0:T(8,128)(2,1)S(1)}, bf16[1,48,1280]{2,1,0:T(8,128)(2,1)S(1)}, u32[]{:S(2)}, u32[]{:S(2)}) collective-permute-start(bf16[1,48,1280]{2,1,0:T(8,128)(2,1)S(1)} %fusion.17), channel_id=1, source_target_pairs={{0,16},{1,17},{2,18},{3,19},{4,20},{5,21},{6,22},{7,23},{8,24},{9,... | collective-permute-start | bytes 368648 | tf_op jit(solution)/shard_map/ppermute | solution.py:679
  7.7 5.7 %collective-permute-done = bf16[1,48,1280]{2,1,0:T(8,128)(2,1)S(1)} collective-permute-done((bf16[1,48,1280]{2,1,0:T(8,128)(2,1)S(1)}, bf16[1,48,1280]{2,1,0:T(8,128)(2,1)S(1)}, u32[]{:S(2)}, u32[]{:S(2)}) %collective-permute-start) | collective-permute-done | bytes 122912 | tf_op jit(solution)/shard_map/ppermute | solution.py:679
  18.8 3.3 collective-permute-done.1
  27.0 3.3 collective-permute-start.2
  31.3 8.9 %collective-permute-done.2 = bf16[1,48,2432]{2,1,0:T(8,128)(2,1)S(1)} collective-permute-done((bf16[1,48,2432]{2,1,0:T(8,128)(2,1)S(1)}, bf16[1,48,2432]{2,1,0:T(8,128)(2,1)S(1)}, u32[]{:S(2)}, u32[]{:S(2)}) %collective-permute-start.2) | collective-permute-done | bytes 233504 | tf_op jit(solution)/shard_map/ppermute | solution.py:679
  43.3 5.3 %collective-permute-done.7 = bf16[2,48,1280]{2,1,0:T(8,128)(2,1)S(1)} collective-permute-done((bf16[2,48,1280]{2,1,0:T(8,128)(2,1)S(1)}, bf16[2,48,1280]{2,1,0:T(8,128)(2,1)S(1)}, u32[]{:S(2)}, u32[]{:S(2)}) %collective-permute-start.7) | collective-permute-done | bytes 245792 | tf_op jit(solution)/shard_map/ppermute | solution.py:679
  51.0 3.4 %collective-permute-start.3 = (bf16[1,48,1536]{2,1,0:T(8,128)(2,1)S(1)}, bf16[1,48,1536]{2,1,0:T(8,128)(2,1)}, u32[]{:S(2)}, u32[]{:S(2)}) collective-permute-start(bf16[1,48,1536]{2,1,0:T(8,128)(2,1)S(1)} %maximum_select_fusion.1), channel_id=1, source_target_pairs={{0,16},{1,17},{2,18},{3,19},{4,20},{5,21},{6,22},{7,23},{8,24},{9,... | collective-permute-start | bytes 442376 | tf_op jit(solution)/shard_map/ppermute | solution.py:679
  64.1 12.3 %shard_map.493 = (f32[1024,384]{1,0:T(8,128)}, f32[8,384]{1,0:T(8,128)S(1)}, bf16[1024,1152]{1,0:T(8,128)(2,1)}, bf16[1024,384]{1,0:T(8,128)(2,1)S(1)}, bf16[102...) custom-call(bf16[1024,256]{1,0:T(8,128)(2,1)S(1)} %concatenate.184.refs_0_.refs_5, ...), custom_call_target="tpu_custom_call" | custom-call | flops 3825205248 | bytes 44826624 | tf_op jit(solution)/shard_map/pallas_call | solution.py:382
  85.4 12.6 %shard_map.494 = (bf16[1024,1152]{1,0:T(8,128)(2,1)}, bf16[1024,384]{1,0:T(8,128)(2,1)S(1)}, bf16[1024,384]{1,0:T(8,128)(2,1)S(1)}, f32[1024,384]{1,0:T(8,128)S(...) custom-call(f32[1024,384]{1,0:T(8,128)} %get-tuple-element.175.refs_0_.refs_1_, bf16[8,48,2432]{2,1,0:T(8,128)(2,1)} %copy-done.29, ...), custom_call_target="tpu_custom_call" | custom-call | flops 3623878656 | bytes 42467328 | tf_op jit(solution)/shard_map/pallas_call | solution.py:382
  103.2 4.7 %collective-permute-done.17 = bf16[2,48,1536]{2,1,0:T(8,128)(2,1)S(1)} collective-permute-done((bf16[2,48,1536]{2,1,0:T(8,128)(2,1)S(1)}, bf16[2,48,1536]{2,1,0:T(8,128)(2,1)S(1)}, u32[]{:S(2)}, u32[]{:S(2)}) %collective-permute-start.17) | collective-permute-done | bytes 294944 | tf_op jit(solution)/shard_map/ppermute | solution.py:679
  113.7 12.7 %shard_map.495 = (bf16[1024,1152]{1,0:T(8,128)(2,1)}, bf16[1024,384]{1,0:T(8,128)(2,1)S(1)}, bf16[1024,384]{1,0:T(8,128)(2,1)S(1)}, f32[1024,384]{1,0:T(8,128)},...) custom-call(f32[1024,384]{1,0:T(8,128)} %get-tuple-element.182.refs_0_.refs_1_, ...), custom_call_target="tpu_custom_call" | custom-call | flops 3623878656 | bytes 42467328 | tf_op jit(solution)/shard_map/pallas_call | solution.py:382
  128.4 10.0 %shard_map.496 = (f32[1024,384]{1,0:T(8,128)S(1)}, bf16[384,1152]{1,0:T(8,128)(2,1)S(1)}, f32[8,384]{1,0:T(8,128)S(1)}, f32[8,128]{1,0:T(8,128)S(1)}) custom-call(f32[1024,384]{1,0:T(8,128)S(1)} %copy-done.11, f32[1024,128]{1,0:T(8,128)S(1)} %copy-done.9, f32[1024,128]{1,0:T(8,128)S(1)} %fusion.3.mask_ref, ...), custom_call_target="tpu_custom_call" | custom-call | flops 2717908992 | bytes 8388608 | tf_op jit(solution)/shard_map/pallas_call | solution.py:451
  140.6 26.7 %shard_map.497 = (f32[1024,384]{1,0:T(8,128)}, bf16[8,48,2944]{2,1,0:T(8,128)(2,1)}, bf16[8,48,2944]{2,1,0:T(8,128)(2,1)}, f32[8,384]{1,0:T(8,128)}, f32[48,128]{1,0:T(8,128)}, /*index=5*/f32[8,384]{1,0:T(8,128)}) custom-call(f32[1024,384]{1,0:T(8,128)} %copy-done.10, f32[1024,384]{1,0:T(8,128)} %get-tuple-element.182.refs_0_.refs_1_, ...), custom_call_target="tpu_custom_call" | custom-call | flops 7247757312 | bytes 84934656 | tf_op jit(solution)/shard_map/pallas_call | solution.py:647
  167.6 4.4 %collective-permute-done.20 = bf16[8,48,2944]{2,1,0:T(8,128)(2,1)S(1)} collective-permute-done((bf16[8,48,2944]{2,1,0:T(8,128)(2,1)}, bf16[8,48,2944]{2,1,0:T(8,128)(2,1)S(1)}, u32[]{:S(2)}, u32[]{:S(2)}) %collective-permute-start.20) | collective-permute-done | bytes 2261024 | tf_op jit(solution)/shard_map/ppermute | solution.py:679
  175.2 25.9 %shard_map.498 = (f32[1024,384]{1,0:T(8,128)}, bf16[8,48,2432]{2,1,0:T(8,128)(2,1)}, bf16[8,48,2432]{2,1,0:T(8,128)(2,1)}, f32[8,384]{1,0:T(8,128)}, f32[48,128]{1,0:T(8,128)}, /*index=5*/f32[8,384]{1,0:T(8,128)}) custom-call(f32[1024,384]{1,0:T(8,128)} %get-tuple-element.203.refs_0_, f32[1024,384]{1,0:T(8,128)} %get-tuple-element.175.refs_0_.refs_1_, ...), custom_call_target="tpu_custom_call" | custom-call | flops 7247757312 | bytes 84934656 | tf_op jit(solution)/shard_map/pallas_call | solution.py:647
  209.4 15.2 %shard_map.499 = (f32[1024,384]{1,0:T(8,128)}, bf16[8,48,1664]{2,1,0:T(8,128)(2,1)}, bf16[8,48,1664]{2,1,0:T(8,128)(2,1)}, f32[8,384]{1,0:T(8,128)}) custom-call(f32[1024,384]{1,0:T(8,128)} %get-tuple-element.219.refs_0_, f32[1024,384]{1,0:T(8,128)} %get-tuple-element.220.refs_1_, bf16[1024,2048]{1,0:T(8,128)(2,1)} %get-tuple-element.221.refs_2_, ...), custom_call_target="tpu_custom_call" | custom-call | flops 4831838208 | bytes 56623104 | tf_op jit(solution)/shard_map/pallas_call | solution.py:647
  224.6 4.7 %collective-permute-done.23 = bf16[4,48,2432]{2,1,0:T(8,128)(2,1)S(1)} collective-permute-done((bf16[4,48,2432]{2,1,0:T(8,128)(2,1)S(1)}, bf16[4,48,2432]{2,1,0:T(8,128)(2,1)S(1)}, u32[]{:S(2)}, u32[]{:S(2)}) %collective-permute-start.23) | collective-permute-done | bytes 933920 | tf_op jit(solution)/shard_map/ppermute | solution.py:679
  237.5 15.5 %shard_map.500 = (bf16[8,48,896]{2,1,0:T(8,128)(2,1)}, bf16[8,48,896]{2,1,0:T(8,128)(2,1)}, f32[8,384]{1,0:T(8,128)}, f32[48,128]{1,0:T(8,128)}) custom-call(f32[1024,384]{1,0:T(8,128)} %get-tuple-element.233.refs_0_, f32[1024,384]{1,0:T(8,128)} %get-tuple-element.234.refs_1_, bf16[1024,1152]{1,0:T(8,128)(2,1)} %get-tuple-element.235.refs_2_, ...), custom_call_target="tpu_custom_call" | custom-call | flops 2818572288 | bytes 33030144 | tf_op jit(solution)/shard_map/pallas_call | solution.py:647
  270.6 3.4 collective-permute-done.31
  278.7 4.1 %collective-permute-done.34 = bf16[1,48,1664]{2,1,0:T(8,128)(2,1)S(1)} collective-permute-done((bf16[1,48,1664]{2,1,0:T(8,128)(2,1)S(1)}, bf16[1,48,1664]{2,1,0:T(8,128)(2,1)S(1)}, u32[]{:S(2)}, u32[]{:S(2)}) %collective-permute-start.34) | collective-permute-done | bytes 159776 | tf_op jit(solution)/shard_map/ppermute | solution.py:679
  282.8 3.5 %collective-permute-done.33 = bf16[2,48,896]{2,1,0:T(8,128)(2,1)S(1)} collective-permute-done((bf16[2,48,896]{2,1,0:T(8,128)(2,1)S(1)}, bf16[2,48,896]{2,1,0:T(8,128)(2,1)S(1)}, u32[]{:S(2)}, u32[]{:S(2)}) %collective-permute-start.33) | collective-permute-done | bytes 172064 | tf_op jit(solution)/shard_map/ppermute | solution.py:679
  288.6 5.2 %collective-permute-done.35 = bf16[1,48,896]{2,1,0:T(8,128)(2,1)S(1)} collective-permute-done((bf16[1,48,896]{2,1,0:T(8,128)(2,1)S(1)}, bf16[1,48,896]{2,1,0:T(8,128)(2,1)S(1)}, u32[]{:S(2)}, u32[]{:S(2)}) %collective-permute-start.35) | collective-permute-done | bytes 86048 | tf_op jit(solution)/shard_map/ppermute | solution.py:679
  307.0 4.6 %collective-permute-done.42 = f32[8,384]{1,0:T(8,128)S(1)} collective-permute-done((f32[8,384]{1,0:T(8,128)S(1)}, f32[8,384]{1,0:T(8,128)S(1)}, u32[]{:S(2)}, u32[]{:S(2)}) %collective-permute-start.42) | collective-permute-done | bytes 12320 | tf_op jit(solution)/shard_map/ppermute | solution.py:679
  311.6 3.7 %collective-permute-done.43 = f32[8,384]{1,0:T(8,128)S(1)} collective-permute-done((f32[8,384]{1,0:T(8,128)S(1)}, f32[8,384]{1,0:T(8,128)S(1)}, u32[]{:S(2)}, u32[]{:S(2)}) %collective-permute-start.43) | collective-permute-done | bytes 12320 | tf_op jit(solution)/shard_map/ppermute | solution.py:679
  (440 shorter events, 125.2 us)
Async XLA Ops:
  22.2 18.8 %collective-permute-start.6 = (bf16[4,48,1280]{2,1,0:T(8,128)(2,1)S(1)}, bf16[4,48,1280]{2,1,0:T(8,128)(2,1)S(1)}, u32[]{:S(2)}, u32[]{:S(2)}) collective-permute-start(bf16[4,48,1280]{2,1,0:T(8,128)(2,1)S(1)} %pad_maximum_fusion.7), channel_id=1, source_target_pairs={{0,2},{1,3},{2,0},{3,1},{4,6},{5,7},{6,4},{7,5},{8,10},{9,11},{10,... | collective-permute-start | bytes 1474568 | tf_op jit(solution)/shard_map/ppermute | solution.py:679
  23.5 18.1 %collective-permute-start.4 = (bf16[4,48,1280]{2,1,0:T(8,128)(2,1)S(1)}, bf16[4,48,1280]{2,1,0:T(8,128)(2,1)S(1)}, u32[]{:S(2)}, u32[]{:S(2)}) collective-permute-start(bf16[4,48,1280]{2,1,0:T(8,128)(2,1)S(1)} %pad_maximum_fusion.7), channel_id=1, source_target_pairs={{0,4},{1,5},{2,6},{3,7},{4,0},{5,1},{6,2},{7,3},{8,12},{9,13},{10,... | collective-permute-start | bytes 1474568 | tf_op jit(solution)/shard_map/ppermute | solution.py:679
  27.0 13.1 %collective-permute-start.2 = (bf16[1,48,2432]{2,1,0:T(8,128)(2,1)S(1)}, bf16[1,48,2432]{2,1,0:T(8,128)(2,1)S(1)}, u32[]{:S(2)}, u32[]{:S(2)}) collective-permute-start(bf16[1,48,2432]{2,1,0:T(8,128)(2,1)S(1)} %maximum_select_fusion), channel_id=1, source_target_pairs={{0,16},{1,17},{2,18},{3,19},{4,20},{5,21},{6,22},{7,23},{8,24},{9,... | collective-permute-start | bytes 700424 | tf_op jit(solution)/shard_map/ppermute | solution.py:679
  40.2 14.1 %collective-permute-start.10 = (bf16[2,48,2432]{2,1,0:T(8,128)(2,1)S(1)}, bf16[2,48,2432]{2,1,0:T(8,128)(2,1)S(1)}, u32[]{:S(2)}, u32[]{:S(2)}) collective-permute-start(bf16[2,48,2432]{2,1,0:T(8,128)(2,1)S(1)} %pad_maximum_fusion.8), channel_id=1, source_target_pairs={{0,8},{1,9},{2,10},{3,11},{4,12},{5,13},{6,14},{7,15},{8,0},{9,1},... | collective-permute-start | bytes 1400840 | tf_op jit(solution)/shard_map/ppermute | solution.py:679
  42.3 21.8 %collective-permute-start.5 = (bf16[8,48,1280]{2,1,0:T(8,128)(2,1)S(1)}, bf16[8,48,1280]{2,1,0:T(8,128)(2,1)}, u32[]{:S(2)}, u32[]{:S(2)}) collective-permute-start(bf16[8,48,1280]{2,1,0:T(8,128)(2,1)S(1)} %pad_maximum_fusion.1.refs_1_.refs_3_.refs_6_), channel_id=1, source_target_pairs={{0,1},{1,0},{2,3},{3,2},{4,5},{5,4},{6,7},{7,6},{8,9},{9,8},{10,11... | collective-permute-start | bytes 2949128 | tf_op jit(solution)/shard_map/ppermute | solution.py:679
  50.0 14.0 %collective-permute-start.9 = (bf16[8,48,1280]{2,1,0:T(8,128)(2,1)}, bf16[8,48,1280]{2,1,0:T(8,128)(2,1)}, u32[]{:S(2)}, u32[]{:S(2)}) collective-permute-start(bf16[8,48,1280]{2,1,0:T(8,128)(2,1)} %constant_dynamic-update-slice_fusion.1.refs_3_.refs_5_.refs_8_), channel_id=1, source_target_pairs={{0,1},{1,0},{2,3},{3,2},{4,5},{5,4},{6,7},{7,6},{8,9},{9,8},{10,11... | collective-permute-start | bytes 2949128 | tf_op jit(solution)/shard_map/ppermute | solution.py:679
  51.0 11.6 %collective-permute-start.3 = (bf16[1,48,1536]{2,1,0:T(8,128)(2,1)S(1)}, bf16[1,48,1536]{2,1,0:T(8,128)(2,1)}, u32[]{:S(2)}, u32[]{:S(2)}) collective-permute-start(bf16[1,48,1536]{2,1,0:T(8,128)(2,1)S(1)} %maximum_select_fusion.1), channel_id=1, source_target_pairs={{0,16},{1,17},{2,18},{3,19},{4,20},{5,21},{6,22},{7,23},{8,24},{9,... | collective-permute-start | bytes 442376 | tf_op jit(solution)/shard_map/ppermute | solution.py:679
  55.4 23.1 %collective-permute-start.11 = (bf16[4,48,2432]{2,1,0:T(8,128)(2,1)}, bf16[4,48,2432]{2,1,0:T(8,128)(2,1)}, u32[]{:S(2)}, u32[]{:S(2)}) collective-permute-start(bf16[4,48,2432]{2,1,0:T(8,128)(2,1)} %pad_maximum_fusion.2), channel_id=1, source_target_pairs={{0,4},{1,5},{2,6},{3,7},{4,0},{5,1},{6,2},{7,3},{8,12},{9,13},{10,... | collective-permute-start | bytes 2801672 | tf_op jit(solution)/shard_map/ppermute | solution.py:679
  63.7 14.9 %collective-permute-start.12 = (bf16[2,48,1536]{2,1,0:T(8,128)(2,1)S(1)}, bf16[2,48,1536]{2,1,0:T(8,128)(2,1)S(1)}, u32[]{:S(2)}, u32[]{:S(2)}) collective-permute-start(bf16[2,48,1536]{2,1,0:T(8,128)(2,1)S(1)} %pad_maximum_fusion.10), channel_id=1, source_target_pairs={{0,8},{1,9},{2,10},{3,11},{4,12},{5,13},{6,14},{7,15},{8,0},{9,1},... | collective-permute-start | bytes 884744 | tf_op jit(solution)/shard_map/ppermute | solution.py:679
  81.7 17.1 %collective-permute-start.14 = (bf16[4,48,1536]{2,1,0:T(8,128)(2,1)S(1)}, bf16[4,48,1536]{2,1,0:T(8,128)(2,1)S(1)}, u32[]{:S(2)}, u32[]{:S(2)}) collective-permute-start(bf16[4,48,1536]{2,1,0:T(8,128)(2,1)S(1)} %get-tuple-element.352), channel_id=1, source_target_pairs={{0,4},{1,5},{2,6},{3,7},{4,0},{5,1},{6,2},{7,3},{8,12},{9,13},{10,... | collective-permute-start | bytes 1769480 | tf_op jit(solution)/shard_map/ppermute | solution.py:679
  82.9 16.0 %collective-permute-start.15 = (bf16[4,48,1536]{2,1,0:T(8,128)(2,1)S(1)}, bf16[4,48,1536]{2,1,0:T(8,128)(2,1)S(1)}, u32[]{:S(2)}, u32[]{:S(2)}) collective-permute-start(bf16[4,48,1536]{2,1,0:T(8,128)(2,1)S(1)} %get-tuple-element.352), channel_id=1, source_target_pairs={{0,2},{1,3},{2,0},{3,1},{4,6},{5,7},{6,4},{7,5},{8,10},{9,11},{10,... | collective-permute-start | bytes 1769480 | tf_op jit(solution)/shard_map/ppermute | solution.py:679
  174.2 27.1 %collective-permute-start.21 = (bf16[4,48,2944]{2,1,0:T(8,128)(2,1)S(1)}, bf16[4,48,2944]{2,1,0:T(8,128)(2,1)S(1)}, u32[]{:S(2)}, u32[]{:S(2)}) collective-permute-start(bf16[4,48,2944]{2,1,0:T(8,128)(2,1)S(1)} %get-tuple-element.215), channel_id=1, source_target_pairs={{0,4},{1,5},{2,6},{3,7},{4,0},{5,1},{6,2},{7,3},{8,12},{9,13},{10,... | collective-permute-start | bytes 3391496 | tf_op jit(solution)/shard_map/ppermute | solution.py:679
  206.2 23.2 %collective-permute-start.23 = (bf16[4,48,2432]{2,1,0:T(8,128)(2,1)S(1)}, bf16[4,48,2432]{2,1,0:T(8,128)(2,1)S(1)}, u32[]{:S(2)}, u32[]{:S(2)}) collective-permute-start(bf16[4,48,2432]{2,1,0:T(8,128)(2,1)S(1)} %get-tuple-element.226), channel_id=1, source_target_pairs={{0,4},{1,5},{2,6},{3,7},{4,0},{5,1},{6,2},{7,3},{8,12},{9,13},{10,... | collective-permute-start | bytes 2801672 | tf_op jit(solution)/shard_map/ppermute | solution.py:679
  207.9 16.8 %collective-permute-start.24 = (bf16[2,48,2944]{2,1,0:T(8,128)(2,1)S(1)}, bf16[2,48,2944]{2,1,0:T(8,128)(2,1)S(1)}, u32[]{:S(2)}, u32[]{:S(2)}) collective-permute-start(bf16[2,48,2944]{2,1,0:T(8,128)(2,1)S(1)} %get-tuple-element.227), channel_id=1, source_target_pairs={{0,8},{1,9},{2,10},{3,11},{4,12},{5,13},{6,14},{7,15},{8,0},{9,1},... | collective-permute-start | bytes 1695752 | tf_op jit(solution)/shard_map/ppermute | solution.py:679
  232.9 20.8 %collective-permute-start.26 = (bf16[4,48,1664]{2,1,0:T(8,128)(2,1)S(1)}, bf16[4,48,1664]{2,1,0:T(8,128)(2,1)S(1)}, u32[]{:S(2)}, u32[]{:S(2)}) collective-permute-start(bf16[4,48,1664]{2,1,0:T(8,128)(2,1)S(1)} %get-tuple-element.242), channel_id=1, source_target_pairs={{0,4},{1,5},{2,6},{3,7},{4,0},{5,1},{6,2},{7,3},{8,12},{9,13},{10,... | collective-permute-start | bytes 1916936 | tf_op jit(solution)/shard_map/ppermute | solution.py:679
  235.1 18.6 %collective-permute-start.27 = (bf16[2,48,2432]{2,1,0:T(8,128)(2,1)S(1)}, bf16[2,48,2432]{2,1,0:T(8,128)(2,1)}, u32[]{:S(2)}, u32[]{:S(2)}) collective-permute-start(bf16[2,48,2432]{2,1,0:T(8,128)(2,1)S(1)} %get-tuple-element.243), channel_id=1, source_target_pairs={{0,8},{1,9},{2,10},{3,11},{4,12},{5,13},{6,14},{7,15},{8,0},{9,1},... | collective-permute-start | bytes 1400840 | tf_op jit(solution)/shard_map/ppermute | solution.py:679
  235.9 17.2 %collective-permute-start.28 = (bf16[1,48,2944]{2,1,0:T(8,128)(2,1)}, bf16[1,48,2944]{2,1,0:T(8,128)(2,1)}, u32[]{:S(2)}, u32[]{:S(2)}) collective-permute-start(bf16[1,48,2944]{2,1,0:T(8,128)(2,1)} %get-tuple-element.244), channel_id=1, source_target_pairs={{0,16},{1,17},{2,18},{3,19},{4,20},{5,21},{6,22},{7,23},{8,24},{9,... | collective-permute-start | bytes 847880 | tf_op jit(solution)/shard_map/ppermute | solution.py:679
  256.3 14.1 %collective-permute-start.32 = (bf16[1,48,2432]{2,1,0:T(8,128)(2,1)S(1)}, bf16[1,48,2432]{2,1,0:T(8,128)(2,1)S(1)}, u32[]{:S(2)}, u32[]{:S(2)}) collective-permute-start(bf16[1,48,2432]{2,1,0:T(8,128)(2,1)S(1)} %get-tuple-element.268), channel_id=1, source_target_pairs={{0,16},{1,17},{2,18},{3,19},{4,20},{5,21},{6,22},{7,23},{8,24},{9,... | collective-permute-start | bytes 700424 | tf_op jit(solution)/shard_map/ppermute | solution.py:679
  258.5 15.8 %collective-permute-start.39 = (bf16[1,48,2944]{2,1,0:T(8,128)(2,1)S(1)}, bf16[1,48,2944]{2,1,0:T(8,128)(2,1)S(1)}, u32[]{:S(2)}, u32[]{:S(2)}) collective-permute-start(bf16[1,48,2944]{2,1,0:T(8,128)(2,1)S(1)} %add_convert_fusion.15), channel_id=1, source_target_pairs={{0,2},{1,3},{2,0},{3,1},{4,6},{5,7},{6,4},{7,5},{8,10},{9,11},{10,... | collective-permute-start | bytes 847880 | tf_op jit(solution)/shard_map/ppermute | solution.py:679
  259.7 14.3 %collective-permute-start.31 = (bf16[2,48,1664]{2,1,0:T(8,128)(2,1)S(1)}, bf16[2,48,1664]{2,1,0:T(8,128)(2,1)S(1)}, u32[]{:S(2)}, u32[]{:S(2)}) collective-permute-start(bf16[2,48,1664]{2,1,0:T(8,128)(2,1)S(1)} %get-tuple-element.266), channel_id=1, source_target_pairs={{0,8},{1,9},{2,10},{3,11},{4,12},{5,13},{6,14},{7,15},{8,0},{9,1},... | collective-permute-start | bytes 958472 | tf_op jit(solution)/shard_map/ppermute | solution.py:679
  261.4 12.6 %collective-permute-start.30 = (bf16[4,48,896]{2,1,0:T(8,128)(2,1)S(1)}, bf16[4,48,896]{2,1,0:T(8,128)(2,1)S(1)}, u32[]{:S(2)}, u32[]{:S(2)}) collective-permute-start(bf16[4,48,896]{2,1,0:T(8,128)(2,1)S(1)} %get-tuple-element.264), channel_id=1, source_target_pairs={{0,4},{1,5},{2,6},{3,7},{4,0},{5,1},{6,2},{7,3},{8,12},{9,13},{10,... | collective-permute-start | bytes 1032200 | tf_op jit(solution)/shard_map/ppermute | solution.py:679
  275.5 26.4 %collective-permute-start.47 = (bf16[48,2944]{1,0:T(8,128)(2,1)S(1)}, bf16[48,2944]{1,0:T(8,128)(2,1)S(1)}, u32[]{:S(2)}, u32[]{:S(2)}) collective-permute-start(bf16[48,2944]{1,0:T(8,128)(2,1)S(1)} %get-tuple-element.310), channel_id=1, source_target_pairs={{0,1},{1,0},{2,3},{3,2},{4,5},{5,4},{6,7},{7,6},{8,9},{9,8},{10,11... | collective-permute-start | bytes 847880 | tf_op jit(solution)/shard_map/ppermute | solution.py:679
  275.6 12.0 %collective-permute-start.38 = (bf16[1,48,2432]{2,1,0:T(8,128)(2,1)S(1)}, bf16[1,48,2432]{2,1,0:T(8,128)(2,1)S(1)}, u32[]{:S(2)}, u32[]{:S(2)}) collective-permute-start(bf16[1,48,2432]{2,1,0:T(8,128)(2,1)S(1)} %add_convert_fusion.19), channel_id=1, source_target_pairs={{0,2},{1,3},{2,0},{3,1},{4,6},{5,7},{6,4},{7,5},{8,10},{9,11},{10,... | collective-permute-start | bytes 700424 | tf_op jit(solution)/shard_map/ppermute | solution.py:679
  316.4 12.7 %collective-permute-start.48 = (bf16[48,1664]{1,0:T(8,128)(2,1)S(1)}, bf16[48,1664]{1,0:T(8,128)(2,1)S(1)}, u32[]{:S(2)}, u32[]{:S(2)}) collective-permute-start(bf16[48,1664]{1,0:T(8,128)(2,1)S(1)} %get-tuple-element.314), channel_id=1, source_target_pairs={{0,1},{1,0},{2,3},{3,2},{4,5},{5,4},{6,7},{7,6},{8,9},{9,8},{10,11... | collective-permute-start | bytes 479240 | tf_op jit(solution)/shard_map/ppermute | solution.py:679
  (109 other events, 1106.1 us)

commit v5 on v4

--- a/solution.py
+++ b/solution.py
@@ -151,14 +151,15 @@
 
 
     def squares(self, own):
+        own, core = lax.optimization_barrier((own, lax.axis_index("dp") & 1))
         row = lax.broadcasted_iota(jnp.int32, own.shape, 0)
-        col = lax.broadcasted_iota(jnp.int32, own.shape, 1)
-        used = [jnp.zeros(own.shape, bool)] * 2
+        col = lax.broadcasted_iota(jnp.int32, own.shape, 1) + core * self.width
+        used = col < sum(width for _, width in self.fields)
         for part, at, name, _, width in self.pieces:
-            inside = (col >= at) & (col < at + width) & (row < self.row_span(name)[1])
-            used[part] = used[part] | inside
-        core = lax.axis_index("dp") & 1
-        used = (used[0] & (core == 0)) | (used[1] & (core == 1))
+            count = self.row_span(name)[1]
+            if count < self.rows:
+                start = part * self.width + at
+                used = used & ((row < count) | (col < start) | (col >= start + width))
         return jnp.sum(jnp.where(used, jnp.square(own.astype(F32)), 0.0)).reshape(1, 1)
 
 
@@ -875,13 +876,79 @@
     return (master_new, first_new, second_new)
 
 
-def sum_moves(sizes, dp_from=1):
-    moves = []
-    dp_mask = dp_from
-    while dp_mask < sizes[1]:
+def beside(x, sizes, across):
+    moves = [(mask, 0) for mask in masks_of(sizes[0])]
+    if across:
+        moves = []
+    dp_mask = 2 if across else 1
+    while dp_mask < (sizes[1] if across else 2):
         moves.append((0, dp_mask))
         dp_mask *= 2
-    return moves + [(mask, 0) for mask in masks_of(sizes[0])]
+    for fsdp_mask, dp_mask in moves:
+        x = x + swap(x, sizes, fsdp_mask, dp_mask)
+    return x
+
+
+STACKED = ("qkv", "o", "gu", "d")
+
+
+def update_body(groups, layers, *refs):
+    take = Taker(refs)
+    scale_ref = take()
+    parts = [take(group.parts) for group in groups]
+    names = STACKED + ("head",)
+    states = [take.named(names) for _ in range(3)]
+    fresh = [take.named(names) for _ in range(3)]
+    scale = scale_ref[0, 0]
+
+    def one(name, index, grad):
+        old = [state[name][index] for state in states]
+        new = adam_update(old[0], grad.astype(F32) * scale, old[1], old[2], True)
+        for target, value in zip(fresh, new):
+            target[name][index] = value
+
+    def layer_step(layer, place_here):
+        for group, group_parts, at_layer in zip(groups, parts, layers):
+            if at_layer != layer:
+                continue
+            for part, at, name, start, width in group.pieces:
+                if name == "in":
+                    continue
+                first, count, _ = group.row_span(name)
+                grad = group_parts[part ^ place_here][0:count, at : at + width]
+                cols = slice(start, start + width)
+                if name == "head":
+                    one("head", (slice(0, count), cols), grad)
+                else:
+                    rows = slice(first, first + count) if name[0] == "d" else slice(0, count)
+                    one(name[0] if name[0] == "d" else name, (0, rows, cols), grad)
+
+    core = lax.axis_index("dp") & 1
+    for layer in range(L):
+        for which in range(2):
+            chosen = (pl.program_id(0) == layer) & (core == which)
+            pl.when(chosen)(functools.partial(layer_step, layer, which))
+
+
+def update(groups, layers, parts, scale, states):
+    def spec(x):
+        if x.ndim == 2:
+            return whole_spec(x.shape)
+        return pl.BlockSpec((1,) + x.shape[1:], lambda i: (i, 0, 0))
+
+    flat = [x for state in states for x in state]
+    got = pl.pallas_call(
+        functools.partial(update_body, groups, layers),
+        grid=(L,),
+        in_specs=[pl.BlockSpec(memory_space=pltpu.SMEM)]
+        + [whole_spec(p.shape) for pair in parts for p in pair]
+        + [spec(x) for x in flat],
+        out_specs=[spec(x) for x in flat],
+        out_shape=[jax.ShapeDtypeStruct(x.shape, F32) for x in flat],
+        compiler_params=params(60),
+        cost_estimate=pl.CostEstimate(flops=1 << 24, bytes_accessed=18 << 20, transcendentals=0),
+    )(scale.reshape(1, 1), *[p for pair in parts for p in pair], *flat)
+    return [got[i : i + len(states[0])] for i in range(0, len(flat), len(states[0]))]
 
 
 def per_device(sizes, *args):
@@ -1041,6 +1108,7 @@
     small = jnp.concatenate([jnp.sum(loss)[None], live[None], bias_grads.reshape(-1)])
     small = jnp.pad(small, (0, D - small.shape[0]))
     rows = jnp.stack(gain_grads + [small])
+    rows = beside(rows, sizes, across=True)
     pending = list(zip(range(count), totals))
     own_parts = [None] * count
     first = True
@@ -1055,12 +1123,10 @@
             hold((), *[one for _, one in pending])
         first = False
     squares = jnp.zeros((1, 1), F32)
-    for n in range(count):
-        squares = squares + groups[n].squares(own_parts[n])
-    rows = rows + jnp.pad(squares, ((NGAIN, 0), (D - 1, 0)))
-    for fsdp_mask, dp_mask in sum_moves(sizes):
-        rows = rows + swap(rows, sizes, fsdp_mask, dp_mask)
-    squares = rows[NGAIN, D - 1] / (sizes[1] // 2)
+    for n, part in enumerate(own_parts):
+        squares = squares + groups[n].squares(part)
+    rows = beside(rows + jnp.pad(squares, ((NGAIN, 0), (D - 1, 0))), sizes, across=False)
+    squares = rows[NGAIN, D - 1]
     loss_sum, total_count = rows[NGAIN, 0], rows[NGAIN, 1]
     inverse_count = 1.0 / total_count
     bias_grad = rows[NGAIN, 2 : 2 + var_bias.size].reshape(var_bias.shape) * inverse_count
@@ -1071,22 +1137,27 @@
     gain_all = rows[:NGAIN]
     gain_own = lax.dynamic_slice_in_dim(gain_all, lax.axis_index("fsdp") * own, own, axis=1)
 
-    pieces = []
-    for n in range(count):
-        low, high = by_core(own_parts[n], swap(own_parts[n], sizes, 0, 1))
-        pieces.append(groups[n].unpack((low, high)))
-    in_piece = pieces[0]["in"][:, :IN_CAT]
-    head_piece = pieces[-1]["head"]
-    matrices = [[piece[m] for piece in pieces if m in piece] for m in ("qkv", "o", "gu", "d")]
     grad_norm = jnp.sqrt(squares) * inverse_count
     factor = jnp.minimum(1.0, CLIP_NORM / grad_norm)
     scale = factor * inverse_count
 
-    gradients = [in_piece.T] + [jnp.stack(m) for m in matrices] + [head_piece, gain_own]
+
+    pairs = [(part, swap(part, sizes, 0, 1)) for part in own_parts]
+    whole_parts = [by_core(*pair) for pair in pairs]
+    fresh = [None] * 8
+    if direct:
+        states = [[group_of[m] for m in (1, 2, 3, 4, 5)] for group_of in (masters, firsts, seconds)]
+        new = update(groups, layers, pairs, scale, states)
+        for at, m in enumerate((1, 2, 3, 4, 5)):
+            fresh[m] = tuple(kind[at] for kind in new)
+    pieces = [groups[n].unpack(whole_parts[n]) for n in range(count)]
+    matrices = [[piece[m] for piece in pieces if m in piece] for m in STACKED]
+    gradients = [pieces[0]["in"][:, :IN_CAT].T] + [jnp.stack(m) for m in matrices]
+    gradients += [pieces[-1]["head"], gain_own]
     clipped = [g.astype(F32) * scale for g in gradients] + [bias_grad * factor]
-    fresh = [
-        adam_update(masters[m], clipped[m], firsts[m], seconds[m], m < 6) for m in range(8)
-    ]
+    for m in range(8):
+        if fresh[m] is None:
+            fresh[m] = adam_update(masters[m], clipped[m], firsts[m], seconds[m], m < 6)
     return (
         (loss_sum, total_count, grad_norm)
         + tuple(f[0] for f in fresh)

time: 343 us -> 334 us (0.974)
  other arithmetic: 50.3 us -> 30.1 us
  Pallas kernels: 131 us -> 141 us
  waiting for transfers between devices: 80.2 us -> 87.2 us
  local copies, waits for them, and re-layouts: 25.8 us -> 21.7 us
    pallas_call x0 -> x1, Pallas kernels: none -> 9.81 us  [update(): pl.pallas_call(functools.partial(update_body, groups, layers), grid=(L,),...]
    sub x6 -> x1, other arithmetic: 8.18 us -> 0.72 us  [adam_update(): master_new = master - RATE_MATRIX * (direction + WEIGHT_DECAY * master)]
    ppermute x49, waiting for transfers between devices: 80.2 us -> 87.2 us  [swap(): return lax.ppermute(x, AXES, partners(sizes, fsdp_mask, dp_mask))]
    unnamed x178 -> x136, local copies, waits for them, and re-layouts: 15.9 us -> 12.1 us
    and x8 -> x0, other arithmetic: 3.56 us -> none  [squares(): inside = (col >= at) & (col < at + width) & (row < self.row_span(name)[1])]
    reduce_sum x7, other arithmetic: 3.66 us -> 0.13 us  [per_device(): gain_grads = [jnp.sum(gain_grads[g], axis=0) for g in range(NGAIN)]]
  transfers between devices with their start and end apart: 49 -> 49, of which waited for: 25 -> 25; matrix products, arithmetic and copies ran while one was open for 16% -> 11% of each run, Pallas kernels for 24% -> 25%
where the time goes in v5:
time: 334 us; the launch traced here: 329 us
  Pallas kernels  141 us (42%)
  waiting for transfers between devices  87.2 us (26%)
  starting transfers between devices  40.4 us (12%)
  other arithmetic  30.1 us (9%)
  local copies, waits for them, and re-layouts  21.7 us (6%)
  between operations  8.35 us (2%)
    ppermute x49, waiting for transfers between devices, swap(): return lax.ppermute(x, AXES, partners(sizes, fsdp_mask, dp_mask))  87.2 us
    pallas_call x4, Pallas kernels, backward_layer(): pl.pallas_call(functools.partial(backward_body, names, extra[0] if extra...  83.1 us
    ppermute x49, starting transfers between devices, swap(): return lax.ppermute(x, AXES, partners(sizes, fsdp_mask, dp_mask))  40.4 us
    pallas_call x3, Pallas kernels, forward_layer(): pl.pallas_call(functools.partial(forward_body, names, group), grid=(rows...  37.8 us
    unnamed x136, local copies, waits for them, and re-layouts  12.1 us
    pallas_call x1, Pallas kernels, head(): pl.pallas_call(functools.partial(head_body, group), grid=(rows // TILE,),...  10 us
    pallas_call x1, Pallas kernels, update(): pl.pallas_call(functools.partial(update_body, groups, layers), grid=(L,),...  9.81 us
  transfers between devices with their start and end apart: 49, of which 25 were waited for; matrix products, arithmetic and copies ran while one was open for 11% of the time, Pallas kernels for 25%

profile of v5, /device:TPU:0, one launch (start us, length us, event | category | flops | bytes accessed | tf_op | source)
XLA Modules:
  0.0 328.6 jit_solution(16570550028721739807)
XLA Ops:
  4.7 4.1 %collective-permute-start = (bf16[1,48,1280]{2,1,0:T(8,128)(2,1)S(1)}, bf16[1,48,1280]{2,1,0:T(8,128)(2,1)S(1)}, u32[]{:S(2)}, u32[]{:S(2)}) collective-permute-start(bf16[1,48,1280]{2,1,0:T(8,128)(2,1)S(1)} %fusion.12), channel_id=1, source_target_pairs={{0,16},{1,17},{2,18},{3,19},{4,20},{5,21},{6,22},{7,23},{8,24},{9,... | collective-permute-start | bytes 368648 | tf_op jit(solution)/shard_map/ppermute | solution.py:680
  9.1 5.7 %collective-permute-done = bf16[1,48,1280]{2,1,0:T(8,128)(2,1)S(1)} collective-permute-done((bf16[1,48,1280]{2,1,0:T(8,128)(2,1)S(1)}, bf16[1,48,1280]{2,1,0:T(8,128)(2,1)S(1)}, u32[]{:S(2)}, u32[]{:S(2)}) %collective-permute-start) | collective-permute-done | bytes 122912 | tf_op jit(solution)/shard_map/ppermute | solution.py:680
  26.0 3.4 %collective-permute-start.2 = (bf16[1,48,2432]{2,1,0:T(8,128)(2,1)S(1)}, bf16[1,48,2432]{2,1,0:T(8,128)(2,1)S(1)}, u32[]{:S(2)}, u32[]{:S(2)}) collective-permute-start(bf16[1,48,2432]{2,1,0:T(8,128)(2,1)S(1)} %maximum_select_fusion), channel_id=1, source_target_pairs={{0,16},{1,17},{2,18},{3,19},{4,20},{5,21},{6,22},{7,23},{8,24},{9,... | collective-permute-start | bytes 700424 | tf_op jit(solution)/shard_map/ppermute | solution.py:680
  33.1 6.2 %collective-permute-done.2 = bf16[1,48,2432]{2,1,0:T(8,128)(2,1)S(1)} collective-permute-done((bf16[1,48,2432]{2,1,0:T(8,128)(2,1)S(1)}, bf16[1,48,2432]{2,1,0:T(8,128)(2,1)S(1)}, u32[]{:S(2)}, u32[]{:S(2)}) %collective-permute-start.2) | collective-permute-done | bytes 233504 | tf_op jit(solution)/shard_map/ppermute | solution.py:680
  42.3 5.3 %collective-permute-done.7 = bf16[2,48,1280]{2,1,0:T(8,128)(2,1)S(1)} collective-permute-done((bf16[2,48,1280]{2,1,0:T(8,128)(2,1)S(1)}, bf16[2,48,1280]{2,1,0:T(8,128)(2,1)S(1)}, u32[]{:S(2)}, u32[]{:S(2)}) %collective-permute-start.7) | collective-permute-done | bytes 245792 | tf_op jit(solution)/shard_map/ppermute | solution.py:680
  62.9 12.3 %shard_map.493 = (f32[1024,384]{1,0:T(8,128)}, f32[8,384]{1,0:T(8,128)S(1)}, bf16[1024,1152]{1,0:T(8,128)(2,1)}, bf16[1024,384]{1,0:T(8,128)(2,1)S(1)}, bf16[102...) custom-call(bf16[1024,256]{1,0:T(8,128)(2,1)S(1)} %concatenate.163.refs_0_.refs_5, ...), custom_call_target="tpu_custom_call" | custom-call | flops 3825205248 | bytes 44826624 | tf_op jit(solution)/shard_map/pallas_call | solution.py:383
  84.3 12.6 %shard_map.494 = (bf16[1024,1152]{1,0:T(8,128)(2,1)}, bf16[1024,384]{1,0:T(8,128)(2,1)S(1)}, bf16[1024,384]{1,0:T(8,128)(2,1)S(1)}, f32[1024,384]{1,0:T(8,128)S(...) custom-call(f32[1024,384]{1,0:T(8,128)} %get-tuple-element.198.refs_0_.refs_1_, bf16[8,48,2432]{2,1,0:T(8,128)(2,1)} %copy-done.28, ...), custom_call_target="tpu_custom_call" | custom-call | flops 3623878656 | bytes 42467328 | tf_op jit(solution)/shard_map/pallas_call | solution.py:383
  101.3 4.7 %collective-permute-done.17 = bf16[2,48,1536]{2,1,0:T(8,128)(2,1)S(1)} collective-permute-done((bf16[2,48,1536]{2,1,0:T(8,128)(2,1)S(1)}, bf16[2,48,1536]{2,1,0:T(8,128)(2,1)S(1)}, u32[]{:S(2)}, u32[]{:S(2)}) %collective-permute-start.17) | collective-permute-done | bytes 294944 | tf_op jit(solution)/shard_map/ppermute | solution.py:680
  111.8 13.0 %shard_map.495 = (bf16[1024,1152]{1,0:T(8,128)(2,1)}, bf16[1024,384]{1,0:T(8,128)(2,1)S(1)}, bf16[1024,384]{1,0:T(8,128)(2,1)S(1)}, f32[1024,384]{1,0:T(8,128)},...) custom-call(f32[1024,384]{1,0:T(8,128)} %get-tuple-element.205.refs_0_.refs_1_, ...), custom_call_target="tpu_custom_call" | custom-call | flops 3623878656 | bytes 42467328 | tf_op jit(solution)/shard_map/pallas_call | solution.py:383
  126.8 10.0 %shard_map.496 = (f32[1024,384]{1,0:T(8,128)S(1)}, bf16[384,1152]{1,0:T(8,128)(2,1)S(1)}, f32[8,384]{1,0:T(8,128)S(1)}, f32[8,128]{1,0:T(8,128)S(1)}) custom-call(f32[1024,384]{1,0:T(8,128)S(1)} %copy-done.11, f32[1024,128]{1,0:T(8,128)S(1)} %copy-done.9, f32[1024,128]{1,0:T(8,128)S(1)} %fusion.mask_ref, ...), custom_call_target="tpu_custom_call" | custom-call | flops 2717908992 | bytes 8388608 | tf_op jit(solution)/shard_map/pallas_call | solution.py:452
  138.9 26.7 %shard_map.497 = (f32[1024,384]{1,0:T(8,128)}, bf16[8,48,2944]{2,1,0:T(8,128)(2,1)}, bf16[8,48,2944]{2,1,0:T(8,128)(2,1)}, f32[8,384]{1,0:T(8,128)}, f32[48,128]{1,0:T(8,128)}, /*index=5*/f32[8,384]{1,0:T(8,128)}) custom-call(f32[1024,384]{1,0:T(8,128)} %copy-done.10, f32[1024,384]{1,0:T(8,128)} %get-tuple-element.205.refs_0_.refs_1_, ...), custom_call_target="tpu_custom_call" | custom-call | flops 7247757312 | bytes 84934656 | tf_op jit(solution)/shard_map/pallas_call | solution.py:648
  165.8 4.4 %collective-permute-done.20 = bf16[8,48,2944]{2,1,0:T(8,128)(2,1)S(1)} collective-permute-done((bf16[8,48,2944]{2,1,0:T(8,128)(2,1)}, bf16[8,48,2944]{2,1,0:T(8,128)(2,1)S(1)}, u32[]{:S(2)}, u32[]{:S(2)}) %collective-permute-start.20) | collective-permute-done | bytes 2261024 | tf_op jit(solution)/shard_map/ppermute | solution.py:680
  173.7 25.9 %shard_map.498 = (f32[1024,384]{1,0:T(8,128)}, bf16[8,48,2432]{2,1,0:T(8,128)(2,1)}, bf16[8,48,2432]{2,1,0:T(8,128)(2,1)}, f32[8,384]{1,0:T(8,128)}, f32[48,128]{1,0:T(8,128)}, /*index=5*/f32[8,384]{1,0:T(8,128)}) custom-call(f32[1024,384]{1,0:T(8,128)} %get-tuple-element.226.refs_0_, f32[1024,384]{1,0:T(8,128)} %get-tuple-element.198.refs_0_.refs_1_, ...), custom_call_target="tpu_custom_call" | custom-call | flops 7247757312 | bytes 84934656 | tf_op jit(solution)/shard_map/pallas_call | solution.py:648
  199.9 3.8 %collective-permute-done.22 = bf16[8,48,2432]{2,1,0:T(8,128)(2,1)S(1)} collective-permute-done((bf16[8,48,2432]{2,1,0:T(8,128)(2,1)}, bf16[8,48,2432]{2,1,0:T(8,128)(2,1)S(1)}, u32[]{:S(2)}, u32[]{:S(2)}) %collective-permute-start.22) | collective-permute-done | bytes 1867808 | tf_op jit(solution)/shard_map/ppermute | solution.py:680
  205.6 15.1 %shard_map.499 = (f32[1024,384]{1,0:T(8,128)}, bf16[8,48,1664]{2,1,0:T(8,128)(2,1)}, bf16[8,48,1664]{2,1,0:T(8,128)(2,1)}, f32[8,384]{1,0:T(8,128)}) custom-call(f32[1024,384]{1,0:T(8,128)} %get-tuple-element.242.refs_0_, f32[1024,384]{1,0:T(8,128)} %get-tuple-element.243.refs_1_, bf16[1024,2048]{1,0:T(8,128)(2,1)} %get-tuple-element.244.refs_2_, ...), custom_call_target="tpu_custom_call" | custom-call | flops 4831838208 | bytes 56623104 | tf_op jit(solution)/shard_map/pallas_call | solution.py:648
  220.7 6.2 %collective-permute-done.23 = bf16[4,48,2432]{2,1,0:T(8,128)(2,1)S(1)} collective-permute-done((bf16[4,48,2432]{2,1,0:T(8,128)(2,1)S(1)}, bf16[4,48,2432]{2,1,0:T(8,128)(2,1)S(1)}, u32[]{:S(2)}, u32[]{:S(2)}) %collective-permute-start.23) | collective-permute-done | bytes 933920 | tf_op jit(solution)/shard_map/ppermute | solution.py:680
  232.8 15.5 %shard_map.500 = (bf16[8,48,896]{2,1,0:T(8,128)(2,1)}, bf16[8,48,896]{2,1,0:T(8,128)(2,1)}, f32[8,384]{1,0:T(8,128)}, f32[48,128]{1,0:T(8,128)}) custom-call(f32[1024,384]{1,0:T(8,128)} %get-tuple-element.256.refs_0_, f32[1024,384]{1,0:T(8,128)} %get-tuple-element.257.refs_1_, bf16[1024,1152]{1,0:T(8,128)(2,1)} %get-tuple-element.258.refs_2_, ...), custom_call_target="tpu_custom_call" | custom-call | flops 2818572288 | bytes 33030144 | tf_op jit(solution)/shard_map/pallas_call | solution.py:648
  261.4 4.8 %collective-permute-done.33 = bf16[1,48,2432]{2,1,0:T(8,128)(2,1)S(1)} collective-permute-done((bf16[1,48,2432]{2,1,0:T(8,128)(2,1)S(1)}, bf16[1,48,2432]{2,1,0:T(8,128)(2,1)S(1)}, u32[]{:S(2)}, u32[]{:S(2)}) %collective-permute-start.33) | collective-permute-done | bytes 233504 | tf_op jit(solution)/shard_map/ppermute | solution.py:680
  267.2 5.7 %collective-permute-done.32 = bf16[2,48,1664]{2,1,0:T(8,128)(2,1)S(1)} collective-permute-done((bf16[2,48,1664]{2,1,0:T(8,128)(2,1)S(1)}, bf16[2,48,1664]{2,1,0:T(8,128)(2,1)S(1)}, u32[]{:S(2)}, u32[]{:S(2)}) %collective-permute-start.32) | collective-permute-done | bytes 319520 | tf_op jit(solution)/shard_map/ppermute | solution.py:680
  277.0 5.7 %collective-permute-done.35 = bf16[1,48,1664]{2,1,0:T(8,128)(2,1)S(1)} collective-permute-done((bf16[1,48,1664]{2,1,0:T(8,128)(2,1)S(1)}, bf16[1,48,1664]{2,1,0:T(8,128)(2,1)S(1)}, u32[]{:S(2)}, u32[]{:S(2)}) %collective-permute-start.35) | collective-permute-done | bytes 159776 | tf_op jit(solution)/shard_map/ppermute | solution.py:680
  286.2 3.4 %collective-permute-done.36 = bf16[1,48,896]{2,1,0:T(8,128)(2,1)S(1)} collective-permute-done((bf16[1,48,896]{2,1,0:T(8,128)(2,1)S(1)}, bf16[1,48,896]{2,1,0:T(8,128)(2,1)S(1)}, u32[]{:S(2)}, u32[]{:S(2)}) %collective-permute-start.36) | collective-permute-done | bytes 86048 | tf_op jit(solution)/shard_map/ppermute | solution.py:680
  297.6 4.6 %collective-permute-done.41 = f32[8,384]{1,0:T(8,128)S(1)} collective-permute-done((f32[8,384]{1,0:T(8,128)S(1)}, f32[8,384]{1,0:T(8,128)S(1)}, u32[]{:S(2)}, u32[]{:S(2)}) %collective-permute-start.41) | collective-permute-done | bytes 12320 | tf_op jit(solution)/shard_map/ppermute | solution.py:680
  302.2 3.7 %collective-permute-done.42 = f32[8,384]{1,0:T(8,128)S(1)} collective-permute-done((f32[8,384]{1,0:T(8,128)S(1)}, f32[8,384]{1,0:T(8,128)S(1)}, u32[]{:S(2)}, u32[]{:S(2)}) %collective-permute-start.42) | collective-permute-done | bytes 12320 | tf_op jit(solution)/shard_map/ppermute | solution.py:680
  317.2 9.8 %shard_map.501 = (f32[3,48,1152]{2,1,0:T(8,128)}, f32[3,48,384]{2,1,0:T(8,128)}, f32[3,48,2048]{2,1,0:T(8,128)}, f32[3,128,384]{2,1,0:T(8,128)}, f32[48,1152]{1,...) custom-call(f32[1,1]{1,0:T(1,128)} %bitcast.36.refs_0_, ...), custom_call_target="tpu_custom_call" | custom-call | flops 16777216 | bytes 18874368 | tf_op jit(solution)/shard_map/pallas_call | solution.py:940
  (366 shorter events, 107.7 us)
Async XLA Ops:
  4.7 10.1 %collective-permute-start = (bf16[1,48,1280]{2,1,0:T(8,128)(2,1)S(1)}, bf16[1,48,1280]{2,1,0:T(8,128)(2,1)S(1)}, u32[]{:S(2)}, u32[]{:S(2)}) collective-permute-start(bf16[1,48,1280]{2,1,0:T(8,128)(2,1)S(1)} %fusion.12), channel_id=1, source_target_pairs={{0,16},{1,17},{2,18},{3,19},{4,20},{5,21},{6,22},{7,23},{8,24},{9,... | collective-permute-start | bytes 368648 | tf_op jit(solution)/shard_map/ppermute | solution.py:680
  23.2 16.8 %collective-permute-start.6 = (bf16[4,48,1280]{2,1,0:T(8,128)(2,1)S(1)}, bf16[4,48,1280]{2,1,0:T(8,128)(2,1)S(1)}, u32[]{:S(2)}, u32[]{:S(2)}) collective-permute-start(bf16[4,48,1280]{2,1,0:T(8,128)(2,1)S(1)} %pad_maximum_fusion.6), channel_id=1, source_target_pairs={{0,2},{1,3},{2,0},{3,1},{4,6},{5,7},{6,4},{7,5},{8,10},{9,11},{10,... | collective-permute-start | bytes 1474568 | tf_op jit(solution)/shard_map/ppermute | solution.py:680
  24.5 16.1 %collective-permute-start.4 = (bf16[4,48,1280]{2,1,0:T(8,128)(2,1)S(1)}, bf16[4,48,1280]{2,1,0:T(8,128)(2,1)S(1)}, u32[]{:S(2)}, u32[]{:S(2)}) collective-permute-start(bf16[4,48,1280]{2,1,0:T(8,128)(2,1)S(1)} %pad_maximum_fusion.6), channel_id=1, source_target_pairs={{0,4},{1,5},{2,6},{3,7},{4,0},{5,1},{6,2},{7,3},{8,12},{9,13},{10,... | collective-permute-start | bytes 1474568 | tf_op jit(solution)/shard_map/ppermute | solution.py:680
  26.0 13.2 %collective-permute-start.2 = (bf16[1,48,2432]{2,1,0:T(8,128)(2,1)S(1)}, bf16[1,48,2432]{2,1,0:T(8,128)(2,1)S(1)}, u32[]{:S(2)}, u32[]{:S(2)}) collective-permute-start(bf16[1,48,2432]{2,1,0:T(8,128)(2,1)S(1)} %maximum_select_fusion), channel_id=1, source_target_pairs={{0,16},{1,17},{2,18},{3,19},{4,20},{5,21},{6,22},{7,23},{8,24},{9,... | collective-permute-start | bytes 700424 | tf_op jit(solution)/shard_map/ppermute | solution.py:680
  39.3 14.1 %collective-permute-start.10 = (bf16[2,48,2432]{2,1,0:T(8,128)(2,1)S(1)}, bf16[2,48,2432]{2,1,0:T(8,128)(2,1)S(1)}, u32[]{:S(2)}, u32[]{:S(2)}) collective-permute-start(bf16[2,48,2432]{2,1,0:T(8,128)(2,1)S(1)} %pad_maximum_fusion.7), channel_id=1, source_target_pairs={{0,8},{1,9},{2,10},{3,11},{4,12},{5,13},{6,14},{7,15},{8,0},{9,1},... | collective-permute-start | bytes 1400840 | tf_op jit(solution)/shard_map/ppermute | solution.py:680
  41.4 21.5 %collective-permute-start.5 = (bf16[8,48,1280]{2,1,0:T(8,128)(2,1)S(1)}, bf16[8,48,1280]{2,1,0:T(8,128)(2,1)}, u32[]{:S(2)}, u32[]{:S(2)}) collective-permute-start(bf16[8,48,1280]{2,1,0:T(8,128)(2,1)S(1)} %pad_maximum_fusion.1.refs_1_.refs_3_.refs_6_), channel_id=1, source_target_pairs={{0,1},{1,0},{2,3},{3,2},{4,5},{5,4},{6,7},{7,6},{8,9},{9,8},{10,11... | collective-permute-start | bytes 2949128 | tf_op jit(solution)/shard_map/ppermute | solution.py:680
  49.1 13.8 %collective-permute-start.9 = (bf16[8,48,1280]{2,1,0:T(8,128)(2,1)}, bf16[8,48,1280]{2,1,0:T(8,128)(2,1)}, u32[]{:S(2)}, u32[]{:S(2)}) collective-permute-start(bf16[8,48,1280]{2,1,0:T(8,128)(2,1)} %constant_dynamic-update-slice_fusion.1.refs_3_.refs_5_.refs_8_), channel_id=1, source_target_pairs={{0,1},{1,0},{2,3},{3,2},{4,5},{5,4},{6,7},{7,6},{8,9},{9,8},{10,11... | collective-permute-start | bytes 2949128 | tf_op jit(solution)/shard_map/ppermute | solution.py:680
  50.0 11.3 %collective-permute-start.3 = (bf16[1,48,1536]{2,1,0:T(8,128)(2,1)S(1)}, bf16[1,48,1536]{2,1,0:T(8,128)(2,1)}, u32[]{:S(2)}, u32[]{:S(2)}) collective-permute-start(bf16[1,48,1536]{2,1,0:T(8,128)(2,1)S(1)} %maximum_select_fusion.1), channel_id=1, source_target_pairs={{0,16},{1,17},{2,18},{3,19},{4,20},{5,21},{6,22},{7,23},{8,24},{9,... | collective-permute-start | bytes 442376 | tf_op jit(solution)/shard_map/ppermute | solution.py:680
  54.5 23.1 %collective-permute-start.11 = (bf16[4,48,2432]{2,1,0:T(8,128)(2,1)}, bf16[4,48,2432]{2,1,0:T(8,128)(2,1)}, u32[]{:S(2)}, u32[]{:S(2)}) collective-permute-start(bf16[4,48,2432]{2,1,0:T(8,128)(2,1)} %pad_maximum_fusion.2), channel_id=1, source_target_pairs={{0,4},{1,5},{2,6},{3,7},{4,0},{5,1},{6,2},{7,3},{8,12},{9,13},{10,... | collective-permute-start | bytes 2801672 | tf_op jit(solution)/shard_map/ppermute | solution.py:680
  62.5 15.1 %collective-permute-start.12 = (bf16[2,48,1536]{2,1,0:T(8,128)(2,1)S(1)}, bf16[2,48,1536]{2,1,0:T(8,128)(2,1)S(1)}, u32[]{:S(2)}, u32[]{:S(2)}) collective-permute-start(bf16[2,48,1536]{2,1,0:T(8,128)(2,1)S(1)} %pad_maximum_fusion.8), channel_id=1, source_target_pairs={{0,8},{1,9},{2,10},{3,11},{4,12},{5,13},{6,14},{7,15},{8,0},{9,1},... | collective-permute-start | bytes 884744 | tf_op jit(solution)/shard_map/ppermute | solution.py:680
  80.8 16.1 %collective-permute-start.15 = (bf16[4,48,1536]{2,1,0:T(8,128)(2,1)S(1)}, bf16[4,48,1536]{2,1,0:T(8,128)(2,1)S(1)}, u32[]{:S(2)}, u32[]{:S(2)}) collective-permute-start(bf16[4,48,1536]{2,1,0:T(8,128)(2,1)S(1)} %get-tuple-element.369), channel_id=1, source_target_pairs={{0,2},{1,3},{2,0},{3,1},{4,6},{5,7},{6,4},{7,5},{8,10},{9,11},{10,... | collective-permute-start | bytes 1769480 | tf_op jit(solution)/shard_map/ppermute | solution.py:680
  81.4 15.6 %collective-permute-start.14 = (bf16[4,48,1536]{2,1,0:T(8,128)(2,1)S(1)}, bf16[4,48,1536]{2,1,0:T(8,128)(2,1)S(1)}, u32[]{:S(2)}, u32[]{:S(2)}) collective-permute-start(bf16[4,48,1536]{2,1,0:T(8,128)(2,1)S(1)} %get-tuple-element.369), channel_id=1, source_target_pairs={{0,4},{1,5},{2,6},{3,7},{4,0},{5,1},{6,2},{7,3},{8,12},{9,13},{10,... | collective-permute-start | bytes 1769480 | tf_op jit(solution)/shard_map/ppermute | solution.py:680
  172.5 27.1 %collective-permute-start.21 = (bf16[4,48,2944]{2,1,0:T(8,128)(2,1)S(1)}, bf16[4,48,2944]{2,1,0:T(8,128)(2,1)S(1)}, u32[]{:S(2)}, u32[]{:S(2)}) collective-permute-start(bf16[4,48,2944]{2,1,0:T(8,128)(2,1)S(1)} %get-tuple-element.238), channel_id=1, source_target_pairs={{0,4},{1,5},{2,6},{3,7},{4,0},{5,1},{6,2},{7,3},{8,12},{9,13},{10,... | collective-permute-start | bytes 3391496 | tf_op jit(solution)/shard_map/ppermute | solution.py:680
  204.1 22.8 %collective-permute-start.23 = (bf16[4,48,2432]{2,1,0:T(8,128)(2,1)S(1)}, bf16[4,48,2432]{2,1,0:T(8,128)(2,1)S(1)}, u32[]{:S(2)}, u32[]{:S(2)}) collective-permute-start(bf16[4,48,2432]{2,1,0:T(8,128)(2,1)S(1)} %get-tuple-element.249), channel_id=1, source_target_pairs={{0,4},{1,5},{2,6},{3,7},{4,0},{5,1},{6,2},{7,3},{8,12},{9,13},{10,... | collective-permute-start | bytes 2801672 | tf_op jit(solution)/shard_map/ppermute | solution.py:680
  205.3 15.4 %collective-permute-start.24 = (bf16[2,48,2944]{2,1,0:T(8,128)(2,1)S(1)}, bf16[2,48,2944]{2,1,0:T(8,128)(2,1)S(1)}, u32[]{:S(2)}, u32[]{:S(2)}) collective-permute-start(bf16[2,48,2944]{2,1,0:T(8,128)(2,1)S(1)} %get-tuple-element.250), channel_id=1, source_target_pairs={{0,8},{1,9},{2,10},{3,11},{4,12},{5,13},{6,14},{7,15},{8,0},{9,1},... | collective-permute-start | bytes 1695752 | tf_op jit(solution)/shard_map/ppermute | solution.py:680
  230.4 19.6 %collective-permute-start.26 = (bf16[4,48,1664]{2,1,0:T(8,128)(2,1)S(1)}, bf16[4,48,1664]{2,1,0:T(8,128)(2,1)S(1)}, u32[]{:S(2)}, u32[]{:S(2)}) collective-permute-start(bf16[4,48,1664]{2,1,0:T(8,128)(2,1)S(1)} %get-tuple-element.265), channel_id=1, source_target_pairs={{0,4},{1,5},{2,6},{3,7},{4,0},{5,1},{6,2},{7,3},{8,12},{9,13},{10,... | collective-permute-start | bytes 1916936 | tf_op jit(solution)/shard_map/ppermute | solution.py:680
  231.6 18.5 %collective-permute-start.27 = (bf16[2,48,2432]{2,1,0:T(8,128)(2,1)S(1)}, bf16[2,48,2432]{2,1,0:T(8,128)(2,1)S(1)}, u32[]{:S(2)}, u32[]{:S(2)}) collective-permute-start(bf16[2,48,2432]{2,1,0:T(8,128)(2,1)S(1)} %get-tuple-element.266), channel_id=1, source_target_pairs={{0,8},{1,9},{2,10},{3,11},{4,12},{5,13},{6,14},{7,15},{8,0},{9,1},... | collective-permute-start | bytes 1400840 | tf_op jit(solution)/shard_map/ppermute | solution.py:680
  231.9 16.5 %collective-permute-start.28 = (bf16[1,48,2944]{2,1,0:T(8,128)(2,1)S(1)}, bf16[1,48,2944]{2,1,0:T(8,128)(2,1)S(1)}, u32[]{:S(2)}, u32[]{:S(2)}) collective-permute-start(bf16[1,48,2944]{2,1,0:T(8,128)(2,1)S(1)} %get-tuple-element.267), channel_id=1, source_target_pairs={{0,16},{1,17},{2,18},{3,19},{4,20},{5,21},{6,22},{7,23},{8,24},{9,... | collective-permute-start | bytes 847880 | tf_op jit(solution)/shard_map/ppermute | solution.py:680
  252.6 13.6 %collective-permute-start.33 = (bf16[1,48,2432]{2,1,0:T(8,128)(2,1)S(1)}, bf16[1,48,2432]{2,1,0:T(8,128)(2,1)S(1)}, u32[]{:S(2)}, u32[]{:S(2)}) collective-permute-start(bf16[1,48,2432]{2,1,0:T(8,128)(2,1)S(1)} %get-tuple-element.291), channel_id=1, source_target_pairs={{0,16},{1,17},{2,18},{3,19},{4,20},{5,21},{6,22},{7,23},{8,24},{9,... | collective-permute-start | bytes 700424 | tf_op jit(solution)/shard_map/ppermute | solution.py:680
  257.5 39.9 %collective-permute-start.30 = (f32[8,384]{1,0:T(8,128)S(1)}, f32[8,384]{1,0:T(8,128)S(1)}, u32[]{:S(2)}, u32[]{:S(2)}) collective-permute-start(f32[8,384]{1,0:T(8,128)S(1)} %stack.39), channel_id=1, source_target_pairs={{0,2},{1,3},{2,0},{3,1},{4,6},{5,7},{6,4},{7,5},{8,10},{9,11},{10,... | collective-permute-start | bytes 36872 | tf_op jit(solution)/shard_map/ppermute | solution.py:680
  259.6 13.3 %collective-permute-start.32 = (bf16[2,48,1664]{2,1,0:T(8,128)(2,1)S(1)}, bf16[2,48,1664]{2,1,0:T(8,128)(2,1)S(1)}, u32[]{:S(2)}, u32[]{:S(2)}) collective-permute-start(bf16[2,48,1664]{2,1,0:T(8,128)(2,1)S(1)} %get-tuple-element.289), channel_id=1, source_target_pairs={{0,8},{1,9},{2,10},{3,11},{4,12},{5,13},{6,14},{7,15},{8,0},{9,1},... | collective-permute-start | bytes 958472 | tf_op jit(solution)/shard_map/ppermute | solution.py:680
  260.5 12.6 %collective-permute-start.31 = (bf16[4,48,896]{2,1,0:T(8,128)(2,1)S(1)}, bf16[4,48,896]{2,1,0:T(8,128)(2,1)S(1)}, u32[]{:S(2)}, u32[]{:S(2)}) collective-permute-start(bf16[4,48,896]{2,1,0:T(8,128)(2,1)S(1)} %get-tuple-element.287), channel_id=1, source_target_pairs={{0,4},{1,5},{2,6},{3,7},{4,0},{5,1},{6,2},{7,3},{8,12},{9,13},{10,... | collective-permute-start | bytes 1032200 | tf_op jit(solution)/shard_map/ppermute | solution.py:680
  273.2 9.5 %collective-permute-start.35 = (bf16[1,48,1664]{2,1,0:T(8,128)(2,1)S(1)}, bf16[1,48,1664]{2,1,0:T(8,128)(2,1)S(1)}, u32[]{:S(2)}, u32[]{:S(2)}) collective-permute-start(bf16[1,48,1664]{2,1,0:T(8,128)(2,1)S(1)} %get-tuple-element.295), channel_id=1, source_target_pairs={{0,16},{1,17},{2,18},{3,19},{4,20},{5,21},{6,22},{7,23},{8,24},{9,... | collective-permute-start | bytes 479240 | tf_op jit(solution)/shard_map/ppermute | solution.py:680
  274.1 9.7 %collective-permute-start.34 = (bf16[2,48,896]{2,1,0:T(8,128)(2,1)S(1)}, bf16[2,48,896]{2,1,0:T(8,128)(2,1)S(1)}, u32[]{:S(2)}, u32[]{:S(2)}) collective-permute-start(bf16[2,48,896]{2,1,0:T(8,128)(2,1)S(1)} %get-tuple-element.293), channel_id=1, source_target_pairs={{0,8},{1,9},{2,10},{3,11},{4,12},{5,13},{6,14},{7,15},{8,0},{9,1},... | collective-permute-start | bytes 516104 | tf_op jit(solution)/shard_map/ppermute | solution.py:680
  (88 other events, 1053.9 us)

commit v6 on v5

--- a/solution.py
+++ b/solution.py
@@ -387,7 +387,7 @@
         out_specs=out_specs,
         out_shape=out_shape,
         scratch_shapes=scratch,
-        compiler_params=params(48),
+        compiler_params=params(60),
         cost_estimate=pl.CostEstimate(
             flops=2 * rows * size, bytes_accessed=24 * size, transcendentals=0
         ),
@@ -476,7 +476,7 @@
             pltpu.VMEM((D, HEADW), BF),
             semaphores(group),
         ],
-        compiler_params=params(40),
+        compiler_params=params(60),
         cost_estimate=pl.CostEstimate(
             flops=6 * rows * D * HEADW, bytes_accessed=8 << 20, transcendentals=0
         ),
@@ -652,7 +652,7 @@
         out_specs=out_specs,
         out_shape=out_shape,
         scratch_shapes=scratch,
-        compiler_params=params(56),
+        compiler_params=params(60),
         cost_estimate=pl.CostEstimate(
             flops=4 * rows * size, bytes_accessed=48 * size, transcendentals=0
         ),
@@ -866,8 +866,8 @@
 def adam_update(master, clipped, first_old, second_old, matrix):
     first_new = BETA_ONE * first_old + (1.0 - BETA_ONE) * clipped
     second_new = BETA_TWO * second_old + (1.0 - BETA_TWO) * clipped * clipped
-    first_hat = first_new / (1.0 - BETA_ONE**STEP_NUM)
-    second_hat = second_new / (1.0 - BETA_TWO**STEP_NUM)
+    first_hat = first_new * (1.0 / (1.0 - BETA_ONE**STEP_NUM))
+    second_hat = second_new * (1.0 / (1.0 - BETA_TWO**STEP_NUM))
     direction = first_hat / (jnp.sqrt(second_hat) + ADAM_EPS)
     if matrix:
         master_new = master - RATE_MATRIX * (direction + WEIGHT_DECAY * master)
@@ -1086,7 +1086,7 @@
             arrays = from_whole(groups[n], wholes[n], arrays, sizes)
         keep, give = arrays
         flying = totals[n + 1 :]
-        give = after_landing(give, flying)
+        give = after_landing(give, flying[1:] if n == 1 else flying)
         totals[n] = Scatter(keep, give, sizes)
         if n:
             grad = hold(grad, totals[n], *flying)

time: 334 us -> 330 us (0.988)
  waiting for transfers between devices: 87.2 us -> 76 us
  local copies, waits for them, and re-layouts: 21.7 us -> 15.3 us
  other arithmetic: 30.1 us -> 36.4 us
  Pallas kernels: 141 us -> 146 us
    ppermute x49, waiting for transfers between devices: 87.2 us -> 76 us  [swap(): return lax.ppermute(x, AXES, partners(sizes, fsdp_mask, dp_mask))]
    unnamed x136 -> x110, local copies, waits for them, and re-layouts: 12.1 us -> 5.81 us
    convert_element_type x16, other arithmetic: 4.48 us -> 9.37 us  [add(): return (a.astype(F32) + b.astype(F32)).astype(BF)]
  transfers between devices with their start and end apart: 49 -> 49, of which waited for: 25 -> 25; matrix products, arithmetic and copies ran while one was open for 11% -> 12% of each run, Pallas kernels for 25% -> 26%
where the time goes in v6:
time: 330 us; the launch traced here: 324 us
  Pallas kernels  146 us (44%)
  waiting for transfers between devices  76 us (23%)
  starting transfers between devices  42.2 us (13%)
  other arithmetic  36.4 us (11%)
  local copies, waits for them, and re-layouts  15.3 us (5%)
  between operations  7.99 us (2%)
    pallas_call x4, Pallas kernels, backward_layer(): pl.pallas_call(functools.partial(backward_body, names, extra[0] if extra...  83.4 us
    ppermute x49, waiting for transfers between devices, swap(): return lax.ppermute(x, AXES, partners(sizes, fsdp_mask, dp_mask))  76 us
    ppermute x49, starting transfers between devices, swap(): return lax.ppermute(x, AXES, partners(sizes, fsdp_mask, dp_mask))  42.2 us
    pallas_call x3, Pallas kernels, forward_layer(): pl.pallas_call(functools.partial(forward_body, names, group), grid=(rows...  40.6 us
    pallas_call x1, Pallas kernels, head(): pl.pallas_call(functools.partial(head_body, group), grid=(rows // TILE,),...  12.2 us
    pallas_call x1, Pallas kernels, update(): pl.pallas_call(functools.partial(update_body, groups, layers), grid=(L,),...  9.81 us
    convert_element_type x16, other arithmetic, add(): return (a.astype(F32) + b.astype(F32)).astype(BF)  9.37 us
  transfers between devices with their start and end apart: 49, of which 25 were waited for; matrix products, arithmetic and copies ran while one was open for 12% of the time, Pallas kernels for 26%

profile of v6, /device:TPU:0, one launch (start us, length us, event | category | flops | bytes accessed | tf_op | source)
XLA Modules:
  0.0 324.0 jit_solution(16855373009802500466)
XLA Ops:
  4.7 4.1 %collective-permute-start = (bf16[1,48,1280]{2,1,0:T(8,128)(2,1)S(1)}, bf16[1,48,1280]{2,1,0:T(8,128)(2,1)S(1)}, u32[]{:S(2)}, u32[]{:S(2)}) collective-permute-start(bf16[1,48,1280]{2,1,0:T(8,128)(2,1)S(1)} %fusion.12), channel_id=1, source_target_pairs={{0,16},{1,17},{2,18},{3,19},{4,20},{5,21},{6,22},{7,23},{8,24},{9,... | collective-permute-start | bytes 368648 | tf_op jit(solution)/shard_map/ppermute | solution.py:680
  9.7 5.1 %collective-permute-done = bf16[1,48,1280]{2,1,0:T(8,128)(2,1)S(1)} collective-permute-done((bf16[1,48,1280]{2,1,0:T(8,128)(2,1)S(1)}, bf16[1,48,1280]{2,1,0:T(8,128)(2,1)S(1)}, u32[]{:S(2)}, u32[]{:S(2)}) %collective-permute-start) | collective-permute-done | bytes 122912 | tf_op jit(solution)/shard_map/ppermute | solution.py:680
  26.0 3.4 %collective-permute-start.2 = (bf16[1,48,2432]{2,1,0:T(8,128)(2,1)S(1)}, bf16[1,48,2432]{2,1,0:T(8,128)(2,1)S(1)}, u32[]{:S(2)}, u32[]{:S(2)}) collective-permute-start(bf16[1,48,2432]{2,1,0:T(8,128)(2,1)S(1)} %maximum_select_fusion), channel_id=1, source_target_pairs={{0,16},{1,17},{2,18},{3,19},{4,20},{5,21},{6,22},{7,23},{8,24},{9,... | collective-permute-start | bytes 700424 | tf_op jit(solution)/shard_map/ppermute | solution.py:680
  33.1 6.2 %collective-permute-done.2 = bf16[1,48,2432]{2,1,0:T(8,128)(2,1)S(1)} collective-permute-done((bf16[1,48,2432]{2,1,0:T(8,128)(2,1)S(1)}, bf16[1,48,2432]{2,1,0:T(8,128)(2,1)S(1)}, u32[]{:S(2)}, u32[]{:S(2)}) %collective-permute-start.2) | collective-permute-done | bytes 233504 | tf_op jit(solution)/shard_map/ppermute | solution.py:680
  41.5 6.2 %collective-permute-done.7 = bf16[2,48,1280]{2,1,0:T(8,128)(2,1)S(1)} collective-permute-done((bf16[2,48,1280]{2,1,0:T(8,128)(2,1)S(1)}, bf16[2,48,1280]{2,1,0:T(8,128)(2,1)S(1)}, u32[]{:S(2)}, u32[]{:S(2)}) %collective-permute-start.7) | collective-permute-done | bytes 245792 | tf_op jit(solution)/shard_map/ppermute | solution.py:680
  49.0 3.4 %collective-permute-start.3 = (bf16[1,48,1536]{2,1,0:T(8,128)(2,1)}, bf16[1,48,1536]{2,1,0:T(8,128)(2,1)}, u32[]{:S(2)}, u32[]{:S(2)}) collective-permute-start(bf16[1,48,1536]{2,1,0:T(8,128)(2,1)} %maximum_select_fusion.1), channel_id=1, source_target_pairs={{0,16},{1,17},{2,18},{3,19},{4,20},{5,21},{6,22},{7,23},{8,24},{9,... | collective-permute-start | bytes 442376 | tf_op jit(solution)/shard_map/ppermute | solution.py:680
  61.3 13.6 %shard_map.493 = (f32[1024,384]{1,0:T(8,128)}, f32[8,384]{1,0:T(8,128)}, bf16[1024,1152]{1,0:T(8,128)(2,1)}, bf16[1024,384]{1,0:T(8,128)(2,1)}, bf16[1024,384]{1...) custom-call(bf16[1024,256]{1,0:T(8,128)(2,1)} %concatenate.163.refs_0_.refs_5_, ...), custom_call_target="tpu_custom_call" | custom-call | flops 3825205248 | bytes 44826624 | tf_op jit(solution)/shard_map/pallas_call | solution.py:383
  83.9 13.3 %shard_map.494 = (bf16[1024,1152]{1,0:T(8,128)(2,1)}, bf16[1024,384]{1,0:T(8,128)(2,1)}, bf16[1024,384]{1,0:T(8,128)(2,1)}, f32[1024,384]{1,0:T(8,128)}, f32[102...) custom-call(f32[1024,384]{1,0:T(8,128)} %get-tuple-element.197.refs_0_.refs_1_, bf16[8,48,2432]{2,1,0:T(8,128)(2,1)} %copy-done.8, ...), custom_call_target="tpu_custom_call" | custom-call | flops 3623878656 | bytes 42467328 | tf_op jit(solution)/shard_map/pallas_call | solution.py:383
  100.3 5.7 %collective-permute-done.17 = bf16[2,48,1536]{2,1,0:T(8,128)(2,1)S(1)} collective-permute-done((bf16[2,48,1536]{2,1,0:T(8,128)(2,1)S(1)}, bf16[2,48,1536]{2,1,0:T(8,128)(2,1)S(1)}, u32[]{:S(2)}, u32[]{:S(2)}) %collective-permute-start.17) | collective-permute-done | bytes 294944 | tf_op jit(solution)/shard_map/ppermute | solution.py:680
  110.1 13.7 %shard_map.495 = (bf16[1024,1152]{1,0:T(8,128)(2,1)}, bf16[1024,384]{1,0:T(8,128)(2,1)}, bf16[1024,384]{1,0:T(8,128)(2,1)}, f32[1024,384]{1,0:T(8,128)}, f32[102...) custom-call(f32[1024,384]{1,0:T(8,128)} %get-tuple-element.204.refs_0_.refs_1_, ...), custom_call_target="tpu_custom_call" | custom-call | flops 3623878656 | bytes 42467328 | tf_op jit(solution)/shard_map/pallas_call | solution.py:383
  123.8 12.2 %shard_map.496 = (f32[1024,384]{1,0:T(8,128)}, bf16[384,1152]{1,0:T(8,128)(2,1)}, f32[8,384]{1,0:T(8,128)}, f32[8,128]{1,0:T(8,128)}) custom-call(f32[1024,384]{1,0:T(8,128)} %get-tuple-element.207.x_ref, f32[1024,128]{1,0:T(8,128)} %target_ref.1, f32[1024,128]{1,0:T(8,128)} %fusion.mask_ref, ...), custom_call_target="tpu_custom_call" | custom-call | flops 2717908992 | bytes 8388608 | tf_op jit(solution)/shard_map/pallas_call | solution.py:452
  136.0 26.9 %shard_map.497 = (f32[1024,384]{1,0:T(8,128)}, bf16[8,48,2944]{2,1,0:T(8,128)(2,1)}, bf16[8,48,2944]{2,1,0:T(8,128)(2,1)}, f32[8,384]{1,0:T(8,128)}, f32[48,128]{1,0:T(8,128)}, /*index=5*/f32[8,384]{1,0:T(8,128)}) custom-call(f32[1024,384]{1,0:T(8,128)} %get-tuple-element.212.refs_0_, f32[1024,384]{1,0:T(8,128)} %get-tuple-element.204.refs_0_.refs_1_, ...), custom_call_target="tpu_custom_call" | custom-call | flops 7247757312 | bytes 84934656 | tf_op jit(solution)/shard_map/pallas_call | solution.py:648
  163.2 4.5 %collective-permute-done.20 = bf16[8,48,2944]{2,1,0:T(8,128)(2,1)S(1)} collective-permute-done((bf16[8,48,2944]{2,1,0:T(8,128)(2,1)}, bf16[8,48,2944]{2,1,0:T(8,128)(2,1)S(1)}, u32[]{:S(2)}, u32[]{:S(2)}) %collective-permute-start.20) | collective-permute-done | bytes 2261024 | tf_op jit(solution)/shard_map/ppermute | solution.py:680
  170.8 25.8 %shard_map.498 = (f32[1024,384]{1,0:T(8,128)}, bf16[8,48,2432]{2,1,0:T(8,128)(2,1)}, bf16[8,48,2432]{2,1,0:T(8,128)(2,1)}, f32[8,384]{1,0:T(8,128)}, f32[48,128]{1,0:T(8,128)}, /*index=5*/f32[8,384]{1,0:T(8,128)}) custom-call(f32[1024,384]{1,0:T(8,128)} %get-tuple-element.225.refs_0_, f32[1024,384]{1,0:T(8,128)} %get-tuple-element.197.refs_0_.refs_1_, ...), custom_call_target="tpu_custom_call" | custom-call | flops 7247757312 | bytes 84934656 | tf_op jit(solution)/shard_map/pallas_call | solution.py:648
  202.7 15.2 %shard_map.499 = (f32[1024,384]{1,0:T(8,128)}, bf16[8,48,1664]{2,1,0:T(8,128)(2,1)}, bf16[8,48,1664]{2,1,0:T(8,128)(2,1)}, f32[8,384]{1,0:T(8,128)}) custom-call(f32[1024,384]{1,0:T(8,128)} %get-tuple-element.241.refs_0_, f32[1024,384]{1,0:T(8,128)} %get-tuple-element.242.refs_1_, bf16[1024,2048]{1,0:T(8,128)(2,1)} %get-tuple-element.243.refs_2_, ...), custom_call_target="tpu_custom_call" | custom-call | flops 4831838208 | bytes 56623104 | tf_op jit(solution)/shard_map/pallas_call | solution.py:648
  219.9 4.4 %collective-permute-done.25 = bf16[4,48,2432]{2,1,0:T(8,128)(2,1)S(1)} collective-permute-done((bf16[4,48,2432]{2,1,0:T(8,128)(2,1)S(1)}, bf16[4,48,2432]{2,1,0:T(8,128)(2,1)S(1)}, u32[]{:S(2)}, u32[]{:S(2)}) %collective-permute-start.25) | collective-permute-done | bytes 933920 | tf_op jit(solution)/shard_map/ppermute | solution.py:680
  229.8 15.4 %shard_map.500 = (bf16[8,48,896]{2,1,0:T(8,128)(2,1)}, bf16[8,48,896]{2,1,0:T(8,128)(2,1)}, f32[8,384]{1,0:T(8,128)}, f32[48,128]{1,0:T(8,128)}) custom-call(f32[1024,384]{1,0:T(8,128)} %get-tuple-element.254.refs_0_, f32[1024,384]{1,0:T(8,128)} %get-tuple-element.255.refs_1_, bf16[1024,1152]{1,0:T(8,128)(2,1)} %get-tuple-element.256.refs_2_, ...), custom_call_target="tpu_custom_call" | custom-call | flops 2818572288 | bytes 33030144 | tf_op jit(solution)/shard_map/pallas_call | solution.py:648
  256.8 5.2 %collective-permute-done.33 = bf16[1,48,2432]{2,1,0:T(8,128)(2,1)} collective-permute-done((bf16[1,48,2432]{2,1,0:T(8,128)(2,1)}, bf16[1,48,2432]{2,1,0:T(8,128)(2,1)}, u32[]{:S(2)}, u32[]{:S(2)}) %collective-permute-start.33) | collective-permute-done | bytes 233504 | tf_op jit(solution)/shard_map/ppermute | solution.py:680
  263.1 5.5 %collective-permute-done.32 = bf16[2,48,1664]{2,1,0:T(8,128)(2,1)S(1)} collective-permute-done((bf16[2,48,1664]{2,1,0:T(8,128)(2,1)S(1)}, bf16[2,48,1664]{2,1,0:T(8,128)(2,1)S(1)}, u32[]{:S(2)}, u32[]{:S(2)}) %collective-permute-start.32) | collective-permute-done | bytes 319520 | tf_op jit(solution)/shard_map/ppermute | solution.py:680
  272.2 6.1 %collective-permute-done.35 = bf16[1,48,1664]{2,1,0:T(8,128)(2,1)S(1)} collective-permute-done((bf16[1,48,1664]{2,1,0:T(8,128)(2,1)S(1)}, bf16[1,48,1664]{2,1,0:T(8,128)(2,1)S(1)}, u32[]{:S(2)}, u32[]{:S(2)}) %collective-permute-start.35) | collective-permute-done | bytes 159776 | tf_op jit(solution)/shard_map/ppermute | solution.py:680
  281.9 3.3 %collective-permute-done.36 = bf16[1,48,896]{2,1,0:T(8,128)(2,1)S(1)} collective-permute-done((bf16[1,48,896]{2,1,0:T(8,128)(2,1)S(1)}, bf16[1,48,896]{2,1,0:T(8,128)(2,1)S(1)}, u32[]{:S(2)}, u32[]{:S(2)}) %collective-permute-start.36) | collective-permute-done | bytes 86048 | tf_op jit(solution)/shard_map/ppermute | solution.py:680
  293.2 4.6 %collective-permute-done.41 = f32[8,384]{1,0:T(8,128)S(1)} collective-permute-done((f32[8,384]{1,0:T(8,128)S(1)}, f32[8,384]{1,0:T(8,128)S(1)}, u32[]{:S(2)}, u32[]{:S(2)}) %collective-permute-start.41) | collective-permute-done | bytes 12320 | tf_op jit(solution)/shard_map/ppermute | solution.py:680
  297.8 3.7 %collective-permute-done.42 = f32[8,384]{1,0:T(8,128)S(1)} collective-permute-done((f32[8,384]{1,0:T(8,128)S(1)}, f32[8,384]{1,0:T(8,128)S(1)}, u32[]{:S(2)}, u32[]{:S(2)}) %collective-permute-start.42) | collective-permute-done | bytes 12320 | tf_op jit(solution)/shard_map/ppermute | solution.py:680
  312.8 9.8 %shard_map.501 = (f32[3,48,1152]{2,1,0:T(8,128)}, f32[3,48,384]{2,1,0:T(8,128)}, f32[3,48,2048]{2,1,0:T(8,128)}, f32[3,128,384]{2,1,0:T(8,128)}, f32[48,1152]{1,...) custom-call(f32[1,1]{1,0:T(1,128)} %bitcast.36.refs_0_, ...), custom_call_target="tpu_custom_call" | custom-call | flops 16777216 | bytes 18874368 | tf_op jit(solution)/shard_map/pallas_call | solution.py:940
  (340 shorter events, 98.7 us)
Async XLA Ops:
  4.7 10.1 %collective-permute-start = (bf16[1,48,1280]{2,1,0:T(8,128)(2,1)S(1)}, bf16[1,48,1280]{2,1,0:T(8,128)(2,1)S(1)}, u32[]{:S(2)}, u32[]{:S(2)}) collective-permute-start(bf16[1,48,1280]{2,1,0:T(8,128)(2,1)S(1)} %fusion.12), channel_id=1, source_target_pairs={{0,16},{1,17},{2,18},{3,19},{4,20},{5,21},{6,22},{7,23},{8,24},{9,... | collective-permute-start | bytes 368648 | tf_op jit(solution)/shard_map/ppermute | solution.py:680
  23.2 16.8 %collective-permute-start.6 = (bf16[4,48,1280]{2,1,0:T(8,128)(2,1)S(1)}, bf16[4,48,1280]{2,1,0:T(8,128)(2,1)S(1)}, u32[]{:S(2)}, u32[]{:S(2)}) collective-permute-start(bf16[4,48,1280]{2,1,0:T(8,128)(2,1)S(1)} %pad_maximum_fusion.6), channel_id=1, source_target_pairs={{0,2},{1,3},{2,0},{3,1},{4,6},{5,7},{6,4},{7,5},{8,10},{9,11},{10,... | collective-permute-start | bytes 1474568 | tf_op jit(solution)/shard_map/ppermute | solution.py:680
  24.5 16.1 %collective-permute-start.4 = (bf16[4,48,1280]{2,1,0:T(8,128)(2,1)S(1)}, bf16[4,48,1280]{2,1,0:T(8,128)(2,1)S(1)}, u32[]{:S(2)}, u32[]{:S(2)}) collective-permute-start(bf16[4,48,1280]{2,1,0:T(8,128)(2,1)S(1)} %pad_maximum_fusion.6), channel_id=1, source_target_pairs={{0,4},{1,5},{2,6},{3,7},{4,0},{5,1},{6,2},{7,3},{8,12},{9,13},{10,... | collective-permute-start | bytes 1474568 | tf_op jit(solution)/shard_map/ppermute | solution.py:680
  26.0 13.2 %collective-permute-start.2 = (bf16[1,48,2432]{2,1,0:T(8,128)(2,1)S(1)}, bf16[1,48,2432]{2,1,0:T(8,128)(2,1)S(1)}, u32[]{:S(2)}, u32[]{:S(2)}) collective-permute-start(bf16[1,48,2432]{2,1,0:T(8,128)(2,1)S(1)} %maximum_select_fusion), channel_id=1, source_target_pairs={{0,16},{1,17},{2,18},{3,19},{4,20},{5,21},{6,22},{7,23},{8,24},{9,... | collective-permute-start | bytes 700424 | tf_op jit(solution)/shard_map/ppermute | solution.py:680
  39.3 13.1 %collective-permute-start.10 = (bf16[2,48,2432]{2,1,0:T(8,128)(2,1)S(1)}, bf16[2,48,2432]{2,1,0:T(8,128)(2,1)S(1)}, u32[]{:S(2)}, u32[]{:S(2)}) collective-permute-start(bf16[2,48,2432]{2,1,0:T(8,128)(2,1)S(1)} %pad_maximum_fusion.7), channel_id=1, source_target_pairs={{0,8},{1,9},{2,10},{3,11},{4,12},{5,13},{6,14},{7,15},{8,0},{9,1},... | collective-permute-start | bytes 1400840 | tf_op jit(solution)/shard_map/ppermute | solution.py:680
  41.4 20.0 %collective-permute-start.5 = (bf16[8,48,1280]{2,1,0:T(8,128)(2,1)S(1)}, bf16[8,48,1280]{2,1,0:T(8,128)(2,1)}, u32[]{:S(2)}, u32[]{:S(2)}) collective-permute-start(bf16[8,48,1280]{2,1,0:T(8,128)(2,1)S(1)} %pad_maximum_fusion.1.refs_1_.refs_3_.refs_6_), channel_id=1, source_target_pairs={{0,1},{1,0},{2,3},{3,2},{4,5},{5,4},{6,7},{7,6},{8,9},{9,8},{10,11... | collective-permute-start | bytes 2949128 | tf_op jit(solution)/shard_map/ppermute | solution.py:680
  48.0 13.3 %collective-permute-start.9 = (bf16[8,48,1280]{2,1,0:T(8,128)(2,1)S(1)}, bf16[8,48,1280]{2,1,0:T(8,128)(2,1)}, u32[]{:S(2)}, u32[]{:S(2)}) collective-permute-start(bf16[8,48,1280]{2,1,0:T(8,128)(2,1)S(1)} %constant_dynamic-update-slice_fusion.1.refs_3_.refs_5_.refs_8_), channel_id=1, source_target_pairs={{0,1},{1,0},{2,3},{3,2},{4,5},{5,4},{6,7},{7,6},{8,9},{9,8},{10,11... | collective-permute-start | bytes 2949128 | tf_op jit(solution)/shard_map/ppermute | solution.py:680
  49.0 11.1 %collective-permute-start.3 = (bf16[1,48,1536]{2,1,0:T(8,128)(2,1)}, bf16[1,48,1536]{2,1,0:T(8,128)(2,1)}, u32[]{:S(2)}, u32[]{:S(2)}) collective-permute-start(bf16[1,48,1536]{2,1,0:T(8,128)(2,1)} %maximum_select_fusion.1), channel_id=1, source_target_pairs={{0,16},{1,17},{2,18},{3,19},{4,20},{5,21},{6,22},{7,23},{8,24},{9,... | collective-permute-start | bytes 442376 | tf_op jit(solution)/shard_map/ppermute | solution.py:680
  53.5 23.1 %collective-permute-start.11 = (bf16[4,48,2432]{2,1,0:T(8,128)(2,1)}, bf16[4,48,2432]{2,1,0:T(8,128)(2,1)}, u32[]{:S(2)}, u32[]{:S(2)}) collective-permute-start(bf16[4,48,2432]{2,1,0:T(8,128)(2,1)} %pad_maximum_fusion.2), channel_id=1, source_target_pairs={{0,4},{1,5},{2,6},{3,7},{4,0},{5,1},{6,2},{7,3},{8,12},{9,13},{10,... | collective-permute-start | bytes 2801672 | tf_op jit(solution)/shard_map/ppermute | solution.py:680
  61.1 15.5 %collective-permute-start.12 = (bf16[2,48,1536]{2,1,0:T(8,128)(2,1)S(1)}, bf16[2,48,1536]{2,1,0:T(8,128)(2,1)S(1)}, u32[]{:S(2)}, u32[]{:S(2)}) collective-permute-start(bf16[2,48,1536]{2,1,0:T(8,128)(2,1)S(1)} %pad_maximum_fusion.8), channel_id=1, source_target_pairs={{0,8},{1,9},{2,10},{3,11},{4,12},{5,13},{6,14},{7,15},{8,0},{9,1},... | collective-permute-start | bytes 884744 | tf_op jit(solution)/shard_map/ppermute | solution.py:680
  80.0 17.2 %collective-permute-start.15 = (bf16[4,48,1536]{2,1,0:T(8,128)(2,1)}, bf16[4,48,1536]{2,1,0:T(8,128)(2,1)S(1)}, u32[]{:S(2)}, u32[]{:S(2)}) collective-permute-start(bf16[4,48,1536]{2,1,0:T(8,128)(2,1)} %get-tuple-element.367), channel_id=1, source_target_pairs={{0,2},{1,3},{2,0},{3,1},{4,6},{5,7},{6,4},{7,5},{8,10},{9,11},{10,... | collective-permute-start | bytes 1769480 | tf_op jit(solution)/shard_map/ppermute | solution.py:680
  80.5 16.7 %collective-permute-start.14 = (bf16[4,48,1536]{2,1,0:T(8,128)(2,1)}, bf16[4,48,1536]{2,1,0:T(8,128)(2,1)S(1)}, u32[]{:S(2)}, u32[]{:S(2)}) collective-permute-start(bf16[4,48,1536]{2,1,0:T(8,128)(2,1)} %get-tuple-element.367), channel_id=1, source_target_pairs={{0,4},{1,5},{2,6},{3,7},{4,0},{5,1},{6,2},{7,3},{8,12},{9,13},{10,... | collective-permute-start | bytes 1769480 | tf_op jit(solution)/shard_map/ppermute | solution.py:680
  169.8 27.0 %collective-permute-start.21 = (bf16[4,48,2944]{2,1,0:T(8,128)(2,1)S(1)}, bf16[4,48,2944]{2,1,0:T(8,128)(2,1)S(1)}, u32[]{:S(2)}, u32[]{:S(2)}) collective-permute-start(bf16[4,48,2944]{2,1,0:T(8,128)(2,1)S(1)} %get-tuple-element.237), channel_id=1, source_target_pairs={{0,4},{1,5},{2,6},{3,7},{4,0},{5,1},{6,2},{7,3},{8,12},{9,13},{10,... | collective-permute-start | bytes 3391496 | tf_op jit(solution)/shard_map/ppermute | solution.py:680
  201.4 16.5 %collective-permute-start.23 = (bf16[2,48,2944]{2,1,0:T(8,128)(2,1)}, bf16[2,48,2944]{2,1,0:T(8,128)(2,1)}, u32[]{:S(2)}, u32[]{:S(2)}) collective-permute-start(bf16[2,48,2944]{2,1,0:T(8,128)(2,1)} %get-tuple-element.248), channel_id=1, source_target_pairs={{0,8},{1,9},{2,10},{3,11},{4,12},{5,13},{6,14},{7,15},{8,0},{9,1},... | collective-permute-start | bytes 1695752 | tf_op jit(solution)/shard_map/ppermute | solution.py:680
  201.8 22.5 %collective-permute-start.25 = (bf16[4,48,2432]{2,1,0:T(8,128)(2,1)S(1)}, bf16[4,48,2432]{2,1,0:T(8,128)(2,1)S(1)}, u32[]{:S(2)}, u32[]{:S(2)}) collective-permute-start(bf16[4,48,2432]{2,1,0:T(8,128)(2,1)S(1)} %get-tuple-element.251), channel_id=1, source_target_pairs={{0,4},{1,5},{2,6},{3,7},{4,0},{5,1},{6,2},{7,3},{8,12},{9,13},{10,... | collective-permute-start | bytes 2801672 | tf_op jit(solution)/shard_map/ppermute | solution.py:680
  225.6 19.7 %collective-permute-start.26 = (bf16[4,48,1664]{2,1,0:T(8,128)(2,1)S(1)}, bf16[4,48,1664]{2,1,0:T(8,128)(2,1)S(1)}, u32[]{:S(2)}, u32[]{:S(2)}) collective-permute-start(bf16[4,48,1664]{2,1,0:T(8,128)(2,1)S(1)} %get-tuple-element.263), channel_id=1, source_target_pairs={{0,4},{1,5},{2,6},{3,7},{4,0},{5,1},{6,2},{7,3},{8,12},{9,13},{10,... | collective-permute-start | bytes 1916936 | tf_op jit(solution)/shard_map/ppermute | solution.py:680
  226.6 18.7 %collective-permute-start.27 = (bf16[2,48,2432]{2,1,0:T(8,128)(2,1)}, bf16[2,48,2432]{2,1,0:T(8,128)(2,1)S(1)}, u32[]{:S(2)}, u32[]{:S(2)}) collective-permute-start(bf16[2,48,2432]{2,1,0:T(8,128)(2,1)} %get-tuple-element.264), channel_id=1, source_target_pairs={{0,8},{1,9},{2,10},{3,11},{4,12},{5,13},{6,14},{7,15},{8,0},{9,1},... | collective-permute-start | bytes 1400840 | tf_op jit(solution)/shard_map/ppermute | solution.py:680
  228.3 17.0 %collective-permute-start.28 = (bf16[1,48,2944]{2,1,0:T(8,128)(2,1)}, bf16[1,48,2944]{2,1,0:T(8,128)(2,1)S(1)}, u32[]{:S(2)}, u32[]{:S(2)}) collective-permute-start(bf16[1,48,2944]{2,1,0:T(8,128)(2,1)} %get-tuple-element.265), channel_id=1, source_target_pairs={{0,16},{1,17},{2,18},{3,19},{4,20},{5,21},{6,22},{7,23},{8,24},{9,... | collective-permute-start | bytes 847880 | tf_op jit(solution)/shard_map/ppermute | solution.py:680
  247.8 14.1 %collective-permute-start.33 = (bf16[1,48,2432]{2,1,0:T(8,128)(2,1)}, bf16[1,48,2432]{2,1,0:T(8,128)(2,1)}, u32[]{:S(2)}, u32[]{:S(2)}) collective-permute-start(bf16[1,48,2432]{2,1,0:T(8,128)(2,1)} %get-tuple-element.289), channel_id=1, source_target_pairs={{0,16},{1,17},{2,18},{3,19},{4,20},{5,21},{6,22},{7,23},{8,24},{9,... | collective-permute-start | bytes 700424 | tf_op jit(solution)/shard_map/ppermute | solution.py:680
  253.1 40.0 %collective-permute-start.30 = (f32[8,384]{1,0:T(8,128)S(1)}, f32[8,384]{1,0:T(8,128)S(1)}, u32[]{:S(2)}, u32[]{:S(2)}) collective-permute-start(f32[8,384]{1,0:T(8,128)S(1)} %stack.39), channel_id=1, source_target_pairs={{0,2},{1,3},{2,0},{3,1},{4,6},{5,7},{6,4},{7,5},{8,10},{9,11},{10,... | collective-permute-start | bytes 36872 | tf_op jit(solution)/shard_map/ppermute | solution.py:680
  255.2 13.5 %collective-permute-start.32 = (bf16[2,48,1664]{2,1,0:T(8,128)(2,1)S(1)}, bf16[2,48,1664]{2,1,0:T(8,128)(2,1)S(1)}, u32[]{:S(2)}, u32[]{:S(2)}) collective-permute-start(bf16[2,48,1664]{2,1,0:T(8,128)(2,1)S(1)} %get-tuple-element.287), channel_id=1, source_target_pairs={{0,8},{1,9},{2,10},{3,11},{4,12},{5,13},{6,14},{7,15},{8,0},{9,1},... | collective-permute-start | bytes 958472 | tf_op jit(solution)/shard_map/ppermute | solution.py:680
  255.7 13.0 %collective-permute-start.31 = (bf16[4,48,896]{2,1,0:T(8,128)(2,1)S(1)}, bf16[4,48,896]{2,1,0:T(8,128)(2,1)S(1)}, u32[]{:S(2)}, u32[]{:S(2)}) collective-permute-start(bf16[4,48,896]{2,1,0:T(8,128)(2,1)S(1)} %get-tuple-element.285), channel_id=1, source_target_pairs={{0,4},{1,5},{2,6},{3,7},{4,0},{5,1},{6,2},{7,3},{8,12},{9,13},{10,... | collective-permute-start | bytes 1032200 | tf_op jit(solution)/shard_map/ppermute | solution.py:680
  269.7 9.7 %collective-permute-start.34 = (bf16[2,48,896]{2,1,0:T(8,128)(2,1)S(1)}, bf16[2,48,896]{2,1,0:T(8,128)(2,1)S(1)}, u32[]{:S(2)}, u32[]{:S(2)}) collective-permute-start(bf16[2,48,896]{2,1,0:T(8,128)(2,1)S(1)} %get-tuple-element.291), channel_id=1, source_target_pairs={{0,8},{1,9},{2,10},{3,11},{4,12},{5,13},{6,14},{7,15},{8,0},{9,1},... | collective-permute-start | bytes 516104 | tf_op jit(solution)/shard_map/ppermute | solution.py:680
  271.0 10.0 %collective-permute-start.39 = (bf16[1,48,2432]{2,1,0:T(8,128)(2,1)S(1)}, bf16[1,48,2432]{2,1,0:T(8,128)(2,1)S(1)}, u32[]{:S(2)}, u32[]{:S(2)}) collective-permute-start(bf16[1,48,2432]{2,1,0:T(8,128)(2,1)S(1)} %add_convert_fusion.19), channel_id=1, source_target_pairs={{0,2},{1,3},{2,0},{3,1},{4,6},{5,7},{6,4},{7,5},{8,10},{9,11},{10,... | collective-permute-start | bytes 700424 | tf_op jit(solution)/shard_map/ppermute | solution.py:680
  (75 other events, 662.3 us)
